TPU v7x, 256 devices: a whole 4x4x8 slice. The times are simulated.
256 devices in a mesh: row: 16 (over y, z_lo, core), col: 16 (over x, z_hi).
Axes of the slice: x: 4, y: 4, z: 8 (z_hi: 4, z_lo: 2; z = z_hi * 2 + z_lo), core: 2. Of those that a mesh axis runs over, the one named last changes fastest.
Arguments:
- query_single: bfloat16 [1024, 384], P('row'), may hold values from -6 to 6
- key_single: bfloat16 [4096, 384], P('col'), may hold values from -6 to 6
- query_weight: bfloat16 [384, 336], replicated, may hold values from -0.3125 to 0.3125
- key_weight: bfloat16 [384, 816], replicated, may hold values from -0.3125 to 0.3125
- pair_weight: bfloat16 [128, 12], replicated, may hold values from -1 to 1
- head_weight: float32 [12], replicated, may hold values from 0.2 to 2
- chain_bias: float32 [12], replicated, may hold values from -2 to 2
- pair: bfloat16 [1024, 4096, 128], P('row', 'col'), may hold values from -1000 to 1000
- residue_mask: int32 [4096], replicated, may hold values 0 or 1
- chain_index: int32 [4096], replicated, may hold values from 0 to 7, never falling along the last dimension, each value on 1 to 1024 neighbouring positions
- strip_offsets: int32 [16], replicated, may hold values from 0 to 4032, as said below
- grad_single_out: bfloat16 [1024, 192], P('row'), may hold values from -4 to 4
- grad_point_out: bfloat16 [1024, 288], P('row'), may hold values from -3 to 3
- grad_pair_out: bfloat16 [1024, 1536], P('row'), may hold values from -1 to 1
Outputs:
- grad_query_single: float32 [1024, 384], P('row')
- grad_key_single: float32 [4096, 384], P('col')
- grad_query_weight: float32 [384, 336], replicated
- grad_key_weight: float32 [384, 816], replicated
- grad_pair_weight: float32 [128, 12], replicated
- grad_pair: bfloat16 [1024, 4096, 128], P('row', 'col')
Inputs may be any that keep to these rules, and one draw needn't show every extreme that they name: `strip_offsets`: distinct multiples of 64; the first and the last strip of 64 residues are both among them.
All inputs are finite; a program needn't handle non-finite values.
Results may differ from a plain program's by a relative error of at most 0.012.
Values sent between devices are 32-bit elements; how exact they have to be, the bound alone decides.
No kernel may reach another device: no remote copies, remote signals or barrier semaphores. Data moves between devices by JAX's collectives and lax.ppermute only.
A program may use at most 64 MiB of HBM per device.

v0:
```python
import math

import jax
import jax.numpy as jnp
from jax import lax
from jax.sharding import PartitionSpec as P

H = 12
C = 16
P_SIZE = 4
PV = 8
DZ = 128


LOGIT_WEIGHT = math.sqrt(1.0 / 3.0)
MASKED_LOGIT = -100000.0


def local(
    query_single,
    key_single,
    query_weight,
    key_weight,
    pair_weight,
    head_weight,
    chain_bias,
    pair,
    residue_mask,
    chain_index,
    strip_offsets,
    grad_single_out,
    grad_point_out,
    grad_pair_out,
):
    query_rows = query_single.shape[0]
    key_rows = key_single.shape[0]
    head_cols = H * C
    point_cols = 3 * H * P_SIZE
    highest = lax.Precision.HIGHEST
    query_feats = jnp.dot(query_single, query_weight, preferred_element_type=jnp.float32).astype(
        jnp.bfloat16
    )
    key_feats = jnp.dot(key_single, key_weight, preferred_element_type=jnp.float32).astype(
        jnp.bfloat16
    )
    query_vec = query_feats[:, :head_cols].reshape(query_rows, H, C)
    query_pts = query_feats[:, head_cols:].reshape(query_rows, 3, H, P_SIZE)
    key_vec = key_feats[:, :head_cols].reshape(key_rows, H, C)
    value_vec = key_feats[:, head_cols : 2 * head_cols].reshape(key_rows, H, C)
    key_pts = key_feats[:, 2 * head_cols : 2 * head_cols + point_cols].reshape(
        key_rows, 3, H, P_SIZE
    )
    value_pts = key_feats[:, 2 * head_cols + point_cols :].reshape(key_rows, 3, H, PV)
    grad_vec = grad_single_out.reshape(query_rows, H, C)
    grad_pts = grad_point_out.reshape(query_rows, 3, H, PV)
    grad_pairs = grad_pair_out.reshape(query_rows, H, DZ)
    strip_begin = lax.dynamic_index_in_dim(strip_offsets, lax.axis_index("row"), 0, keepdims=False)
    key_begin = lax.axis_index("col") * key_rows
    query_live = lax.dynamic_slice_in_dim(residue_mask, strip_begin, query_rows, 0) == 1
    query_chain = lax.dynamic_slice_in_dim(chain_index, strip_begin, query_rows, 0)
    key_live = lax.dynamic_slice_in_dim(residue_mask, key_begin, key_rows, 0) == 1
    key_chain = lax.dynamic_slice_in_dim(chain_index, key_begin, key_rows, 0)
    live_pairs = query_live[:, None] & key_live[None, :]
    same_chain = (query_chain[:, None] == key_chain[None, :]).astype(jnp.float32)
    scalar = jnp.einsum("ihc,jhc->hij", query_vec, key_vec, preferred_element_type=jnp.float32)
    cross_term = jnp.einsum(
        "ixhp,jxhp->hij", query_pts, key_pts, preferred_element_type=jnp.float32
    )
    query_float = query_pts.astype(jnp.float32)
    key_float = key_pts.astype(jnp.float32)
    query_norm = jnp.sum(query_float * query_float, axis=(1, 3)).T
    key_norm = jnp.sum(key_float * key_float, axis=(1, 3)).T
    distance = query_norm[:, :, None] + key_norm[:, None, :] - 2.0 * cross_term
    pair_bias = jnp.einsum("ijc,ch->hij", pair, pair_weight, preferred_element_type=jnp.float32)
    point_coef = head_weight * (math.sqrt(2.0 / (9.0 * P_SIZE)) / 2.0)
    logits = LOGIT_WEIGHT * (
        scalar * C ** (-0.5) + pair_bias - point_coef[:, None, None] * distance
    )
    logits = logits + chain_bias[:, None, None] * same_chain[None]
    logits = jnp.where(live_pairs[None], logits, MASKED_LOGIT)
    row_top = lax.pmax(jnp.max(logits, axis=2), "col")
    upstream = jnp.einsum("ihc,jhc->hij", grad_vec, value_vec, preferred_element_type=jnp.float32)
    upstream = upstream + jnp.einsum(
        "ixhv,jxhv->hij", grad_pts, value_pts, preferred_element_type=jnp.float32
    )
    upstream = upstream + jnp.einsum(
        "ihc,ijc->hij", grad_pairs, pair, preferred_element_type=jnp.float32
    )
    exp_terms = jnp.exp(logits - row_top[:, :, None])
    row_total, moment = lax.psum(
        (jnp.sum(exp_terms, axis=2), jnp.sum(exp_terms * upstream, axis=2)), "col"
    )
    weights = exp_terms / row_total[:, :, None]
    centre = moment / row_total
    score_grad = jnp.where(live_pairs[None], weights * (upstream - centre[:, :, None]), 0.0)
    weight_bf = weights.astype(jnp.bfloat16)
    score_bf = score_grad.astype(jnp.bfloat16)
    scale_qk = LOGIT_WEIGHT * C ** (-0.5)
    grad_coef = -2.0 * LOGIT_WEIGHT * point_coef
    row_score = jnp.sum(score_bf, axis=2, dtype=jnp.float32)
    col_score = jnp.sum(score_bf, axis=1, dtype=jnp.float32)
    grad_qvec = scale_qk * jnp.einsum(
        "hij,jhc->ihc", score_bf, key_vec, preferred_element_type=jnp.float32
    )
    grad_qpts = grad_coef[None, None, :, None] * (
        query_float * row_score.T[:, None, :, None]
        - jnp.einsum("hij,jxhp->ixhp", score_bf, key_pts, preferred_element_type=jnp.float32)
    )
    query_part = jnp.concatenate(
        [grad_qvec.reshape(query_rows, -1), grad_qpts.reshape(query_rows, -1)], axis=1
    )
    query_grad = lax.psum(query_part, "col")
    grad_kvec = scale_qk * jnp.einsum(
        "hij,ihc->jhc", score_bf, query_vec, preferred_element_type=jnp.float32
    )
    grad_vvec = jnp.einsum("hij,ihc->jhc", weight_bf, grad_vec, preferred_element_type=jnp.float32)
    grad_kpts = grad_coef[None, None, :, None] * (
        key_float * col_score.T[:, None, :, None]
        - jnp.einsum("hij,ixhp->jxhp", score_bf, query_pts, preferred_element_type=jnp.float32)
    )
    grad_vpts = jnp.einsum(
        "hij,ixhv->jxhv", weight_bf, grad_pts, preferred_element_type=jnp.float32
    )
    key_part = jnp.concatenate(
        [
            grad_kvec.reshape(key_rows, -1),
            grad_vvec.reshape(key_rows, -1),
            grad_kpts.reshape(key_rows, -1),
            grad_vpts.reshape(key_rows, -1),
        ],
        axis=1,
    )
    bias_part = LOGIT_WEIGHT * jnp.einsum(
        "ijc,hij->ch", pair, score_bf, preferred_element_type=jnp.float32
    )
    key_weight_float = key_weight.astype(jnp.float32)
    key_single_float = key_single.astype(jnp.float32)
    key_grad = lax.psum(key_part, "row")
    grad_key_single = jnp.dot(key_grad, key_weight_float.T, precision=highest)
    grad_key_weight = lax.psum(jnp.dot(key_single_float.T, key_grad, precision=highest), "col")
    grad_pair_weight = lax.psum(bias_part, ("row", "col"))
    grad_query_single = jnp.dot(query_grad, query_weight.astype(jnp.float32).T, precision=highest)
    grad_query_weight = lax.psum(
        jnp.dot(query_single.astype(jnp.float32).T, query_grad, precision=highest), "row"
    )
    pair_grad = LOGIT_WEIGHT * jnp.einsum(
        "hij,ch->ijc", score_bf, pair_weight, preferred_element_type=jnp.float32
    )
    pair_grad = pair_grad + jnp.einsum(
        "hij,ihc->ijc", weight_bf, grad_pairs, preferred_element_type=jnp.float32
    )
    grad_pair = pair_grad.astype(jnp.bfloat16)
    return (
        grad_query_single,
        grad_key_single,
        grad_query_weight,
        grad_key_weight,
        grad_pair_weight,
        grad_pair,
    )


def solution(mesh):
    in_specs = (
        P("row", None),
        P("col", None),
        P(),
        P(),
        P(),
        P(),
        P(),
        P("row", "col", None),
        P(),
        P(),
        P(),
        P("row", None),
        P("row", None),
        P("row", None),
    )
    out_specs = (P("row", None), P("col", None), P(), P(), P(), P("row", "col", None))
    return jax.shard_map(local, mesh=mesh, in_specs=in_specs, out_specs=out_specs, check_vma=False)
```

profile of v0, /device:TPU:1, one launch (start us, length us, event | category | flops | bytes accessed | tf_op | source)
XLA Modules:
  0.0 589.8 jit_solution(5173191952428739225)
XLA Ops:
  7.2 0.0 copy-start
  7.2 0.0 all-reduce.6.cloned.1.call-start
  7.2 1.3 dynamic_slice.16
  10.5 0.8 dynamic-slice_compare_fusion.1
  11.2 0.8 dynamic_slice.19
  12.0 0.8 dynamic_slice.20
  12.8 0.8 dynamic-slice_compare_fusion
  13.5 1.3 convolution_convert_fusion
  14.9 0.0 copy-start.2
  14.9 0.7 fusion.34
  15.6 1.2 convolution_convert_fusion.1
  16.8 0.1 slice.26
  16.9 0.1 copy.40
  17.0 0.0 copy-start.12
  17.1 0.0 copy-start.9
  17.1 0.1 fusion.26
  17.1 0.1 copy.42
  17.3 1.2 broadcast_multiply_fusion
  18.5 3.4 fusion.32
  21.9 0.6 fusion.9
  22.6 0.1 compare_convert_fusion
  22.7 0.0 copy-done.5
  22.7 0.0 copy-start.17
  22.7 0.0 slice-start
  22.7 0.6 fusion.35
  23.4 41.9 %pmax.7 = f32[12,64]{1,0:T(8,128)S(1)} all-reduce(f32[12,64]{1,0:T(8,128)S(1)} %get-tuple-element.20), channel_id=1, replica_groups=mesh['row'=16,'col'=16] {'col'}, use_global_device_ids=true, to_apply=%region_3.4 | all-reduce | flops 768 | bytes 6144 | tf_op jit(solution)/shard_map/pmax | solution.py:81
  65.3 0.1 copy.48
  65.4 0.0 copy-start.11
  65.4 0.1 reshape.130
  65.6 3.4 fusion.36
  69.0 0.7 copy.47
  69.7 0.3 convolution_bitcast_fusion.1
  70.0 2.5 fusion.17
  72.5 62.8 %all-reduce = (f32[12,64]{1,0:T(8,128)S(1)}, f32[12,64]{1,0:T(8,128)S(1)}) all-reduce(f32[12,64]{1,0:T(8,128)} %get-tuple-element.7, f32[12,64]{1,0:T(8,128)} %get-tuple-element.6), channel_id=1, replica_groups=mesh['row'=16,'col'=16] {'col'}, use_global_device_ids=true, to_apply=%region_7.8 | all-reduce | flops 1536 | bytes 12288 | tf_op jit(solution)/shard_map/psum | solution.py:90
  135.3 1.9 convert_reduce_fusion
  137.2 1.1 convolution_bitcast_fusion.4
  138.3 1.0 fusion.39
  139.3 1.0 convolution_multiply_fusion.1
  140.3 1.1 fusion.11
  141.4 0.1 reshape.135
  141.4 0.0 copy-start.18
  141.5 1.0 pad_maximum_fusion
  142.4 0.0 all-reduce.6.cloned.1.call-update
  142.4 0.0 all-reduce.10.cloned.1.call-start
  142.5 0.2 fusion.13
  142.8 0.2 convolution_multiply_fusion.2
  143.0 0.7 pad_maximum_fusion.1
  143.7 135.0 %all-reduce.6.cloned.1.call-done = f32[256,816]{0,1:T(8,128)} async-done(((f32[256,816]{0,1:T(8,128)}), f32[256,816]{0,1:T(8,128)}) %all-reduce.6.cloned.1.call-update) | async-done | bytes 835600 | tf_op jit(solution)/shard_map/psum | solution.py:138
  278.7 3.0 convolution_bitcast_fusion
  281.7 0.0 all-reduce.10.cloned.1.call-update
  281.7 0.0 all-reduce.8.cloned.1.call-start
  281.8 1.3 fusion.18
  283.1 0.0 copy-start.14
  283.1 4.0 add_convert_fusion
  287.2 161.8 %all-reduce.10.cloned.1.call-done = (f32[64,336]{0,1:T(8,128)}, f32[384,816]{0,1:T(8,128)}) async-done(((f32[64,336]{0,1:T(8,128)}, f32[384,816]{0,1:T(8,128)}), (f32[64,336]{0,1:T(8,128)}, f32[384,816]{0,1:T(8,128)})) %all-reduce.10.cloned.1.call-update) | async-done | bytes 1339408 | tf_op jit(solution)/shard_map/psum | solution.py:112
  449.0 2.1 convolution_bitcast_fusion.3
  451.1 0.0 all-reduce.8.cloned.1.call-update
  451.1 3.1 fusion.15
  454.2 82.8 %psum.55 = f32[128,12]{0,1:T(8,128)} all-reduce(f32[128,12]{0,1:T(8,128)S(1)} %fusion.15), channel_id=1, replica_groups=mesh['row'=16,'col'=16] {'row','col'}, use_global_device_ids=true, to_apply=%region_14.15 | all-reduce | flops 1536 | bytes 12288 | tf_op jit(solution)/shard_map/psum | solution.py:141
  537.0 1.8 fusion.38
  538.8 1.0 fusion.37
  539.8 40.5 %all-reduce.8.cloned.1.call-done = f32[384,336]{0,1:T(8,128)} async-done(((f32[384,336]{0,1:T(8,128)}), f32[384,336]{0,1:T(8,128)}) %all-reduce.8.cloned.1.call-update) | async-done | bytes 516112 | tf_op jit(solution)/shard_map/psum | solution.py:143
  580.4 1.9 copy.89
  582.2 1.0 copy.90
  (44 shorter events, 0.2 us)
Async XLA Ops:
  7.2 6.4 %copy-start = (bf16[384,816]{0,1:T(8,128)(2,1)S(1)}, bf16[384,816]{0,1:T(8,128)(2,1)}, u32[]{:S(2)}) copy-start(bf16[384,816]{0,1:T(8,128)(2,1)} %param.17) | copy-start | bytes 1880068
  7.2 271.5 %all-reduce.6.cloned.1.call-start = ((), (), s32[]{:S(2)}) async-start(), calls=%async_computation | async-start | bytes 1671168 | tf_op jit(solution)/shard_map/psum | solution.py:138
  14.9 7.7 %copy-start.2 = (bf16[256,816]{0,1:T(8,128)(2,1)}, bf16[256,816]{0,1:T(8,128)(2,1)S(1)}, u32[]{:S(2)}) copy-start(bf16[256,816]{0,1:T(8,128)(2,1)S(1)} %convolution_convert_fusion) | copy-start | bytes 1253380
  15.6 7.1 %copy-start.5 = (bf16[256,192]{0,1:T(8,128)(2,1)}, bf16[256,192]{0,1:T(8,128)(2,1)S(1)}, u32[]{:S(2)}) copy-start(bf16[256,192]{0,1:T(8,128)(2,1)S(1)} %get-tuple-element.16) | copy-start | bytes 294916
  15.6 7.1 %copy-start.21 = (f32[12]{0:T(128)S(1)}, f32[12]{0:T(128)}, u32[]{:S(2)}) copy-start(f32[12]{0:T(128)} %param.20) | copy-start | bytes 148
  17.0 6.3 %copy-start.12 = (bf16[64,192]{0,1:T(8,128)(2,1)}, bf16[64,192]{0,1:T(8,128)(2,1)S(1)}, u32[]{:S(2)}) copy-start(bf16[64,192]{0,1:T(8,128)(2,1)S(1)} %copy.40) | copy-start | bytes 73732
  17.1 6.3 %copy-start.9 = (bf16[256,3,12,4]{0,3,2,1:T(4,128)(2,1)}, bf16[256,3,12,4]{0,3,2,1:T(4,128)(2,1)S(1)}, u32[]{:S(2)}) copy-start(bf16[256,3,12,4]{0,3,2,1:T(4,128)(2,1)S(1)} %reshape.125) | copy-start | bytes 221188
  18.5 46.8 %copy-start.16 = (bf16[64,288]{1,0:T(8,128)(2,1)S(1)}, bf16[64,288]{1,0:T(8,128)(2,1)}, u32[]{:S(2)}) copy-start(bf16[64,288]{1,0:T(8,128)(2,1)} %param.26) | copy-start | bytes 110596
  18.5 46.9 %copy-start.13 = (bf16[64,1536]{1,0:T(8,128)(2,1)S(1)}, bf16[64,1536]{1,0:T(8,128)(2,1)}, u32[]{:S(2)}) copy-start(bf16[64,1536]{1,0:T(8,128)(2,1)} %param.27) | copy-start | bytes 589828
  22.7 42.7 %copy-start.15 = (pred[64,256]{1,0:T(8,128)(4,1)}, pred[64,256]{1,0:T(8,128)(4,1)S(1)}, u32[]{:S(2)}) copy-start(pred[64,256]{1,0:T(8,128)(4,1)S(1)} %get-tuple-element.24) | copy-start | bytes 49156
  22.7 46.3 %copy-start.17 = (bf16[64,192]{1,0:T(8,128)(2,1)S(1)}, bf16[64,192]{1,0:T(8,128)(2,1)}, u32[]{:S(2)}) copy-start(bf16[64,192]{1,0:T(8,128)(2,1)} %param.25) | copy-start | bytes 73732
  22.7 47.0 %slice-start = ((bf16[256,816]{0,1:T(8,128)(2,1)}), bf16[256,288]{0,1:T(8,128)(2,1)S(1)}, s32[]{:S(2)}) async-start(bf16[256,816]{0,1:T(8,128)(2,1)} %copy-done.2), calls=%async_computation.3 | async-start | bytes 294912 | tf_op jit(solution)/shard_map/slice | solution.py:53
  65.4 4.6 copy-start.11
  137.2 5.3 copy-start.10
  137.2 5.3 copy-start.19
  137.2 5.3 copy-start.20
  137.2 5.6 copy-start.6
  137.2 141.5 %copy-start.7 = (bf16[256,384]{1,0:T(8,128)(2,1)S(1)}, bf16[256,384]{1,0:T(8,128)(2,1)}, u32[]{:S(2)}) copy-start(bf16[256,384]{1,0:T(8,128)(2,1)} %param.15) | copy-start | bytes 589828
  141.4 140.3 %copy-start.18 = (bf16[128,12]{0,1:T(8,128)(2,1)S(1)}, bf16[128,12]{0,1:T(8,128)(2,1)}, u32[]{:S(2)}) copy-start(bf16[128,12]{0,1:T(8,128)(2,1)} %param.18) | copy-start | bytes 9220
  142.4 306.5 %all-reduce.10.cloned.1.call-start = ((), (), s32[]{:S(2)}) async-start(), calls=%async_computation.2 | async-start | bytes 2850816 | tf_op jit(solution)/shard_map/psum | solution.py:112
  281.7 298.6 %all-reduce.8.cloned.1.call-start = ((), (), s32[]{:S(2)}) async-start(), calls=%async_computation.1 | async-start | bytes 1032192 | tf_op jit(solution)/shard_map/psum | solution.py:143
  283.1 165.9 %copy-start.14 = (bf16[64,384]{1,0:T(8,128)(2,1)S(1)}, bf16[64,384]{1,0:T(8,128)(2,1)}, u32[]{:S(2)}) copy-start(bf16[64,384]{1,0:T(8,128)(2,1)} %param.14) | copy-start | bytes 147460
  287.2 249.9 %copy-start.1 = (f32[256,816]{0,1:T(8,128)S(1)}, f32[256,816]{0,1:T(8,128)}, u32[]{:S(2)}) copy-start(f32[256,816]{0,1:T(8,128)} %all-reduce.6.cloned.1.call-done) | copy-start | bytes 2506756
  287.2 251.7 %copy-start.4 = (bf16[384,336]{0,1:T(8,128)(2,1)S(1)}, bf16[384,336]{0,1:T(8,128)(2,1)}, u32[]{:S(2)}) copy-start(bf16[384,336]{0,1:T(8,128)(2,1)} %param.16) | copy-start | bytes 774148
  449.0 89.9 %copy-start.8 = (f32[64,336]{0,1:T(8,128)S(1)}, f32[64,336]{0,1:T(8,128)}, u32[]{:S(2)}) copy-start(f32[64,336]{0,1:T(8,128)} %get-tuple-element.12) | copy-start | bytes 258052
  451.1 131.1 %copy-start.3 = (f32[384,816]{0,1:T(8,128)S(1)}, f32[384,816]{0,1:T(8,128)}, u32[]{:S(2)}) copy-start(f32[384,816]{0,1:T(8,128)} %get-tuple-element.28) | copy-start | bytes 3760132
Sparse Core Ops, SparseCore 0:
  142.6 136.0 all-reduce.5
  282.2 166.7 all-reduce.9
  452.4 127.9 all-reduce.7
where the time goes:
time: 591 us; the launch traced here: 590 us
  waiting for transfers between devices  337 us (57%)
  blocking collectives  188 us (32%)
  matrix products  34.3 us (6%)
  between operations  16.1 us (3%)
  local copies, waits for them, and re-layouts  7.96 us (1%)
  other arithmetic  6.43 us (1%)
    psum x1, waiting for transfers between devices, local(): query_grad = lax.psum(query_part, 'col')  162 us
    psum x1, waiting for transfers between devices, local(): key_grad = lax.psum(key_part, 'row')  135 us
    psum x1, blocking collectives, local(): grad_pair_weight = lax.psum(bias_part, ('row', 'col'))  82.8 us
    psum x1, blocking collectives, local(): lax.psum((jnp.sum(exp_terms, axis=2), jnp.sum(exp_terms * upstream, axis=...  62.8 us
    pmax x1, blocking collectives, local(): row_top = lax.pmax(jnp.max(logits, axis=2), 'col')  41.9 us
    psum x1, waiting for transfers between devices, local(): lax.psum(jnp.dot(query_single.astype(jnp.float32).T, query_grad, precisio...  40.5 us
  transfers between devices with their start and end apart: 3, of which 3 were waited for; matrix products, arithmetic and copies ran while one was open for 2% of the time, Pallas kernels for 0%

commit v1 on v0

--- a/solution.py
+++ b/solution.py
@@ -10,10 +10,31 @@
 P_SIZE = 4
 PV = 8
 DZ = 128
-
+QF = 336
+KF = 816
+ROWS = 16
+COLS = 16
 
 LOGIT_WEIGHT = math.sqrt(1.0 / 3.0)
 MASKED_LOGIT = -100000.0
+
+
+def exchange(values, axis):
+    return lax.all_to_all(values, axis, 0, 0)
+
+
+def gather(values, axis, parts):
+    return exchange(jnp.broadcast_to(values[None], (parts, *values.shape)), axis)
+
+
+def sum_over_col(values):
+    for step in (1, 4):
+        others = [
+            lax.ppermute(values, "col", [(i, i ^ (step * k)) for i in range(COLS)])
+            for k in (1, 2, 3)
+        ]
+        values = (values + others[0]) + (others[1] + others[2])
+    return values
 
 
 def local(
@@ -78,7 +99,6 @@
     )
     logits = logits + chain_bias[:, None, None] * same_chain[None]
     logits = jnp.where(live_pairs[None], logits, MASKED_LOGIT)
-    row_top = lax.pmax(jnp.max(logits, axis=2), "col")
     upstream = jnp.einsum("ihc,jhc->hij", grad_vec, value_vec, preferred_element_type=jnp.float32)
     upstream = upstream + jnp.einsum(
         "ixhv,jxhv->hij", grad_pts, value_pts, preferred_element_type=jnp.float32
@@ -86,11 +106,18 @@
     upstream = upstream + jnp.einsum(
         "ihc,ijc->hij", grad_pairs, pair, preferred_element_type=jnp.float32
     )
-    exp_terms = jnp.exp(logits - row_top[:, :, None])
-    row_total, moment = lax.psum(
-        (jnp.sum(exp_terms, axis=2), jnp.sum(exp_terms * upstream, axis=2)), "col"
-    )
-    weights = exp_terms / row_total[:, :, None]
+    own_top = jnp.max(logits, axis=2)
+    exp_terms = jnp.exp(logits - own_top[:, :, None])
+    own_total = jnp.sum(exp_terms, axis=2)
+    own_moment = jnp.sum(exp_terms * upstream, axis=2)
+    with jax.named_scope("row_statistics"):
+        parts = jnp.stack([own_top, own_total, own_moment]).reshape(3, 6, 128)
+        parts = gather(parts, "col", COLS).reshape(COLS, 3, H, query_rows)
+        row_top = jnp.max(parts[:, 0], axis=0)
+        shares = jnp.exp(parts[:, 0] - row_top[None])
+        row_total = jnp.sum(shares * parts[:, 1], axis=0)
+        moment = jnp.sum(shares * parts[:, 2], axis=0)
+    weights = exp_terms * (jnp.exp(own_top - row_top) / row_total)[:, :, None]
     centre = moment / row_total
     score_grad = jnp.where(live_pairs[None], weights * (upstream - centre[:, :, None]), 0.0)
     weight_bf = weights.astype(jnp.bfloat16)
@@ -109,40 +136,79 @@
     query_part = jnp.concatenate(
         [grad_qvec.reshape(query_rows, -1), grad_qpts.reshape(query_rows, -1)], axis=1
     )
-    query_grad = lax.psum(query_part, "col")
+    with jax.named_scope("query_sum"):
+        query_grad = sum_over_col(query_part)
     grad_kvec = scale_qk * jnp.einsum(
-        "hij,ihc->jhc", score_bf, query_vec, preferred_element_type=jnp.float32
-    )
-    grad_vvec = jnp.einsum("hij,ihc->jhc", weight_bf, grad_vec, preferred_element_type=jnp.float32)
-    grad_kpts = grad_coef[None, None, :, None] * (
-        key_float * col_score.T[:, None, :, None]
-        - jnp.einsum("hij,ixhp->jxhp", score_bf, query_pts, preferred_element_type=jnp.float32)
+        "hij,ihc->hcj", score_bf, query_vec, preferred_element_type=jnp.float32
+    )
+    grad_vvec = jnp.einsum("hij,ihc->hcj", weight_bf, grad_vec, preferred_element_type=jnp.float32)
+    grad_kpts = grad_coef[None, :, None, None] * (
+        key_float.transpose(1, 2, 3, 0) * col_score[None, :, None, :]
+        - jnp.einsum("hij,ixhp->xhpj", score_bf, query_pts, preferred_element_type=jnp.float32)
     )
     grad_vpts = jnp.einsum(
-        "hij,ixhv->jxhv", weight_bf, grad_pts, preferred_element_type=jnp.float32
+        "hij,ixhv->xhvj", weight_bf, grad_pts, preferred_element_type=jnp.float32
     )
     key_part = jnp.concatenate(
         [
-            grad_kvec.reshape(key_rows, -1),
-            grad_vvec.reshape(key_rows, -1),
-            grad_kpts.reshape(key_rows, -1),
-            grad_vpts.reshape(key_rows, -1),
+            grad_kvec.reshape(-1, key_rows),
+            grad_vvec.reshape(-1, key_rows),
+            grad_kpts.reshape(-1, key_rows),
+            grad_vpts.reshape(-1, key_rows),
         ],
-        axis=1,
+        axis=0,
     )
     bias_part = LOGIT_WEIGHT * jnp.einsum(
-        "ijc,hij->ch", pair, score_bf, preferred_element_type=jnp.float32
-    )
-    key_weight_float = key_weight.astype(jnp.float32)
-    key_single_float = key_single.astype(jnp.float32)
-    key_grad = lax.psum(key_part, "row")
-    grad_key_single = jnp.dot(key_grad, key_weight_float.T, precision=highest)
-    grad_key_weight = lax.psum(jnp.dot(key_single_float.T, key_grad, precision=highest), "col")
-    grad_pair_weight = lax.psum(bias_part, ("row", "col"))
+        "ijc,hij->hc", pair, score_bf, preferred_element_type=jnp.float32
+    )
+    key_single_part = jnp.dot(key_weight.astype(jnp.float32), key_part, precision=highest)
+    with jax.named_scope("key_sum"):
+        sent = jnp.concatenate(
+            [
+                key_part.reshape(ROWS, KF // ROWS, key_rows),
+                jnp.pad(bias_part, ((0, ROWS - H), (0, key_rows - DZ)))[:, None],
+                key_single_part.reshape(ROWS, -1, key_rows),
+            ],
+            axis=1,
+        )
+        summed = jnp.sum(exchange(sent, "row"), axis=0)
+    feats = KF // ROWS
+    key_share = jnp.dot(
+        summed[:feats], key_single.astype(jnp.float32), precision=highest
+    )
+    share = jnp.concatenate(
+        [key_share, jnp.pad(summed[feats : feats + 1], ((0, 0), (0, 384 - key_rows)))], axis=0
+    )
+    with jax.named_scope("key_weight_sum"):
+        share = sum_over_col(share)
     grad_query_single = jnp.dot(query_grad, query_weight.astype(jnp.float32).T, precision=highest)
-    grad_query_weight = lax.psum(
-        jnp.dot(query_single.astype(jnp.float32).T, query_grad, precision=highest), "row"
-    )
+    query_weight_part = lax.dot_general(
+        query_grad, query_single.astype(jnp.float32), (((0,), (0,)), ((), ())), precision=highest
+    )
+    with jax.named_scope("query_weight_sum"):
+        single = summed[feats + 1 :]
+        lanes = [
+            query_weight_part[:, 128 * k : 128 * (k + 1)].reshape(ROWS, QF // ROWS, 128)
+            for k in range(3)
+        ] + [
+            jnp.broadcast_to(single[None, :, 128 * k : 128 * (k + 1)], (ROWS, 24, 128))
+            for k in range(2)
+        ]
+        got = exchange(jnp.concatenate(lanes, axis=1), "row")
+        step = QF // ROWS
+        query_share = jnp.sum(got[:, : 3 * step], axis=0)
+        query_share = jnp.concatenate(
+            [query_share[step * k : step * (k + 1)] for k in range(3)], axis=1
+        )
+        grad_key_single = jnp.concatenate(
+            [got[:, 3 * step : 3 * step + 24].reshape(384, 128), got[:, 3 * step + 24 :].reshape(384, 128)],
+            axis=1,
+        ).T
+    with jax.named_scope("weight_gather"):
+        full = gather(jnp.concatenate([share, query_share], axis=0), "row", ROWS)
+        grad_key_weight = full[:, :feats].reshape(KF, -1).T
+        grad_pair_weight = full[:H, feats, :DZ].T
+        grad_query_weight = full[:, feats + 1 :].reshape(QF, -1).T
     pair_grad = LOGIT_WEIGHT * jnp.einsum(
         "hij,ch->ijc", score_bf, pair_weight, preferred_element_type=jnp.float32
     )

time: 591 us -> 202 us (0.34)
  waiting for transfers between devices: 337 us -> 72.6 us
  blocking collectives: 188 us -> 22.3 us
  starting transfers between devices: 0.12 us -> 35.2 us
  local copies, waits for them, and re-layouts: 7.96 us -> 31 us
  between operations: 16.1 us -> 3.12 us
  matrix products: 34.3 us -> 24.7 us
    psum x3 -> x0, waiting for transfers between devices: 337 us -> none  [the longest x1 162 us: local(): query_grad = lax.psum(query_part, 'col')]
    psum x2 -> x0, blocking collectives: 146 us -> none  [the longest x1 82.8 us: local(): grad_pair_weight = lax.psum(bias_part, ('row', 'col'))]
    ppermute x0 -> x12, waiting for transfers between devices: none -> 55.3 us  [sum_over_col(): lax.ppermute(values, 'col', [(i, i ^ step * k) for i in range(COLS)])]
    pmax x1 -> x0, blocking collectives: 41.9 us -> none  [local(): row_top = lax.pmax(jnp.max(logits, axis=2), 'col')]
    all_to_all x0 -> x1, blocking collectives: none -> 22.3 us  [exchange(): return lax.all_to_all(values, axis, 0, 0)]
    ppermute x0 -> x12, starting transfers between devices: none -> 18.6 us  [sum_over_col(): lax.ppermute(values, 'col', [(i, i ^ step * k) for i in range(COLS)])]
    all_to_all x0 -> x3, waiting for transfers between devices: none -> 17.3 us  [exchange(): return lax.all_to_all(values, axis, 0, 0)]
    all_to_all x0 -> x3, starting transfers between devices: none -> 16.6 us  [exchange(): return lax.all_to_all(values, axis, 0, 0)]
  transfers between devices with their start and end apart: 3 -> 15, of which waited for: 3 -> 10; matrix products, arithmetic and copies ran while one was open for 2% -> 6% of each run, Pallas kernels for 0% -> 0%
where the time goes in v1:
time: 202 us; the launch traced here: 201 us
  waiting for transfers between devices  72.6 us (36%)
  starting transfers between devices  35.2 us (17%)
  local copies, waits for them, and re-layouts  31 us (15%)
  matrix products  24.7 us (12%)
  blocking collectives  22.3 us (11%)
  other arithmetic  11.9 us (6%)
  between operations  3.12 us (2%)
    ppermute x12, waiting for transfers between devices, sum_over_col(): lax.ppermute(values, 'col', [(i, i ^ step * k) for i in range(COLS)])  55.3 us
    all_to_all x1, blocking collectives, exchange(): return lax.all_to_all(values, axis, 0, 0)  22.3 us
    ppermute x12, starting transfers between devices, sum_over_col(): lax.ppermute(values, 'col', [(i, i ^ step * k) for i in range(COLS)])  18.6 us
    all_to_all x3, waiting for transfers between devices, exchange(): return lax.all_to_all(values, axis, 0, 0)  17.3 us
    all_to_all x3, starting transfers between devices, exchange(): return lax.all_to_all(values, axis, 0, 0)  16.6 us
    concatenate x1, local copies, waits for them, and re-layouts, local(): got = exchange(jnp.concatenate(lanes, axis=1), 'row')  7.1 us
    unnamed x50, local copies, waits for them, and re-layouts  4.85 us
    dot_general x1, matrix products, local(): jnp.einsum('hij,ihc->ijc', weight_bf, grad_pairs, preferred_element_type=...  4.05 us
  transfers between devices with their start and end apart: 15, of which 10 were waited for; matrix products, arithmetic and copies ran while one was open for 6% of the time, Pallas kernels for 0%

profile of v1, /device:TPU:1, one launch (start us, length us, event | category | flops | bytes accessed | tf_op | source)
XLA Modules:
  0.0 200.7 jit_solution(16664716064322212315)
XLA Ops:
  0.7 1.3 dynamic_slice.16
  3.9 1.3 dynamic-slice_compare_fusion.1
  5.2 1.3 dynamic_slice.19
  6.5 0.8 dynamic_slice.20
  7.3 1.4 dynamic-slice_compare_fusion
  8.7 1.3 convolution_convert_fusion
  10.0 0.7 fusion.40
  10.7 1.2 convolution_convert_fusion.1
  12.1 0.7 fusion.23
  13.6 1.2 broadcast_multiply_fusion
  14.8 1.5 copy.80
  16.3 1.1 reshape.184
  17.5 3.5 %fusion.36 = f32[12,64,256]{2,0,1:T(8,128)S(1)} fusion(bf16[64,256,128]{2,1,0:T(8,128)(2,1)} %param.21, bf16[128,12]{0,1:T(8,128)(2,1)} %param.18), kind=kOutput, calls=%fused_computation.82 | convolution fusion | flops 50331648 | bytes 4983808 | tf_op jit(solution)/shard_map/ijc,ch->hij/dot_general | solution.py:95
  21.0 1.2 fusion.44
  22.2 1.5 copy.79
  24.3 0.8 compare_convert_fusion
  25.1 1.5 fusion.43
  27.3 2.5 %fusion.19 = (f32[12,64]{1,0:T(8,128)}, f32[12,64]{1,0:T(8,128)}, f32[12,64,256]{2,1,0:T(8,128)S(1)}) fusion(f32[12,64,256]{2,1,0:T(8,128)S(1)} %get-tuple-element.43, f32[12,64]{1,0:T(8,128)S(1)} %get-tuple-element.42, f32[64,256,12]{1,2,0:T(8,128)S(1)} %fusion.44, f32[12,256,64]{1,2,0:T(8,128)S(1)} %convolution_bitcast_fusion, ...), kind=kOutput, calls=%fused_computation.42 | convolution fusion | flops 7469568 | bytes 3277824 | tf_op jit(solution)/shard_map/ihc,jhc->hij/dot_general | solution.py:102
  29.7 0.8 stack.13
  30.5 0.8 stack.14
  31.3 22.3 %all_to_all.20 = f32[16,3,6,128]{3,2,1,0:T(8,128)S(1)} all-to-all(f32[16,3,6,128]{3,2,1,0:T(8,128)S(1)} %broadcast_in_dim.33), channel_id=1, replica_groups=mesh['row'=16,'col'=16] {'col'}, dimensions={0} | all-to-all | bytes 294912 | tf_op jit(solution)/shard_map/row_statistics/all_to_all | solution.py:23
  53.8 0.7 exponential_divide_fusion
  54.5 1.9 convert_reduce_fusion
  56.6 1.0 fusion.47
  57.9 0.7 reshape.193
  58.7 1.1 pad_maximum_fusion.1
  59.8 2.9 %convolution_bitcast_fusion.2 = f32[384,256]{0,1:T(8,128)} fusion(bf16[384,816]{0,1:T(8,128)(2,1)S(1)} %copy-done, f32[288,256]{1,0:T(8,128)S(1)} %bitcast.164, f32[144,256]{1,0:T(8,128)} %reshape.193, f32[192,256]{1,0:T(8,128)S(1)} %bitcast.170, f32[192,256]{1,0:T(8,128)S(1)} %bitcast.172), kind=kOutput, calls=%fused_computation.17 | convolution fusion | flops 963219456 | bytes 1855488 | tf_op jit(solution)/shard_map/dot_general | solution.py:164
  62.7 0.8 fusion.14
  63.6 1.2 copy.91
  64.8 1.2 pad_maximum_fusion
  66.0 7.0 %all-to-all-start.1 = ((f32[16,76,256]{2,1,0:T(8,128)}), f32[16,76,256]{2,1,0:T(8,128)S(1)}, u32[]{:S(2)}, u32[]{:S(2)}) async-start(f32[16,76,256]{2,1,0:T(8,128)} %pad_maximum_fusion), calls=%async_computation.1 | async-start | bytes 2621440 | tf_op jit(solution)/shard_map/key_sum/all_to_all | solution.py:23
  73.9 1.8 collective-permute-start.1
  75.7 3.6 %collective-permute-start.2 = (f32[64,336]{0,1:T(8,128)S(1)}, f32[64,336]{0,1:T(8,128)S(1)}, u32[]{:S(2)}, u32[]{:S(2)}) collective-permute-start(f32[64,336]{0,1:T(8,128)S(1)} %pad_maximum_fusion.2), channel_id=1, source_target_pairs={{0,3},{1,2},{2,1},{3,0},{4,7},{5,6},{6,5},{7,4},{8,11},{9,10},{10,... | collective-permute-start | bytes 258056 | tf_op jit(solution)/shard_map/query_sum/ppermute | solution.py:33
  79.3 20.2 %collective-permute-done = f32[64,336]{0,1:T(8,128)S(1)} collective-permute-done((f32[64,336]{0,1:T(8,128)S(1)}, f32[64,336]{0,1:T(8,128)S(1)}, u32[]{:S(2)}, u32[]{:S(2)}) %collective-permute-start) | collective-permute-done | bytes 86048 | tf_op jit(solution)/shard_map/query_sum/ppermute | solution.py:33
  99.5 4.6 %collective-permute-done.1 = f32[64,336]{0,1:T(8,128)S(1)} collective-permute-done((f32[64,336]{0,1:T(8,128)S(1)}, f32[64,336]{0,1:T(8,128)S(1)}, u32[]{:S(2)}, u32[]{:S(2)}) %collective-permute-start.1) | collective-permute-done | bytes 86048 | tf_op jit(solution)/shard_map/query_sum/ppermute | solution.py:33
  104.6 1.9 collective-permute-start.4
  106.5 1.6 collective-permute-start.5
  108.1 1.5 collective-permute-done.3
  109.6 4.5 %collective-permute-done.4 = f32[64,336]{0,1:T(8,128)S(1)} collective-permute-done((f32[64,336]{0,1:T(8,128)S(1)}, f32[64,336]{0,1:T(8,128)S(1)}, u32[]{:S(2)}, u32[]{:S(2)}) %collective-permute-start.4) | collective-permute-done | bytes 86048 | tf_op jit(solution)/shard_map/query_sum/ppermute | solution.py:33
  114.1 2.8 %collective-permute-done.5 = f32[64,336]{0,1:T(8,128)S(1)} collective-permute-done((f32[64,336]{0,1:T(8,128)S(1)}, f32[64,336]{0,1:T(8,128)S(1)}, u32[]{:S(2)}, u32[]{:S(2)}) %collective-permute-start.5) | collective-permute-done | bytes 86048 | tf_op jit(solution)/shard_map/query_sum/ppermute | solution.py:33
  117.3 0.7 fusion.39
  118.0 0.9 reshape.190
  119.0 0.7 reduce_sum.98
  119.7 0.8 fusion.41
  120.6 7.1 %concatenate.28 = f32[16,111,128]{2,1,0:T(8,128)} concatenate(f32[16,21,128]{2,1,0:T(8,128)S(1)} %reshape.188, f32[16,21,128]{2,1,0:T(8,128)S(1)} %reshape.189, f32[16,21,128]{2,1,0:T(8,128)S(1)} %reshape.190, f32[16,24,128]{2,1,0:T(8,128)S(1)} %broadcast_in_dim.36, f32[16,24,128]{2,1,0:T(8,128)S(1)} %broadcast_in_dim.37), dimensions={1} | concatenate | bytes 1818624 | tf_op jit(solution)/shard_map/query_weight_sum/concatenate | solution.py:197
  127.7 4.7 %all-to-all-start.2 = ((f32[16,111,128]{2,1,0:T(8,128)}), f32[16,111,128]{2,1,0:T(8,128)S(1)}, u32[]{:S(2)}, u32[]{:S(2)}) async-start(f32[16,111,128]{2,1,0:T(8,128)} %concatenate.28), calls=%async_computation.2 | async-start | bytes 1835008 | tf_op jit(solution)/shard_map/query_weight_sum/all_to_all | solution.py:23
  132.6 2.7 %collective-permute-start.6 = (f32[52,384]{1,0:T(8,128)S(1)}, f32[52,384]{1,0:T(8,128)S(1)}, u32[]{:S(2)}, u32[]{:S(2)}) collective-permute-start(f32[52,384]{1,0:T(8,128)S(1)} %select_maximum_fusion), channel_id=1, source_target_pairs={{0,1},{1,0},{2,3},{3,2},{4,5},{5,4},{6,7},{7,6},{8,9},{9,8},{10,11... | collective-permute-start | bytes 239624 | tf_op jit(solution)/shard_map/key_weight_sum/ppermute | solution.py:33
  135.4 3.3 %collective-permute-start.7 = (f32[52,384]{1,0:T(8,128)S(1)}, f32[52,384]{1,0:T(8,128)S(1)}, u32[]{:S(2)}, u32[]{:S(2)}) collective-permute-start(f32[52,384]{1,0:T(8,128)S(1)} %select_maximum_fusion), channel_id=1, source_target_pairs={{0,2},{1,3},{2,0},{3,1},{4,6},{5,7},{6,4},{7,5},{8,10},{9,11},{10,... | collective-permute-start | bytes 239624 | tf_op jit(solution)/shard_map/key_weight_sum/ppermute | solution.py:33
  138.7 7.6 %collective-permute-done.6 = f32[52,384]{1,0:T(8,128)S(1)} collective-permute-done((f32[52,384]{1,0:T(8,128)S(1)}, f32[52,384]{1,0:T(8,128)S(1)}, u32[]{:S(2)}, u32[]{:S(2)}) %collective-permute-start.6) | collective-permute-done | bytes 79904 | tf_op jit(solution)/shard_map/key_weight_sum/ppermute | solution.py:33
  146.3 9.2 %collective-permute-done.7 = f32[52,384]{1,0:T(8,128)S(1)} collective-permute-done((f32[52,384]{1,0:T(8,128)S(1)}, f32[52,384]{1,0:T(8,128)S(1)}, u32[]{:S(2)}, u32[]{:S(2)}) %collective-permute-start.7) | collective-permute-done | bytes 79904 | tf_op jit(solution)/shard_map/key_weight_sum/ppermute | solution.py:33
  156.0 1.8 collective-permute-start.11
  158.3 2.3 %collective-permute-done.10 = f32[52,384]{1,0:T(8,128)S(1)} collective-permute-done((f32[52,384]{1,0:T(8,128)S(1)}, f32[52,384]{1,0:T(8,128)S(1)}, u32[]{:S(2)}, u32[]{:S(2)}) %collective-permute-start.10) | collective-permute-done | bytes 79904 | tf_op jit(solution)/shard_map/key_weight_sum/ppermute | solution.py:33
  160.5 2.7 %collective-permute-done.11 = f32[52,384]{1,0:T(8,128)S(1)} collective-permute-done((f32[52,384]{1,0:T(8,128)S(1)}, f32[52,384]{1,0:T(8,128)S(1)}, u32[]{:S(2)}, u32[]{:S(2)}) %collective-permute-start.11) | collective-permute-done | bytes 79904 | tf_op jit(solution)/shard_map/key_weight_sum/ppermute | solution.py:33
  163.4 1.5 broadcast_in_dim.38
  164.9 4.9 %all-to-all-start.3 = ((f32[16,73,384]{2,1,0:T(8,128)}), f32[16,73,384]{2,1,0:T(8,128)S(1)}, u32[]{:S(2)}, u32[]{:S(2)}) async-start(f32[16,73,384]{2,1,0:T(8,128)} %broadcast_in_dim.38), calls=%async_computation.3 | async-start | bytes 3932160 | tf_op jit(solution)/shard_map/weight_gather/all_to_all | solution.py:23
  169.8 1.3 fusion.15
  171.1 4.1 %add_convert_fusion = bf16[64,256,128]{2,1,0:T(8,128)(2,1)} fusion(f32[64,256,128]{2,1,0:T(8,128)S(1)} %fusion.15, bf16[64,12,128]{2,1,0:T(8,128)(2,1)S(1)} %copy-done.5, bf16[12,64,256]{2,1,0:T(8,128)(2,1)S(1)} %get-tuple-element.27), kind=kOutput, calls=%fused_computation | convolution fusion | flops 56623104 | bytes 13172736 | tf_op jit(solution)/shard_map/hij,ihc->ijc/dot_general | solution.py:215
  175.2 1.0 fusion.45
  176.2 1.1 fusion.38
  177.3 0.9 copy.95
  178.2 17.3 %all-to-all-done.3 = f32[16,73,384]{2,1,0:T(8,128)S(1)} async-done(((f32[16,73,384]{2,1,0:T(8,128)}), f32[16,73,384]{2,1,0:T(8,128)S(1)}, u32[]{:S(2)}, u32[]{:S(2)}) %all-to-all-start.3) | async-done | bytes 1794080 | tf_op jit(solution)/shard_map/weight_gather/all_to_all | solution.py:23
  195.5 1.2 slice.127
  196.7 2.5 %reshape.200 = f32[816,384]{1,0:T(8,128)} reshape(f32[16,51,384]{2,1,0:T(8,128)} %slice.127) | data formatting | bytes 2506752 | tf_op jit(solution)/shard_map/weight_gather/reshape | solution.py:209
  199.3 0.9 reshape.199
  (103 shorter events, 6.9 us)
Async XLA Ops:
  0.6 8.0 %copy-start = (bf16[384,816]{0,1:T(8,128)(2,1)S(1)}, bf16[384,816]{0,1:T(8,128)(2,1)}, u32[]{:S(2)}) copy-start(bf16[384,816]{0,1:T(8,128)(2,1)} %param.17) | copy-start | bytes 1880068
  10.0 12.2 %copy-start.6 = (bf16[256,816]{0,1:T(8,128)(2,1)}, bf16[256,816]{0,1:T(8,128)(2,1)S(1)}, u32[]{:S(2)}) copy-start(bf16[256,816]{0,1:T(8,128)(2,1)S(1)} %convolution_convert_fusion) | copy-start | bytes 1253380
  12.1 5.3 %copy-start.9 = (bf16[256,3,12,4]{0,3,2,1:T(4,128)(2,1)}, bf16[256,3,12,4]{0,3,2,1:T(4,128)(2,1)S(1)}, u32[]{:S(2)}) copy-start(bf16[256,3,12,4]{0,3,2,1:T(4,128)(2,1)S(1)} %reshape.179) | copy-start | bytes 221188
  12.9 4.5 %copy-start.15 = (bf16[64,144]{0,1:T(8,128)(2,1)}, bf16[64,144]{0,1:T(8,128)(2,1)S(1)}, u32[]{:S(2)}) copy-start(bf16[64,144]{0,1:T(8,128)(2,1)S(1)} %copy.77) | copy-start | bytes 55300
  17.4 4.8 %copy-start.4 = (bf16[64,12,128]{2,1,0:T(8,128)(2,1)}, bf16[64,12,128]{2,1,0:T(8,128)(2,1)S(1)}, u32[]{:S(2)}) copy-start(bf16[64,12,128]{2,1,0:T(8,128)(2,1)S(1)} %reshape.184) | copy-start | bytes 589828
  17.4 3.6 %copy-start.1 = (bf16[64,256,128]{2,1,0:T(8,128)(2,1)S(1)}, bf16[64,256,128]{2,1,0:T(8,128)(2,1)}, u32[]{:S(2)}) copy-start(bf16[64,256,128]{2,1,0:T(8,128)(2,1)} %param.21) | copy-start | bytes 12582916
  23.7 3.0 %slice-start = ((bf16[256,816]{0,1:T(8,128)(2,1)}), bf16[256,288]{0,1:T(8,128)(2,1)S(1)}, s32[]{:S(2)}) async-start(bf16[256,816]{0,1:T(8,128)(2,1)} %copy-done.6), calls=%async_computation.4 | async-start | bytes 294912 | tf_op jit(solution)/shard_map/slice | solution.py:74
  23.7 3.0 %copy-start.12 = (bf16[64,288]{0,1:T(8,128)(2,1)S(1)}, bf16[64,288]{0,1:T(8,128)(2,1)}, u32[]{:S(2)}) copy-start(bf16[64,288]{0,1:T(8,128)(2,1)} %copy.80) | copy-start | bytes 110596
  23.7 3.5 %copy-start.13 = (bf16[64,192]{0,1:T(8,128)(2,1)S(1)}, bf16[64,192]{0,1:T(8,128)(2,1)}, u32[]{:S(2)}) copy-start(bf16[64,192]{0,1:T(8,128)(2,1)} %copy.79) | copy-start | bytes 73732
  25.1 1.9 copy-start.19
  26.7 0.6 copy-start.18
  27.3 30.5 %copy-start.22 = (f32[12]{0:T(128)S(1)}, f32[12]{0:T(128)}, u32[]{:S(2)}) copy-start(f32[12]{0:T(128)} %get-tuple-element.40) | copy-start | bytes 148
  29.7 28.0 %copy-start.10 = (bf16[256,3,12,4]{0,3,2,1:T(4,128)(2,1)S(1)}, bf16[256,3,12,4]{0,3,2,1:T(4,128)(2,1)}, u32[]{:S(2)}) copy-start(bf16[256,3,12,4]{0,3,2,1:T(4,128)(2,1)} %copy-done.9) | copy-start | bytes 221188
  29.7 28.0 %copy-start.16 = (bf16[64,144]{0,1:T(8,128)(2,1)S(1)}, bf16[64,144]{0,1:T(8,128)(2,1)}, u32[]{:S(2)}) copy-start(bf16[64,144]{0,1:T(8,128)(2,1)} %copy-done.15) | copy-start | bytes 55300
  58.7 4.0 %copy-start.2 = (bf16[64,256,128]{2,1,0:T(8,128)(2,1)S(1)}, bf16[64,256,128]{2,1,0:T(8,128)(2,1)}, u32[]{:S(2)}) copy-start(bf16[64,256,128]{2,1,0:T(8,128)(2,1)} %param.21) | copy-start | bytes 12582916
  63.5 9.5 %copy-start.11 = (bf16[256,3,12,4]{0,3,2,1:T(4,128)(2,1)S(1)}, bf16[256,3,12,4]{0,3,2,1:T(4,128)(2,1)}, u32[]{:S(2)}) copy-start(bf16[256,3,12,4]{0,3,2,1:T(4,128)(2,1)} %copy-done.9) | copy-start | bytes 221188
  63.5 9.5 %copy-start.21 = (f32[12,64]{1,0:T(8,128)S(1)}, f32[12,64]{1,0:T(8,128)}, u32[]{:S(2)}) copy-start(f32[12,64]{1,0:T(8,128)} %get-tuple-element.23) | copy-start | bytes 9220
  64.8 52.1 %copy-start.17 = (bf16[64,384]{1,0:T(8,128)(2,1)S(1)}, bf16[64,384]{1,0:T(8,128)(2,1)}, u32[]{:S(2)}) copy-start(bf16[64,384]{1,0:T(8,128)(2,1)} %param.14) | copy-start | bytes 147460
  66.0 53.0 %all-to-all-start.1 = ((f32[16,76,256]{2,1,0:T(8,128)}), f32[16,76,256]{2,1,0:T(8,128)S(1)}, u32[]{:S(2)}, u32[]{:S(2)}) async-start(f32[16,76,256]{2,1,0:T(8,128)} %pad_maximum_fusion), calls=%async_computation.1 | async-start | bytes 2621440 | tf_op jit(solution)/shard_map/key_sum/all_to_all | solution.py:23
  73.5 26.0 %collective-permute-start = (f32[64,336]{0,1:T(8,128)S(1)}, f32[64,336]{0,1:T(8,128)S(1)}, u32[]{:S(2)}, u32[]{:S(2)}) collective-permute-start(f32[64,336]{0,1:T(8,128)S(1)} %pad_maximum_fusion.2), channel_id=1, source_target_pairs={{0,1},{1,0},{2,3},{3,2},{4,5},{5,4},{6,7},{7,6},{8,9},{9,8},{10,11... | collective-permute-start | bytes 258056 | tf_op jit(solution)/shard_map/query_sum/ppermute | solution.py:33
  73.9 30.3 %collective-permute-start.1 = (f32[64,336]{0,1:T(8,128)S(1)}, f32[64,336]{0,1:T(8,128)S(1)}, u32[]{:S(2)}, u32[]{:S(2)}) collective-permute-start(f32[64,336]{0,1:T(8,128)S(1)} %pad_maximum_fusion.2), channel_id=1, source_target_pairs={{0,2},{1,3},{2,0},{3,1},{4,6},{5,7},{6,4},{7,5},{8,10},{9,11},{10,... | collective-permute-start | bytes 258056 | tf_op jit(solution)/shard_map/query_sum/ppermute | solution.py:33
  75.7 28.5 %collective-permute-start.2 = (f32[64,336]{0,1:T(8,128)S(1)}, f32[64,336]{0,1:T(8,128)S(1)}, u32[]{:S(2)}, u32[]{:S(2)}) collective-permute-start(f32[64,336]{0,1:T(8,128)S(1)} %pad_maximum_fusion.2), channel_id=1, source_target_pairs={{0,3},{1,2},{2,1},{3,0},{4,7},{5,6},{6,5},{7,4},{8,11},{9,10},{10,... | collective-permute-start | bytes 258056 | tf_op jit(solution)/shard_map/query_sum/ppermute | solution.py:33
  104.2 5.4 %collective-permute-start.3 = (f32[64,336]{0,1:T(8,128)S(1)}, f32[64,336]{0,1:T(8,128)S(1)}, u32[]{:S(2)}, u32[]{:S(2)}) collective-permute-start(f32[64,336]{0,1:T(8,128)S(1)} %add_add_fusion.1), channel_id=1, source_target_pairs={{0,4},{1,5},{2,6},{3,7},{4,0},{5,1},{6,2},{7,3},{8,12},{9,13},{10,... | collective-permute-start | bytes 258056 | tf_op jit(solution)/shard_map/query_sum/ppermute | solution.py:33
  104.6 9.5 %collective-permute-start.4 = (f32[64,336]{0,1:T(8,128)S(1)}, f32[64,336]{0,1:T(8,128)S(1)}, u32[]{:S(2)}, u32[]{:S(2)}) collective-permute-start(f32[64,336]{0,1:T(8,128)S(1)} %add_add_fusion.1), channel_id=1, source_target_pairs={{0,8},{1,9},{2,10},{3,11},{4,12},{5,13},{6,14},{7,15},{8,0},{9,1},... | collective-permute-start | bytes 258056 | tf_op jit(solution)/shard_map/query_sum/ppermute | solution.py:33
  106.5 10.4 %collective-permute-start.5 = (f32[64,336]{0,1:T(8,128)S(1)}, f32[64,336]{0,1:T(8,128)S(1)}, u32[]{:S(2)}, u32[]{:S(2)}) collective-permute-start(f32[64,336]{0,1:T(8,128)S(1)} %add_add_fusion.1), channel_id=1, source_target_pairs={{0,12},{1,13},{2,14},{3,15},{4,8},{5,9},{6,10},{7,11},{8,4},{9,5},... | collective-permute-start | bytes 258056 | tf_op jit(solution)/shard_map/query_sum/ppermute | solution.py:33
  119.7 12.6 %copy-start.14 = (f32[76,256]{1,0:T(8,128)S(1)}, f32[76,256]{1,0:T(8,128)}, u32[]{:S(2)}) copy-start(f32[76,256]{1,0:T(8,128)} %reduce_sum.98) | copy-start | bytes 233476
  119.7 12.7 %copy-start.8 = (bf16[256,384]{1,0:T(8,128)(2,1)S(1)}, bf16[256,384]{1,0:T(8,128)(2,1)}, u32[]{:S(2)}) copy-start(bf16[256,384]{1,0:T(8,128)(2,1)} %param.15) | copy-start | bytes 589828
  127.7 35.6 %all-to-all-start.2 = ((f32[16,111,128]{2,1,0:T(8,128)}), f32[16,111,128]{2,1,0:T(8,128)S(1)}, u32[]{:S(2)}, u32[]{:S(2)}) async-start(f32[16,111,128]{2,1,0:T(8,128)} %concatenate.28), calls=%async_computation.2 | async-start | bytes 1835008 | tf_op jit(solution)/shard_map/query_weight_sum/all_to_all | solution.py:23
  132.3 37.4 %copy-start.20 = (bf16[128,12]{0,1:T(8,128)(2,1)S(1)}, bf16[128,12]{0,1:T(8,128)(2,1)}, u32[]{:S(2)}) copy-start(bf16[128,12]{0,1:T(8,128)(2,1)} %param.18) | copy-start | bytes 9220
  132.6 13.7 %collective-permute-start.6 = (f32[52,384]{1,0:T(8,128)S(1)}, f32[52,384]{1,0:T(8,128)S(1)}, u32[]{:S(2)}, u32[]{:S(2)}) collective-permute-start(f32[52,384]{1,0:T(8,128)S(1)} %select_maximum_fusion), channel_id=1, source_target_pairs={{0,1},{1,0},{2,3},{3,2},{4,5},{5,4},{6,7},{7,6},{8,9},{9,8},{10,11... | collective-permute-start | bytes 239624 | tf_op jit(solution)/shard_map/key_weight_sum/ppermute | solution.py:33
  135.4 20.1 %collective-permute-start.7 = (f32[52,384]{1,0:T(8,128)S(1)}, f32[52,384]{1,0:T(8,128)S(1)}, u32[]{:S(2)}, u32[]{:S(2)}) collective-permute-start(f32[52,384]{1,0:T(8,128)S(1)} %select_maximum_fusion), channel_id=1, source_target_pairs={{0,2},{1,3},{2,0},{3,1},{4,6},{5,7},{6,4},{7,5},{8,10},{9,11},{10,... | collective-permute-start | bytes 239624 | tf_op jit(solution)/shard_map/key_weight_sum/ppermute | solution.py:33
  138.7 16.8 %collective-permute-start.8 = (f32[52,384]{1,0:T(8,128)S(1)}, f32[52,384]{1,0:T(8,128)S(1)}, u32[]{:S(2)}, u32[]{:S(2)}) collective-permute-start(f32[52,384]{1,0:T(8,128)S(1)} %select_maximum_fusion), channel_id=1, source_target_pairs={{0,3},{1,2},{2,1},{3,0},{4,7},{5,6},{6,5},{7,4},{8,11},{9,10},{10,... | collective-permute-start | bytes 239624 | tf_op jit(solution)/shard_map/key_weight_sum/ppermute | solution.py:33
  155.5 5.0 %collective-permute-start.10 = (f32[52,384]{1,0:T(8,128)S(1)}, f32[52,384]{1,0:T(8,128)S(1)}, u32[]{:S(2)}, u32[]{:S(2)}) collective-permute-start(f32[52,384]{1,0:T(8,128)S(1)} %add_add_fusion.3), channel_id=1, source_target_pairs={{0,8},{1,9},{2,10},{3,11},{4,12},{5,13},{6,14},{7,15},{8,0},{9,1},... | collective-permute-start | bytes 239624 | tf_op jit(solution)/shard_map/key_weight_sum/ppermute | solution.py:33
  156.0 7.3 %collective-permute-start.11 = (f32[52,384]{1,0:T(8,128)S(1)}, f32[52,384]{1,0:T(8,128)S(1)}, u32[]{:S(2)}, u32[]{:S(2)}) collective-permute-start(f32[52,384]{1,0:T(8,128)S(1)} %add_add_fusion.3), channel_id=1, source_target_pairs={{0,12},{1,13},{2,14},{3,15},{4,8},{5,9},{6,10},{7,11},{8,4},{9,5},... | collective-permute-start | bytes 239624 | tf_op jit(solution)/shard_map/key_weight_sum/ppermute | solution.py:33
  157.8 5.4 %collective-permute-start.9 = (f32[52,384]{1,0:T(8,128)S(1)}, f32[52,384]{1,0:T(8,128)S(1)}, u32[]{:S(2)}, u32[]{:S(2)}) collective-permute-start(f32[52,384]{1,0:T(8,128)S(1)} %add_add_fusion.3), channel_id=1, source_target_pairs={{0,4},{1,5},{2,6},{3,7},{4,0},{5,1},{6,2},{7,3},{8,12},{9,13},{10,... | collective-permute-start | bytes 239624 | tf_op jit(solution)/shard_map/key_weight_sum/ppermute | solution.py:33
  163.3 1.6 copy-start.3
  164.9 30.6 %all-to-all-start.3 = ((f32[16,73,384]{2,1,0:T(8,128)}), f32[16,73,384]{2,1,0:T(8,128)S(1)}, u32[]{:S(2)}, u32[]{:S(2)}) async-start(f32[16,73,384]{2,1,0:T(8,128)} %broadcast_in_dim.38), calls=%async_computation.3 | async-start | bytes 3932160 | tf_op jit(solution)/shard_map/weight_gather/all_to_all | solution.py:23
  169.8 1.3 copy-start.5
  171.1 4.1 %copy-start.7 = (bf16[384,336]{0,1:T(8,128)(2,1)S(1)}, bf16[384,336]{0,1:T(8,128)(2,1)}, u32[]{:S(2)}) copy-start(bf16[384,336]{0,1:T(8,128)(2,1)} %param.16) | copy-start | bytes 774148

commit v2 on v0

v2 whole, which is shorter than its diff:
```python
import math

import jax
import jax.numpy as jnp
from jax import lax
from jax.experimental import pallas as pl
from jax.experimental.pallas import tpu as pltpu
from jax.sharding import PartitionSpec as P

H = 12
C = 16
P_SIZE = 4
PV = 8
DZ = 128
DS = 384
QB = 64
KB = 256
QF = 336
KF = 816
VEC = H * C
QPTS = 3 * H * P_SIZE
VPTS = 3 * H * PV
ROWS = 16
COLS = 16
HP = 16
STEP = 16
STEPS = QB // STEP
SLAB = STEP * HP
ALL = QB * HP
FEATS = 56
SHARE = 232

LOGIT_WEIGHT = math.sqrt(1.0 / 3.0)
MASKED_LOGIT = -100000.0
SCALE_QK = LOGIT_WEIGHT * C ** (-0.5)
POINT_SCALE = math.sqrt(2.0 / (9.0 * P_SIZE)) / 2.0
F32 = jnp.float32
BF16 = jnp.bfloat16
HIGHEST = lax.Precision.HIGHEST

NN = (((1,), (0,)), ((), ()))
NT = (((1,), (1,)), ((), ()))
TN = (((0,), (0,)), ((), ()))


def dot(a, b, dims=NN, precision=None):
    return lax.dot_general(a, b, dims, precision=precision, preferred_element_type=F32)


def two_part_dot(fixed, values, dims, values_first=False):
    high = values.astype(BF16)
    low = (values - high.astype(F32)).astype(BF16)
    if values_first:
        return dot(high, fixed, dims) + dot(low, fixed, dims)
    return dot(fixed, high, dims) + dot(fixed, low, dims)


def head_mask(count, group, size, offset=0, axis=1):
    shape = (HP, count) if axis == 1 else (count, HP)
    feature = lax.broadcasted_iota(jnp.int32, shape, axis)
    head = lax.broadcasted_iota(jnp.int32, shape, 1 - axis)
    return jnp.where(lax.div(lax.rem(feature, group), size) == head, 1.0, 0.0).astype(F32)


def query_mask():
    shape = (HP, QF)
    feature = lax.broadcasted_iota(jnp.int32, shape, 1)
    head = lax.broadcasted_iota(jnp.int32, shape, 0)
    of = jnp.where(
        feature < VEC,
        lax.div(feature, C),
        lax.div(lax.rem(jnp.maximum(feature - VEC, 0), H * P_SIZE), P_SIZE),
    )
    return jnp.where(of == head, 1.0, 0.0).astype(F32), feature < VEC


def spread(values, mask):
    rows, count = values.shape
    return (values.astype(F32)[:, None, :] * mask[None]).reshape(rows * HP, count)


def head_column(ref, scale, count):
    index = lax.broadcasted_iota(jnp.int32, (HP, count), 0)
    column = jnp.zeros((HP, count), F32)
    for h in range(H):
        column = jnp.where(index == h, ref[h] * scale, column)
    return column


def head_row(ref, scale, count):
    index = lax.broadcasted_iota(jnp.int32, (count, HP), 1)
    row = jnp.zeros((count, HP), F32)
    for h in range(H):
        row = jnp.where(index == h, ref[h] * scale, row)
    return row


def key_line(ref):
    begin = lax.axis_index("col") * 2
    return jnp.concatenate([ref[pl.ds(begin, 1), :], ref[pl.ds(begin + 1, 1), :]], axis=1)


def score_kernel(
    offsets,
    mask_s,
    chain_s,
    head_weight,
    chain_bias,
    mask_v,
    chain_v,
    query_single,
    key_single,
    query_weight,
    key_weight,
    pair_weight,
    pair,
    grad_single,
    grad_point,
    grad_pairs,
    exp_out,
    up_out,
    key_out,
    query_out,
    heads_out,
    stats_out,
    key_qk,
    key_v,
    key_norm,
    both,
    stat,
    spread_pairs,
):
    step = pl.program_id(0)

    @pl.when(step == 0)
    def _():
        feats = lax.dot_general(
            key_weight[...], key_single[...], (((0,), (1,)), ((), ())), preferred_element_type=F32
        ).astype(BF16)
        key_qk[0:VEC] = feats[0:VEC]
        key_qk[VEC:QF] = feats[2 * VEC : 2 * VEC + QPTS]
        key_v[0:VEC] = feats[VEC : 2 * VEC]
        key_v[VEC:] = feats[2 * VEC + QPTS :]
        key_out[...] = key_qk[...]
        points = feats[2 * VEC : 2 * VEC + QPTS].astype(F32)
        key_norm[...] = dot(
            head_mask(QPTS, H * P_SIZE, P_SIZE), points * points, NN, HIGHEST
        )
        unit = jnp.where(
            lax.broadcasted_iota(jnp.int32, (HP, H), 0)
            == lax.broadcasted_iota(jnp.int32, (HP, H), 1),
            1.0,
            0.0,
        ).astype(BF16)
        both[0:HP] = dot(unit, pair_weight[...], NT).astype(BF16)
        spread_pairs[...] = jnp.zeros_like(spread_pairs)
        stat[...] = jnp.zeros_like(stat)

    mask, is_vec = query_mask()
    query = dot(query_single[...], query_weight[...]).astype(BF16)
    query_out[...] = query
    rows = spread(query, mask)
    vec_rows = jnp.where(is_vec[0:1], rows, 0.0)
    point_rows = rows - vec_rows
    query_norm = jnp.sum(point_rows * point_rows, axis=1, keepdims=True)
    scalar = dot(vec_rows.astype(BF16), key_qk[...])
    cross = dot(point_rows.astype(BF16), key_qk[...])
    upstream = dot(spread(grad_single[...], head_mask(VEC, VEC, C)).astype(BF16), key_v[0:VEC])
    upstream += dot(
        spread(grad_point[...], head_mask(VPTS, H * PV, PV)).astype(BF16), key_v[VEC:]
    )
    pairs = grad_pairs[...].astype(F32)
    for h in range(H):
        spread_pairs[:, h, :] = pairs[:, DZ * h : DZ * (h + 1)]
    heads = spread_pairs[...].astype(BF16)
    heads_out[...] = heads

    point_coef = head_column(head_weight, POINT_SCALE, KB)
    bias = head_column(chain_bias, 1.0, KB)
    key_live = key_line(mask_v) == 1
    key_chain = key_line(chain_v)
    begin = offsets[lax.axis_index("row")] + step * STEP
    lane = lax.broadcasted_iota(jnp.int32, (HP, 128), 1)
    for i in range(STEP):
        at = slice(HP * i, HP * (i + 1))
        left = jnp.concatenate([both[0:HP], heads[i]], axis=0)
        tile = dot(left, pair[i], NT)
        distance = query_norm[at] + key_norm[...] - 2.0 * cross[at]
        logits = LOGIT_WEIGHT * (scalar[at] * C ** (-0.5) + tile[0:HP] - point_coef * distance)
        same = jnp.where(key_chain == chain_s[begin + i], 1.0, 0.0)
        logits = logits + bias * same
        live = jnp.where(key_live, mask_s[begin + i], 0) == 1
        logits = jnp.where(live, logits, MASKED_LOGIT)
        up = upstream[at] + tile[HP:]
        top = jnp.max(logits, axis=1, keepdims=True)
        terms = jnp.exp(logits - top)
        total = jnp.sum(terms, axis=1, keepdims=True)
        moment = jnp.sum(terms * up, axis=1, keepdims=True)
        exp_out[at] = terms
        up_out[at] = up
        stat[at] = jnp.where(lane == 0, top, jnp.where(lane == 1, total, moment))
    for half in range(2):
        turned = stat[128 * half : 128 * (half + 1)].T
        for k in range(3):
            stats_out[k, pl.ds(2 * step + half, 1), :] = turned[k : k + 1]


def grad_kernel(
    offsets,
    mask_s,
    head_weight,
    mask_v,
    parts,
    own,
    exp_terms,
    up,
    key_qk,
    query,
    query_single,
    query_weight,
    key_weight,
    grad_single,
    grad_point,
    weight_out,
    score_out,
    kept_out,
    given_out,
    single_out,
    key_grad,
    key_single_grad,
    query_weight_grad,
):
    row_top = parts[0, 0]
    for s in range(1, COLS):
        row_top = jnp.maximum(row_top, parts[s, 0])
    row_total = jnp.zeros_like(row_top)
    moment = jnp.zeros_like(row_top)
    for s in range(COLS):
        share = jnp.exp(parts[s, 0] - row_top)
        row_total += share * parts[s, 1]
        moment += share * parts[s, 2]
    factor = jnp.exp(own[0] - row_top) / row_total
    centre = moment / row_total
    columns = jnp.concatenate([factor, centre], axis=0).T
    key_live = jnp.where(key_line(mask_v) == 1, 1.0, 0.0)
    begin = offsets[lax.axis_index("row")]
    col_score = jnp.zeros((HP, KB), F32)
    row_score = []
    for i in range(QB):
        at = slice(HP * i, HP * (i + 1))
        chunk, off = i // 8, HP * (i % 8)
        fac = columns[off : off + HP, chunk : chunk + 1]
        mid = columns[off : off + HP, 8 + chunk : 9 + chunk]
        weights = exp_terms[at] * fac
        live = jnp.where(mask_s[begin + i] == 1, 1.0, 0.0)
        score = (weights * (up[at] - mid) * (key_live * live)).astype(BF16)
        weight_out[at] = weights.astype(BF16)
        score_out[at] = score
        score = score.astype(F32)
        col_score += score
        row_score.append(jnp.sum(score, axis=1, keepdims=True))
    row_score = jnp.concatenate(row_score, axis=0)

    mask, is_vec = query_mask()
    is_vec = is_vec[0:1]
    rows = spread(query[...], mask)
    scores = score_out[...]
    weights = weight_out[...]
    grad_coef = -2.0 * LOGIT_WEIGHT * POINT_SCALE
    key_points = head_mask(QPTS, H * P_SIZE, P_SIZE, axis=0)
    coef = jnp.sum(key_points * head_row(head_weight, grad_coef, QPTS), axis=1, keepdims=True)
    raw = dot(rows.astype(BF16), scores, TN)
    key_grad[0:VEC] = SCALE_QK * raw[0:VEC]
    key_grad[VEC : 2 * VEC] = dot(
        spread(grad_single[...], head_mask(VEC, VEC, C)).astype(BF16), weights, TN
    )
    key_grad[2 * VEC : 2 * VEC + QPTS] = coef * (
        key_qk[VEC:QF].astype(F32) * dot(key_points, col_score, NN, HIGHEST) - raw[VEC:QF]
    )
    key_grad[2 * VEC + QPTS : KF] = dot(
        spread(grad_point[...], head_mask(VPTS, H * PV, PV)).astype(BF16), weights, TN
    )
    key_grad[KF:] = jnp.zeros((ROWS * FEATS - KF, KB), F32)
    key_single_grad[...] = two_part_dot(key_weight[...], key_grad[0:KF], NN)
    raw = dot(scores, key_qk[...], NT)
    head_coef = head_column(head_weight, grad_coef, QF)
    head_coef = jnp.concatenate([head_coef] * QB, axis=0)
    masks = jnp.concatenate([mask] * QB, axis=0)
    raw = jnp.where(is_vec, SCALE_QK * raw, head_coef * (rows * row_score - raw)) * masks
    query_grad = jnp.sum(raw.reshape(QB, HP, QF), axis=1)
    single = two_part_dot(query_weight[...], query_grad, NT, values_first=True)
    for k in range(3):
        single_out[QB * k : QB * (k + 1)] = single[:, 128 * k : 128 * (k + 1)]
    query_weight_grad[0:QF] = two_part_dot(query_single[...], query_grad, TN, values_first=True)
    query_weight_grad[QF:] = jnp.zeros((ROWS * 24 - QF, DS), F32)
    core = lax.rem(lax.axis_index("row"), 2)
    for out, parity in ((kept_out, core), (given_out, 1 - core)):
        for q in range(ROWS // 2):
            r = 2 * q + parity
            at = pl.ds(pl.multiple_of(FEATS * r, 8), FEATS)
            for k in range(2):
                out[q, FEATS * k : FEATS * (k + 1)] = key_grad[at, 128 * k : 128 * (k + 1)]
            at = pl.ds(pl.multiple_of(24 * r, 8), 24)
            for k in range(2):
                out[q, 112 + 24 * k : 136 + 24 * k] = key_single_grad[
                    at, 128 * k : 128 * (k + 1)
                ]
            for k in range(3):
                out[q, 160 + 24 * k : 184 + 24 * k] = query_weight_grad[
                    at, 128 * k : 128 * (k + 1)
                ]


def pair_kernel(pair_weight, pair, weights, scores, heads, pair_out, bias_out, lanes):
    step = pl.program_id(0)

    @pl.when(step == 0)
    def _():
        unit = jnp.where(
            lax.broadcasted_iota(jnp.int32, (HP, H), 0)
            == lax.broadcasted_iota(jnp.int32, (HP, H), 1),
            1.0,
            0.0,
        ).astype(BF16)
        values = LOGIT_WEIGHT * dot(unit, pair_weight[...], NT)
        high = values.astype(BF16)
        lanes[0:HP] = high
        lanes[HP:] = (values - high.astype(F32)).astype(BF16)
        bias_out[...] = jnp.zeros_like(bias_out)

    total = jnp.zeros((HP, DZ), F32)
    for i in range(STEP):
        at = slice(HP * i, HP * (i + 1))
        score = scores[at]
        left = jnp.concatenate([weights[at], score, score], axis=0)
        right = jnp.concatenate([heads[i], lanes[...]], axis=0)
        pair_out[i] = dot(left, right, TN).astype(BF16)
        total += dot(score, pair[i])
    bias_out[...] += LOGIT_WEIGHT * total


def whole(shape):
    return pl.BlockSpec(shape, lambda s: (0,) * len(shape))


def rows_of(*shape):
    return pl.BlockSpec(shape, lambda s: (s,) + (0,) * (len(shape) - 1))


SCALARS = pl.BlockSpec(memory_space=pltpu.SMEM)
VECTORS = pl.BlockSpec(memory_space=pltpu.VMEM)
PARAMS = pltpu.CompilerParams(
    dimension_semantics=("arbitrary",), vmem_limit_bytes=48 * 1024 * 1024
)


def scores_of(
    offsets, mask, chain, head_weight, chain_bias, query_single, key_single, query_weight,
    key_weight, pair_weight, pair, grad_single, grad_point, grad_pairs,
):
    return pl.pallas_call(
        score_kernel,
        grid=(STEPS,),
        out_shape=(
            jax.ShapeDtypeStruct((ALL, KB), F32),
            jax.ShapeDtypeStruct((ALL, KB), F32),
            jax.ShapeDtypeStruct((QF, KB), BF16),
            jax.ShapeDtypeStruct((QB, QF), BF16),
            jax.ShapeDtypeStruct((QB, HP, DZ), BF16),
            jax.ShapeDtypeStruct((3, 8, 128), F32),
        ),
        in_specs=[SCALARS] * 5
        + [
            whole((32, 128)),
            whole((32, 128)),
            rows_of(STEP, DS),
            whole((KB, DS)),
            whole((DS, QF)),
            whole((DS, KF)),
            whole((DZ, H)),
            rows_of(STEP, KB, DZ),
            rows_of(STEP, VEC),
            rows_of(STEP, VPTS),
            rows_of(STEP, H * DZ),
        ],
        out_specs=(
            rows_of(SLAB, KB),
            rows_of(SLAB, KB),
            whole((QF, KB)),
            rows_of(STEP, QF),
            rows_of(STEP, HP, DZ),
            whole((3, 8, 128)),
        ),
        scratch_shapes=[
            pltpu.VMEM((QF, KB), BF16),
            pltpu.VMEM((VEC + VPTS, KB), BF16),
            pltpu.VMEM((HP, KB), F32),
            pltpu.VMEM((HP, DZ), BF16),
            pltpu.VMEM((SLAB, 128), F32),
            pltpu.VMEM((STEP, HP, DZ), F32),
        ],
        compiler_params=PARAMS,
        cost_estimate=pl.CostEstimate(
            flops=2_000_000_000, bytes_accessed=8_000_000, transcendentals=262144
        ),
        name="row_scores",
    )(
        offsets, mask, chain, head_weight, chain_bias, mask.reshape(32, 128),
        chain.reshape(32, 128), query_single, key_single, query_weight, key_weight,
        pair_weight, pair, grad_single, grad_point, grad_pairs,
    )


def grads_of(
    offsets, mask, head_weight, parts, own, exp_terms, up, key_qk, query, query_single,
    query_weight, key_weight, grad_single, grad_point,
):
    return pl.pallas_call(
        grad_kernel,
        out_shape=(
            jax.ShapeDtypeStruct((ALL, KB), BF16),
            jax.ShapeDtypeStruct((ALL, KB), BF16),
            jax.ShapeDtypeStruct((ROWS // 2, SHARE, 128), F32),
            jax.ShapeDtypeStruct((ROWS // 2, SHARE, 128), F32),
            jax.ShapeDtypeStruct((3 * QB, 128), F32),
        ),
        in_specs=[SCALARS] * 3 + [VECTORS] * 12,
        out_specs=(VECTORS,) * 5,
        scratch_shapes=[
            pltpu.VMEM((ROWS * FEATS, KB), F32),
            pltpu.VMEM((DS, KB), F32),
            pltpu.VMEM((ROWS * 24, DS), F32),
        ],
        compiler_params=pltpu.CompilerParams(vmem_limit_bytes=48 * 1024 * 1024),
        cost_estimate=pl.CostEstimate(
            flops=3_000_000_000, bytes_accessed=8_000_000, transcendentals=20000
        ),
        name="feature_grads",
    )(
        offsets, mask, head_weight, mask.reshape(32, 128), parts, own, exp_terms, up, key_qk,
        query, query_single, query_weight, key_weight, grad_single, grad_point,
    )


def pair_grads_of(pair_weight, pair, weights, scores, heads):
    return pl.pallas_call(
        pair_kernel,
        grid=(STEPS,),
        out_shape=(
            jax.ShapeDtypeStruct((QB, KB, DZ), BF16),
            jax.ShapeDtypeStruct((HP, DZ), F32),
        ),
        in_specs=[
            whole((DZ, H)),
            rows_of(STEP, KB, DZ),
            rows_of(SLAB, KB),
            rows_of(SLAB, KB),
            rows_of(STEP, HP, DZ),
        ],
        out_specs=(rows_of(STEP, KB, DZ), whole((HP, DZ))),
        scratch_shapes=[pltpu.VMEM((2 * HP, DZ), BF16)],
        compiler_params=PARAMS,
        cost_estimate=pl.CostEstimate(
            flops=2_000_000_000, bytes_accessed=10_000_000, transcendentals=0
        ),
        name="pair_grads",
    )(pair_weight, pair, weights, scores, heads)


CHIPS = [[2 * i + core for i in range(ROWS // 2)] for core in range(2)]


def other_core(values):
    return lax.ppermute(values, "row", [(i, i ^ 1) for i in range(ROWS)])


def exchange(values, axis, groups=None):
    return lax.all_to_all(values, axis, 0, 0, axis_index_groups=groups)


def gather(values, axis, parts, groups=None):
    return exchange(jnp.broadcast_to(values[None], (parts, *values.shape)), axis, groups)


def gather_row(values):
    own = gather(values, "row", ROWS // 2, CHIPS)
    other = other_core(own)
    first = lax.axis_index("row") % 2 == 0
    return jnp.where(first, own, other), jnp.where(first, other, own)


def scatter_row(kept, given):
    return jnp.sum(exchange(kept + other_core(given), "row", CHIPS), axis=0)


def sum_col(values):
    share = jnp.sum(exchange(values.reshape(COLS, -1, values.shape[1]), "col"), axis=0)
    return gather(share, "col", COLS).reshape(values.shape)


def lanes_of(values):
    return [values[..., 128 * k : 128 * (k + 1)] for k in range(values.shape[-1] // 128)]


def joined(values, rows):
    return jnp.concatenate(
        [values[..., k : k + rows, :] for k in range(0, values.shape[-2], rows)], axis=-1
    )


def local(
    query_single,
    key_single,
    query_weight,
    key_weight,
    pair_weight,
    head_weight,
    chain_bias,
    pair,
    residue_mask,
    chain_index,
    strip_offsets,
    grad_single_out,
    grad_point_out,
    grad_pair_out,
):
    terms, up, key_qk, query, heads, own = scores_of(
        strip_offsets, residue_mask, chain_index, head_weight, chain_bias, query_single,
        key_single, query_weight, key_weight, pair_weight, pair, grad_single_out,
        grad_point_out, grad_pair_out,
    )
    with jax.named_scope("row_statistics"):
        parts = gather(own, "col", COLS)
    weights, scores, kept, given, query_single_part = grads_of(
        strip_offsets, residue_mask, head_weight, parts, own, terms, up, key_qk, query,
        query_single, query_weight, key_weight, grad_single_out, grad_point_out,
    )
    with jax.named_scope("row_sum"):
        summed = scatter_row(kept, given)
    grad_pair, bias_part = pair_grads_of(pair_weight, pair, weights, scores, heads)
    key_grad = joined(summed[: 2 * FEATS], FEATS)
    key_share = jnp.dot(key_grad, key_single.astype(F32), precision=HIGHEST)
    with jax.named_scope("col_sum"):
        share = jnp.concatenate(
            lanes_of(key_share)
            + [bias_part, summed[160:232], query_single_part]
            + [jnp.zeros((64, 128), F32)],
            axis=0,
        )
        share = sum_col(share)
    grad_query_single = joined(share[256:448], 64)
    with jax.named_scope("row_gather"):
        even, odd = gather_row(jnp.concatenate([share[:256], summed[112:160]], axis=0))
        full = jnp.stack([even, odd], axis=1).reshape(ROWS, 304, 128)
        grad_key_weight = joined(full[:, :168], FEATS).reshape(ROWS * FEATS, -1)[:KF].T
        grad_pair_weight = jnp.sum(full[:, 168 : 168 + H], axis=0).T
        grad_query_weight = joined(full[:, 184:256], 24).reshape(ROWS * 24, -1)[:QF].T
        grad_key_single = joined(full[:, 256:], 24).reshape(ROWS * 24, -1).T
    return (
        grad_query_single,
        grad_key_single,
        grad_query_weight,
        grad_key_weight,
        grad_pair_weight,
        grad_pair,
    )


def solution(mesh):
    in_specs = (
        P("row", None),
        P("col", None),
        P(),
        P(),
        P(),
        P(),
        P(),
        P("row", "col", None),
        P(),
        P(),
        P(),
        P("row", None),
        P("row", None),
        P("row", None),
    )
    out_specs = (P("row", None), P("col", None), P(), P(), P(), P("row", "col", None))
    return jax.shard_map(local, mesh=mesh, in_specs=in_specs, out_specs=out_specs, check_vma=False)
```

time: 591 us -> 126 us (0.21)
  waiting for transfers between devices: 337 us -> 22.7 us
  blocking collectives: 188 us -> 57.9 us
  matrix products: 34.3 us -> 0.23 us
  Pallas kernels: 0 us -> 16.9 us
  between operations: 16.1 us -> 0.99 us
  starting transfers between devices: 0.12 us -> 13.6 us
    psum x3 -> x0, waiting for transfers between devices: 337 us -> none  [the longest x1 162 us: local(): query_grad = lax.psum(query_part, 'col')]
    psum x2 -> x0, blocking collectives: 146 us -> none  [the longest x1 82.8 us: local(): grad_pair_weight = lax.psum(bias_part, ('row', 'col'))]
    all_to_all x0 -> x3, blocking collectives: none -> 57.9 us  [exchange(): return lax.all_to_all(values, axis, 0, 0, axis_index_groups=groups)]
    pmax x1 -> x0, blocking collectives: 41.9 us -> none  [local(): row_top = lax.pmax(jnp.max(logits, axis=2), 'col')]
    dot_general x21 -> x1, matrix products: 34.3 us -> 0.23 us  [local(): key_share = jnp.dot(key_grad, key_single.astype(F32), precision=HIGHEST)]
    all_to_all x0 -> x2, waiting for transfers between devices: none -> 18.7 us  [exchange(): return lax.all_to_all(values, axis, 0, 0, axis_index_groups=groups)]
    pallas_call x0 -> x3, Pallas kernels: none -> 16.9 us  [the longest x1 6.68 us: grads_of(): pl.pallas_call(grad_kernel, out_shape=(jax.ShapeDtypeStruct((ALL, KB), BF...]
    all_to_all x0 -> x2, starting transfers between devices: none -> 8.29 us  [exchange(): return lax.all_to_all(values, axis, 0, 0, axis_index_groups=groups)]
  transfers between devices with their start and end apart: 3 -> 4, of which waited for: 3 -> 4; matrix products, arithmetic and copies ran while one was open for 2% -> 1% of each run, Pallas kernels for 0% -> 3%
where the time goes in v2:
time: 126 us
  blocking collectives  57.9 us (46%)
  waiting for transfers between devices  22.7 us (18%)
  Pallas kernels  16.9 us (13%)
  starting transfers between devices  13.6 us (11%)
  local copies, waits for them, and re-layouts  9.78 us (8%)
  other arithmetic  3.66 us (3%)
    all_to_all x3, blocking collectives, exchange(): return lax.all_to_all(values, axis, 0, 0, axis_index_groups=groups)  57.9 us
    all_to_all x2, waiting for transfers between devices, exchange(): return lax.all_to_all(values, axis, 0, 0, axis_index_groups=groups)  18.7 us
    all_to_all x2, starting transfers between devices, exchange(): return lax.all_to_all(values, axis, 0, 0, axis_index_groups=groups)  8.29 us
    unnamed x34, local copies, waits for them, and re-layouts  7.65 us
    pallas_call x1, Pallas kernels, grads_of(): pl.pallas_call(grad_kernel, out_shape=(jax.ShapeDtypeStruct((ALL, KB), BF...  6.68 us
    pallas_call x1, Pallas kernels, scores_of(): pl.pallas_call(score_kernel, grid=(STEPS,), out_shape=(jax.ShapeDtypeStru...  6.39 us
    ppermute x2, starting transfers between devices, other_core(): return lax.ppermute(values, 'row', [(i, i ^ 1) for i in range(ROWS)])  5.35 us
    ppermute x2, waiting for transfers between devices, other_core(): return lax.ppermute(values, 'row', [(i, i ^ 1) for i in range(ROWS)])  4.06 us
  transfers between devices with their start and end apart: 4, of which 4 were waited for; matrix products, arithmetic and copies ran while one was open for 1% of the time, Pallas kernels for 3%

profile of v2, /device:TPU:1, one launch (start us, length us, event | category | flops | bytes accessed | tf_op | source)
XLA Modules:
  0.0 125.7 jit_solution(4144051618446281118)
XLA Ops:
  0.6 0.0 copy-start.7
  0.6 0.0 copy-start.4
  0.7 0.0 copy-start.5
  0.7 0.0 copy-start.9
  0.7 0.0 copy-start.10
  0.7 0.0 copy-start
  0.7 0.0 copy-start.3
  0.7 0.0 copy-start.6
  0.7 0.0 copy-start.2
  0.7 0.0 copy-start.8
  0.7 0.9 copy.30.pair_weight
  1.7 1.2 copy.28.query_weight
  2.8 1.4 %copy.29.key_weight = bf16[384,816]{1,0:T(8,128)(2,1)S(1)} copy(bf16[384,816]{0,1:T(8,128)(2,1)} %param.17) | data formatting | bytes 1253376 | tf_op args[3]
  4.2 0.0 copy-done.7
  4.3 0.0 copy-done.4
  4.3 0.0 copy-done.5
  4.3 0.0 copy-done.9
  4.3 0.0 copy-done.10
  4.3 0.0 copy-done
  4.3 0.0 copy-done.3
  4.3 0.0 copy-done.6
  4.3 0.0 copy-done.2
  4.3 0.0 copy-done.8
  4.3 6.4 %row_scores.1 = (f32[1024,256]{1,0:T(8,128)S(1)}, f32[1024,256]{1,0:T(8,128)S(1)}, bf16[336,256]{1,0:T(8,128)(2,1)S(1)}, bf16[64,336]{1,0:T(8,128)(2,1)S(1)}, bf...) custom-call(s32[16]{0:T(128)S(1)} %copy-done.9, s32[4096]{0:T(1024)S(1)} %copy-done.7, s32[4096]{0:T(1024)S(1)} %copy-done.6, ...), custom_call_target="tpu_custom_call" | custom-call | flops 2000000000 | bytes 8000000 | tf_op jit(solution)/shard_map/row_scores/pallas_call | solution.py:361
  10.7 0.0 copy-start.11
  10.8 1.0 copy-done.11
  11.7 22.3 %all_to_all.25.parts = f32[16,3,8,128]{3,2,1,0:T(8,128)S(1)} all-to-all(f32[16,3,8,128]{3,2,1,0:T(8,128)S(1)} %broadcast_in_dim.8), channel_id=1, replica_groups=mesh['row'=16,'col'=16] {'col'}, dimensions={0} | all-to-all | bytes 393216 | tf_op jit(solution)/shard_map/row_statistics/all_to_all | solution.py:478
  34.1 6.7 %feature_grads.1 = (bf16[1024,256]{1,0:T(8,128)(2,1)S(1)}, bf16[1024,256]{1,0:T(8,128)(2,1)S(1)}, f32[8,232,128]{2,1,0:T(8,128)S(1)}, f32[8,232,128]{2,1,0:T(8,128)S(1)}, f32[192,128]{1,0:T(8,128)S(1)}) custom-call(s32[16]{0:T(128)S(1)} %copy-done.9, s32[4096]{0:T(1024)S(1)} %copy-done.7, f32[12]{0:T(128)S(1)} %copy-done.10, s32[32,128]{1,0:T(8,128)S(1)} %bitcast.27, ...), custom_call_target="tpu_custom_call" | custom-call | flops 3000000000 | bytes 8000000 | tf_op jit(solution)/shard_map/feature_grads/pallas_call | solution.py:418
  40.8 2.0 %collective-permute-start = (f32[8,232,128]{2,1,0:T(8,128)S(1)}, f32[8,232,128]{2,1,0:T(8,128)S(1)}, u32[]{:S(2)}, u32[]{:S(2)}) collective-permute-start(f32[8,232,128]{2,1,0:T(8,128)S(1)} %get-tuple-element.25), channel_id=1, source_target_pairs={{0,16},{16,0},{32,48},{48,32},{64,80},{80,64},{96,112},{112,96},{1... | collective-permute-start | bytes 2850824 | tf_op jit(solution)/shard_map/row_sum/ppermute | solution.py:474
  42.7 2.1 %collective-permute-done = f32[8,232,128]{2,1,0:T(8,128)S(1)} collective-permute-done((f32[8,232,128]{2,1,0:T(8,128)S(1)}, f32[8,232,128]{2,1,0:T(8,128)S(1)}, u32[]{:S(2)}, u32[]{:S(2)}) %collective-permute-start) | collective-permute-done | bytes 950304 | tf_op jit(solution)/shard_map/row_sum/ppermute | solution.py:474
  44.9 1.0 add.7
  45.9 4.8 %all-to-all-start.1 = ((f32[8,232,128]{2,1,0:T(8,128)}), f32[8,232,128]{2,1,0:T(8,128)S(1)}, u32[]{:S(2)}, u32[]{:S(2)}) async-start(f32[8,232,128]{2,1,0:T(8,128)} %add.7), calls=%async_computation.1 | async-start | bytes 1900544 | tf_op jit(solution)/shard_map/row_sum/all_to_all | solution.py:478
  50.7 0.0 copy-start.1
  50.7 2.2 %copy-done.1 = bf16[64,256,128]{2,1,0:T(8,128)(2,1)S(1)} copy-done((bf16[64,256,128]{2,1,0:T(8,128)(2,1)S(1)}, bf16[64,256,128]{2,1,0:T(8,128)(2,1)}, u32[]{:S(2)}) %copy-start.1) | copy-done | bytes 4194328
  52.9 3.8 %pair_grads.1 = (bf16[64,256,128]{2,1,0:T(8,128)(2,1)}, f32[16,128]{1,0:T(8,128)S(1)}) custom-call(bf16[128,12]{1,0:T(8,128)(2,1)S(1)} %copy.30.pair_weight, bf16[64,256,128]{2,1,0:T(8,128)(2,1)S(1)} %copy-done.1, bf16[1024,256]{1,0:T(8,128)(2,1)S(1)} %get-tuple-element.26.weights, bf16[1024,256]{1,0:T(8,128)(2,1)S(1)} %get-tuple-element.27.scores, ...), custom_call_target="tpu_custom_call" | custom-call | flops 2000000000 | bytes 10000000 | tf_op jit(solution)/shard_map/pair_grads/pallas_call | solution.py:446
  56.6 8.1 %all-to-all-done.1 = f32[8,232,128]{2,1,0:T(8,128)S(1)} async-done(((f32[8,232,128]{2,1,0:T(8,128)}), f32[8,232,128]{2,1,0:T(8,128)S(1)}, u32[]{:S(2)}, u32[]{:S(2)}) %all-to-all-start.1) | async-done | bytes 950304 | tf_op jit(solution)/shard_map/row_sum/all_to_all | solution.py:478
  64.9 0.2 fusion
  65.2 14.4 %all_to_all.26 = f32[16,32,128]{2,1,0:T(8,128)S(1)} all-to-all(f32[16,32,128]{2,1,0:T(8,128)S(1)} %bitcast.35), channel_id=1, replica_groups=mesh['row'=16,'col'=16] {'col'}, dimensions={0} | all-to-all | bytes 524288 | tf_op jit(solution)/shard_map/col_sum/all_to_all | solution.py:478
  79.6 0.7 broadcast_in_dim.10
  80.4 3.5 %all-to-all-start.3 = ((f32[16,32,128]{2,1,0:T(8,128)}), f32[16,32,128]{2,1,0:T(8,128)S(1)}, u32[]{:S(2)}, u32[]{:S(2)}) async-start(f32[16,32,128]{2,1,0:T(8,128)} %broadcast_in_dim.10), calls=%async_computation.3 | async-start | bytes 524288 | tf_op jit(solution)/shard_map/col_sum/all_to_all | solution.py:478
  83.9 10.5 %all-to-all-done.3 = f32[16,32,128]{2,1,0:T(8,128)S(1)} async-done(((f32[16,32,128]{2,1,0:T(8,128)}), f32[16,32,128]{2,1,0:T(8,128)S(1)}, u32[]{:S(2)}, u32[]{:S(2)}) %all-to-all-start.3) | async-done | bytes 262176 | tf_op jit(solution)/shard_map/col_sum/all_to_all | solution.py:478
  94.5 0.1 broadcast_in_dim.11
  94.6 21.1 %all_to_all.27 = f32[8,304,128]{2,1,0:T(8,128)S(1)} all-to-all(f32[8,304,128]{2,1,0:T(8,128)S(1)} %broadcast_in_dim.11), channel_id=1, replica_groups={{0,32,64,96,128,160,192,224},{16,48,80,112,144,176,208,240},{1,33,65,97..., dimensions={0} | all-to-all | bytes 2490368 | tf_op jit(solution)/shard_map/row_gather/all_to_all | solution.py:478
  115.7 3.4 %collective-permute-start.1 = (f32[8,304,128]{2,1,0:T(8,128)S(1)}, f32[8,304,128]{2,1,0:T(8,128)S(1)}, u32[]{:S(2)}, u32[]{:S(2)}) collective-permute-start(f32[8,304,128]{2,1,0:T(8,128)S(1)} %all_to_all.27), channel_id=1, source_target_pairs={{0,16},{16,0},{32,48},{48,32},{64,80},{80,64},{96,112},{112,96},{1... | collective-permute-start | bytes 3735560 | tf_op jit(solution)/shard_map/row_gather/ppermute | solution.py:474
  119.1 0.6 pad_maximum_fusion.6
  119.7 1.9 %collective-permute-done.1 = f32[8,304,128]{2,1,0:T(8,128)S(1)} collective-permute-done((f32[8,304,128]{2,1,0:T(8,128)S(1)}, f32[8,304,128]{2,1,0:T(8,128)S(1)}, u32[]{:S(2)}, u32[]{:S(2)}) %collective-permute-start.1) | collective-permute-done | bytes 1245216 | tf_op jit(solution)/shard_map/row_gather/ppermute | solution.py:474
  121.6 0.2 select_bitcast_fusion.1
  121.8 0.2 pad_maximum_fusion
  122.0 0.6 slice_reduce_fusion
  122.6 0.1 fusion.6
  122.6 0.1 fusion.5
  122.7 0.1 pad_maximum_fusion.1
  122.8 1.1 slice_bitcast_fusion
  124.0 0.9 copy.35
  124.9 0.8 pad_maximum_fusion.2
  (16 shorter events, 0.2 us)
Async XLA Ops:
  0.6 3.6 %copy-start.7 = (s32[4096]{0:T(1024)S(1)}, s32[4096]{0:T(1024)}, u32[]{:S(2)}) copy-start(s32[4096]{0:T(1024)} %mask_s.3) | copy-start | bytes 49156
  0.6 3.6 %copy-start.4 = (bf16[64,288]{1,0:T(8,128)(2,1)S(1)}, bf16[64,288]{1,0:T(8,128)(2,1)}, u32[]{:S(2)}) copy-start(bf16[64,288]{1,0:T(8,128)(2,1)} %grad_point.3) | copy-start | bytes 110596
  0.7 3.6 %copy-start.5 = (bf16[64,192]{1,0:T(8,128)(2,1)S(1)}, bf16[64,192]{1,0:T(8,128)(2,1)}, u32[]{:S(2)}) copy-start(bf16[64,192]{1,0:T(8,128)(2,1)} %grad_single.3) | copy-start | bytes 73732
  0.7 3.6 %copy-start.9 = (s32[16]{0:T(128)S(1)}, s32[16]{0:T(128)}, u32[]{:S(2)}) copy-start(s32[16]{0:T(128)} %offsets.3) | copy-start | bytes 196
  0.7 3.6 %copy-start.10 = (f32[12]{0:T(128)S(1)}, f32[12]{0:T(128)}, u32[]{:S(2)}) copy-start(f32[12]{0:T(128)} %head_weight.3) | copy-start | bytes 148
  0.7 3.6 %copy-start = (bf16[256,384]{1,0:T(8,128)(2,1)S(1)}, bf16[256,384]{1,0:T(8,128)(2,1)}, u32[]{:S(2)}) copy-start(bf16[256,384]{1,0:T(8,128)(2,1)} %key_single.1) | copy-start | bytes 589828
  0.7 3.6 %copy-start.3 = (bf16[64,384]{1,0:T(8,128)(2,1)S(1)}, bf16[64,384]{1,0:T(8,128)(2,1)}, u32[]{:S(2)}) copy-start(bf16[64,384]{1,0:T(8,128)(2,1)} %query_single.3) | copy-start | bytes 147460
  0.7 3.6 %copy-start.6 = (s32[4096]{0:T(1024)S(1)}, s32[4096]{0:T(1024)}, u32[]{:S(2)}) copy-start(s32[4096]{0:T(1024)} %chain_s.1) | copy-start | bytes 49156
  0.7 3.6 %copy-start.2 = (bf16[64,1536]{1,0:T(8,128)(2,1)S(1)}, bf16[64,1536]{1,0:T(8,128)(2,1)}, u32[]{:S(2)}) copy-start(bf16[64,1536]{1,0:T(8,128)(2,1)} %grad_pairs.1) | copy-start | bytes 589828
  0.7 3.6 %copy-start.8 = (f32[12]{0:T(128)S(1)}, f32[12]{0:T(128)}, u32[]{:S(2)}) copy-start(f32[12]{0:T(128)} %chain_bias.1) | copy-start | bytes 148
  10.7 1.0 copy-start.11
  40.8 4.1 %collective-permute-start = (f32[8,232,128]{2,1,0:T(8,128)S(1)}, f32[8,232,128]{2,1,0:T(8,128)S(1)}, u32[]{:S(2)}, u32[]{:S(2)}) collective-permute-start(f32[8,232,128]{2,1,0:T(8,128)S(1)} %get-tuple-element.25), channel_id=1, source_target_pairs={{0,16},{16,0},{32,48},{48,32},{64,80},{80,64},{96,112},{112,96},{1... | collective-permute-start | bytes 2850824 | tf_op jit(solution)/shard_map/row_sum/ppermute | solution.py:474
  45.9 18.9 %all-to-all-start.1 = ((f32[8,232,128]{2,1,0:T(8,128)}), f32[8,232,128]{2,1,0:T(8,128)S(1)}, u32[]{:S(2)}, u32[]{:S(2)}) async-start(f32[8,232,128]{2,1,0:T(8,128)} %add.7), calls=%async_computation.1 | async-start | bytes 1900544 | tf_op jit(solution)/shard_map/row_sum/all_to_all | solution.py:478
  50.7 2.2 %copy-start.1 = (bf16[64,256,128]{2,1,0:T(8,128)(2,1)S(1)}, bf16[64,256,128]{2,1,0:T(8,128)(2,1)}, u32[]{:S(2)}) copy-start(bf16[64,256,128]{2,1,0:T(8,128)(2,1)} %pair.3) | copy-start | bytes 12582916
  80.4 14.1 %all-to-all-start.3 = ((f32[16,32,128]{2,1,0:T(8,128)}), f32[16,32,128]{2,1,0:T(8,128)S(1)}, u32[]{:S(2)}, u32[]{:S(2)}) async-start(f32[16,32,128]{2,1,0:T(8,128)} %broadcast_in_dim.10), calls=%async_computation.3 | async-start | bytes 524288 | tf_op jit(solution)/shard_map/col_sum/all_to_all | solution.py:478
  115.7 6.0 %collective-permute-start.1 = (f32[8,304,128]{2,1,0:T(8,128)S(1)}, f32[8,304,128]{2,1,0:T(8,128)S(1)}, u32[]{:S(2)}, u32[]{:S(2)}) collective-permute-start(f32[8,304,128]{2,1,0:T(8,128)S(1)} %all_to_all.27), channel_id=1, source_target_pairs={{0,16},{16,0},{32,48},{48,32},{64,80},{80,64},{96,112},{112,96},{1... | collective-permute-start | bytes 3735560 | tf_op jit(solution)/shard_map/row_gather/ppermute | solution.py:474

commit v3 on v2

--- a/solution.py
+++ b/solution.py
@@ -134,9 +134,7 @@
 
     @pl.when(step == 0)
     def _():
-        feats = lax.dot_general(
-            key_weight[...], key_single[...], (((0,), (1,)), ((), ())), preferred_element_type=F32
-        ).astype(BF16)
+        feats = dot(key_weight[...], key_single[...], NT).astype(BF16)
         key_qk[0:VEC] = feats[0:VEC]
         key_qk[VEC:QF] = feats[2 * VEC : 2 * VEC + QPTS]
         key_v[0:VEC] = feats[VEC : 2 * VEC]
@@ -152,12 +150,12 @@
             1.0,
             0.0,
         ).astype(BF16)
-        both[0:HP] = dot(unit, pair_weight[...], NT).astype(BF16)
+        both[0:HP] = dot(unit, pair_weight[...]).astype(BF16)
         spread_pairs[...] = jnp.zeros_like(spread_pairs)
         stat[...] = jnp.zeros_like(stat)
 
     mask, is_vec = query_mask()
-    query = dot(query_single[...], query_weight[...]).astype(BF16)
+    query = dot(query_single[...], query_weight[...], NT).astype(BF16)
     query_out[...] = query
     rows = spread(query, mask)
     vec_rows = jnp.where(is_vec[0:1], rows, 0.0)
@@ -281,14 +279,14 @@
         spread(grad_point[...], head_mask(VPTS, H * PV, PV)).astype(BF16), weights, TN
     )
     key_grad[KF:] = jnp.zeros((ROWS * FEATS - KF, KB), F32)
-    key_single_grad[...] = two_part_dot(key_weight[...], key_grad[0:KF], NN)
+    key_single_grad[...] = two_part_dot(key_weight[...], key_grad[0:KF], TN, values_first=True)
     raw = dot(scores, key_qk[...], NT)
     head_coef = head_column(head_weight, grad_coef, QF)
     head_coef = jnp.concatenate([head_coef] * QB, axis=0)
     masks = jnp.concatenate([mask] * QB, axis=0)
     raw = jnp.where(is_vec, SCALE_QK * raw, head_coef * (rows * row_score - raw)) * masks
     query_grad = jnp.sum(raw.reshape(QB, HP, QF), axis=1)
-    single = two_part_dot(query_weight[...], query_grad, NT, values_first=True)
+    single = two_part_dot(query_weight[...], query_grad, NN, values_first=True)
     for k in range(3):
         single_out[QB * k : QB * (k + 1)] = single[:, 128 * k : 128 * (k + 1)]
     query_weight_grad[0:QF] = two_part_dot(query_single[...], query_grad, TN, values_first=True)
@@ -300,11 +298,12 @@
             at = pl.ds(pl.multiple_of(FEATS * r, 8), FEATS)
             for k in range(2):
                 out[q, FEATS * k : FEATS * (k + 1)] = key_grad[at, 128 * k : 128 * (k + 1)]
-            at = pl.ds(pl.multiple_of(24 * r, 8), 24)
-            for k in range(2):
-                out[q, 112 + 24 * k : 136 + 24 * k] = key_single_grad[
+            at = pl.ds(pl.multiple_of(16 * r, 8), 16)
+            for k in range(3):
+                out[q, 112 + 16 * k : 128 + 16 * k] = key_single_grad[
                     at, 128 * k : 128 * (k + 1)
                 ]
+            at = pl.ds(pl.multiple_of(24 * r, 8), 24)
             for k in range(3):
                 out[q, 160 + 24 * k : 184 + 24 * k] = query_weight_grad[
                     at, 128 * k : 128 * (k + 1)
@@ -322,7 +321,7 @@
             1.0,
             0.0,
         ).astype(BF16)
-        values = LOGIT_WEIGHT * dot(unit, pair_weight[...], NT)
+        values = LOGIT_WEIGHT * dot(unit, pair_weight[...])
         high = values.astype(BF16)
         lanes[0:HP] = high
         lanes[HP:] = (values - high.astype(F32)).astype(BF16)
@@ -339,6 +338,53 @@
     bias_out[...] += LOGIT_WEIGHT * total
 
 
+def assemble_kernel(own, other, share, key_out, query_out, single_out, query_single_out, pair_out):
+    first = lax.rem(lax.axis_index("row"), 2) == 0
+    lane = pl.program_id(0)
+
+    def chunk(r, begin, count):
+        at = pl.ds(pl.multiple_of(begin, 8), count)
+        mine, theirs = own[r // 2, at], other[r // 2, at]
+        if r % 2 == 1:
+            mine, theirs = theirs, mine
+        return jnp.where(first, mine, theirs)
+
+    for r in range(ROWS):
+        count = min(FEATS, KF - FEATS * r)
+        if count > 0:
+            key_out[FEATS * r : FEATS * r + count] = chunk(r, FEATS * lane, count)
+        if r < QF // 24:
+            query_out[24 * r : 24 * (r + 1)] = chunk(r, 184 + 24 * lane, 24)
+        single_out[16 * r : 16 * (r + 1)] = chunk(r, 256 + 16 * lane, 16)
+    query_single_out[...] = share[pl.ds(pl.multiple_of(256 + QB * lane, 8), QB)]
+
+    @pl.when(lane == 0)
+    def _():
+        total = chunk(0, 168, 16)
+        for r in range(1, ROWS):
+            total += chunk(r, 168, 16)
+        pair_out[...] = total[0:H]
+
+
+def assembled(own, other, share):
+    lanes = lambda rows: pl.BlockSpec((rows, 128), lambda k: (0, k))
+    return pl.pallas_call(
+        assemble_kernel,
+        grid=(3,),
+        out_shape=(
+            jax.ShapeDtypeStruct((KF, DS), F32),
+            jax.ShapeDtypeStruct((QF, DS), F32),
+            jax.ShapeDtypeStruct((KB, DS), F32),
+            jax.ShapeDtypeStruct((QB, DS), F32),
+            jax.ShapeDtypeStruct((H, DZ), F32),
+        ),
+        in_specs=[VECTORS] * 3,
+        out_specs=(lanes(KF), lanes(QF), lanes(KB), lanes(QB), whole((H, DZ))),
+        compiler_params=PARAMS,
+        name="assemble",
+    )(own, other, share)
+
+
 def whole(shape):
     return pl.BlockSpec(shape, lambda s: (0,) * len(shape))
 
@@ -349,9 +395,8 @@
 
 SCALARS = pl.BlockSpec(memory_space=pltpu.SMEM)
 VECTORS = pl.BlockSpec(memory_space=pltpu.VMEM)
-PARAMS = pltpu.CompilerParams(
-    dimension_semantics=("arbitrary",), vmem_limit_bytes=48 * 1024 * 1024
-)
+MIB = 1024 * 1024
+PARAMS = pltpu.CompilerParams(dimension_semantics=("arbitrary",), vmem_limit_bytes=48 * MIB)
 
 
 def scores_of(
@@ -375,9 +420,9 @@
             whole((32, 128)),
             rows_of(STEP, DS),
             whole((KB, DS)),
-            whole((DS, QF)),
-            whole((DS, KF)),
-            whole((DZ, H)),
+            whole((QF, DS)),
+            whole((KF, DS)),
+            whole((H, DZ)),
             rows_of(STEP, KB, DZ),
             rows_of(STEP, VEC),
             rows_of(STEP, VPTS),
@@ -428,10 +473,10 @@
         out_specs=(VECTORS,) * 5,
         scratch_shapes=[
             pltpu.VMEM((ROWS * FEATS, KB), F32),
-            pltpu.VMEM((DS, KB), F32),
+            pltpu.VMEM((KB, DS), F32),
             pltpu.VMEM((ROWS * 24, DS), F32),
         ],
-        compiler_params=pltpu.CompilerParams(vmem_limit_bytes=48 * 1024 * 1024),
+        compiler_params=pltpu.CompilerParams(vmem_limit_bytes=24 * MIB),
         cost_estimate=pl.CostEstimate(
             flops=3_000_000_000, bytes_accessed=8_000_000, transcendentals=20000
         ),
@@ -451,7 +496,7 @@
             jax.ShapeDtypeStruct((HP, DZ), F32),
         ),
         in_specs=[
-            whole((DZ, H)),
+            whole((H, DZ)),
             rows_of(STEP, KB, DZ),
             rows_of(SLAB, KB),
             rows_of(SLAB, KB),
@@ -470,6 +515,10 @@
 CHIPS = [[2 * i + core for i in range(ROWS // 2)] for core in range(2)]
 
 
+ALONG_X = [[4 * x + z for x in range(4)] for z in range(4)]
+ALONG_Z = [[4 * x + z for z in range(4)] for x in range(4)]
+
+
 def other_core(values):
     return lax.ppermute(values, "row", [(i, i ^ 1) for i in range(ROWS)])
 
@@ -482,20 +531,15 @@
     return exchange(jnp.broadcast_to(values[None], (parts, *values.shape)), axis, groups)
 
 
-def gather_row(values):
-    own = gather(values, "row", ROWS // 2, CHIPS)
-    other = other_core(own)
-    first = lax.axis_index("row") % 2 == 0
-    return jnp.where(first, own, other), jnp.where(first, other, own)
-
-
 def scatter_row(kept, given):
     return jnp.sum(exchange(kept + other_core(given), "row", CHIPS), axis=0)
 
 
 def sum_col(values):
-    share = jnp.sum(exchange(values.reshape(COLS, -1, values.shape[1]), "col"), axis=0)
-    return gather(share, "col", COLS).reshape(values.shape)
+    share = exchange(values.reshape(4, -1, values.shape[1]), "col", ALONG_X)
+    share = jnp.sum(share, axis=0)
+    share = jnp.sum(gather(share, "col", 4, ALONG_Z), axis=0)
+    return gather(share, "col", 4, ALONG_X).reshape(values.shape)
 
 
 def lanes_of(values):
@@ -524,6 +568,7 @@
     grad_point_out,
     grad_pair_out,
 ):
+    query_weight, key_weight, pair_weight = query_weight.T, key_weight.T, pair_weight.T
     terms, up, key_qk, query, heads, own = scores_of(
         strip_offsets, residue_mask, chain_index, head_weight, chain_bias, query_single,
         key_single, query_weight, key_weight, pair_weight, pair, grad_single_out,
@@ -542,26 +587,20 @@
     key_share = jnp.dot(key_grad, key_single.astype(F32), precision=HIGHEST)
     with jax.named_scope("col_sum"):
         share = jnp.concatenate(
-            lanes_of(key_share)
-            + [bias_part, summed[160:232], query_single_part]
-            + [jnp.zeros((64, 128), F32)],
-            axis=0,
+            lanes_of(key_share) + [bias_part, summed[160:232], query_single_part], axis=0
         )
         share = sum_col(share)
-    grad_query_single = joined(share[256:448], 64)
     with jax.named_scope("row_gather"):
-        even, odd = gather_row(jnp.concatenate([share[:256], summed[112:160]], axis=0))
-        full = jnp.stack([even, odd], axis=1).reshape(ROWS, 304, 128)
-        grad_key_weight = joined(full[:, :168], FEATS).reshape(ROWS * FEATS, -1)[:KF].T
-        grad_pair_weight = jnp.sum(full[:, 168 : 168 + H], axis=0).T
-        grad_query_weight = joined(full[:, 184:256], 24).reshape(ROWS * 24, -1)[:QF].T
-        grad_key_single = joined(full[:, 256:], 24).reshape(ROWS * 24, -1).T
+        own = jnp.concatenate([share[:256], summed[112:160]], axis=0)
+        own = gather(own, "row", ROWS // 2, CHIPS)
+        results = assembled(own, other_core(own), share)
+    key_weight_grad, query_weight_grad, key_single_grad, query_single_grad, pair_weight_grad = results
     return (
-        grad_query_single,
-        grad_key_single,
-        grad_query_weight,
-        grad_key_weight,
-        grad_pair_weight,
+        query_single_grad,
+        key_single_grad,
+        query_weight_grad.T,
+        key_weight_grad.T,
+        pair_weight_grad.T,
         grad_pair,
     )
 

time: 126 us -> 126 us (level)
  waiting for transfers between devices: 22.7 us -> 18.2 us
  local copies, waits for them, and re-layouts: 9.78 us -> 13.4 us
  other arithmetic: 3.66 us -> 1.14 us
  starting transfers between devices: 13.6 us -> 16 us
    all_to_all x2, waiting for transfers between devices: 18.7 us -> 13.5 us  [exchange(): return lax.all_to_all(values, axis, 0, 0, axis_index_groups=groups)]
    unnamed x34 -> x37, local copies, waits for them, and re-layouts: 7.65 us -> 12.5 us
    ppermute x2, starting transfers between devices: 5.35 us -> 7.76 us  [other_core(): return lax.ppermute(values, 'row', [(i, i ^ 1) for i in range(ROWS)])]
    pallas_call x0 -> x1, Pallas kernels: none -> 1.84 us  [assembled(): pl.pallas_call(assemble_kernel, grid=(3,), out_shape=(jax.ShapeDtypeStruc...]
    concatenate x5 -> x1, other arithmetic: 1.6 us -> 0.01 us  [local(): own = jnp.concatenate([share[:256], summed[112:160]], axis=0)]
    all_to_all x3 -> x4, blocking collectives: 57.9 us -> 57.1 us  [exchange(): return lax.all_to_all(values, axis, 0, 0, axis_index_groups=groups)]
  transfers between devices with their start and end apart: 4 -> 4, of which waited for: 4 -> 4; matrix products, arithmetic and copies ran while one was open for 1% -> 0% of each run, Pallas kernels for 3% -> 3%
where the time goes in v3:
time: 126 us; the launch traced here: 125 us
  blocking collectives  57.1 us (45%)
  waiting for transfers between devices  18.2 us (14%)
  Pallas kernels  18.1 us (14%)
  starting transfers between devices  16 us (13%)
  local copies, waits for them, and re-layouts  13.4 us (11%)
    all_to_all x4, blocking collectives, exchange(): return lax.all_to_all(values, axis, 0, 0, axis_index_groups=groups)  57.1 us
    all_to_all x2, waiting for transfers between devices, exchange(): return lax.all_to_all(values, axis, 0, 0, axis_index_groups=groups)  13.5 us
    unnamed x37, local copies, waits for them, and re-layouts  12.5 us
    all_to_all x2, starting transfers between devices, exchange(): return lax.all_to_all(values, axis, 0, 0, axis_index_groups=groups)  8.29 us
    ppermute x2, starting transfers between devices, other_core(): return lax.ppermute(values, 'row', [(i, i ^ 1) for i in range(ROWS)])  7.76 us
    pallas_call x1, Pallas kernels, scores_of(): pl.pallas_call(score_kernel, grid=(STEPS,), out_shape=(jax.ShapeDtypeStru...  6.37 us
    pallas_call x1, Pallas kernels, grads_of(): pl.pallas_call(grad_kernel, out_shape=(jax.ShapeDtypeStruct((ALL, KB), BF...  6.18 us
    ppermute x2, waiting for transfers between devices, other_core(): return lax.ppermute(values, 'row', [(i, i ^ 1) for i in range(ROWS)])  4.71 us
  transfers between devices with their start and end apart: 4, of which 4 were waited for; matrix products, arithmetic and copies ran while one was open for 0% of the time, Pallas kernels for 3%

profile of v3, /device:TPU:1, one launch (start us, length us, event | category | flops | bytes accessed | tf_op | source)
XLA Modules:
  0.0 125.1 jit_solution(9779965775783977073)
XLA Ops:
  0.6 0.0 copy-start
  0.6 0.9 copy-done
  1.6 0.0 copy-start.3
  1.6 1.1 copy-done.3
  2.6 0.0 copy-start.4
  2.6 0.9 copy-done.4
  3.6 0.0 copy-start.5
  3.6 0.9 copy-done.5
  4.5 0.0 copy-start.6
  4.5 0.8 copy-done.6
  5.3 0.0 copy-start.7
  5.3 0.8 copy-done.7
  6.1 0.0 copy-start.8
  6.1 0.8 copy-done.8
  6.9 0.0 copy-start.9
  6.9 0.7 copy-done.9
  7.6 0.0 copy-start.10
  7.6 0.7 copy-done.10
  8.3 0.0 copy-start.11
  8.3 0.7 copy-done.11
  9.0 0.0 copy-start.13
  9.0 0.7 copy-done.13
  9.7 0.0 copy-start.14
  9.7 0.7 copy-done.14
  10.3 0.0 copy-start.15
  10.3 0.7 copy-done.15
  11.0 6.4 %row_scores.1 = (f32[1024,256]{1,0:T(8,128)S(1)}, f32[1024,256]{1,0:T(8,128)S(1)}, bf16[336,256]{1,0:T(8,128)(2,1)S(1)}, bf16[64,336]{1,0:T(8,128)(2,1)S(1)}, bf...) custom-call(s32[16]{0:T(128)S(1)} %copy-done.14, s32[4096]{0:T(1024)S(1)} %copy-done.10, s32[4096]{0:T(1024)S(1)} %copy-done.9, ...), custom_call_target="tpu_custom_call" | custom-call | flops 2000000000 | bytes 8000000 | tf_op jit(solution)/shard_map/row_scores/pallas_call | solution.py:406
  17.4 22.3 %all_to_all.30.parts = f32[16,3,8,128]{3,2,1,0:T(8,128)S(1)} all-to-all(f32[16,3,8,128]{3,2,1,0:T(8,128)S(1)} %broadcast_in_dim.8), channel_id=1, replica_groups=mesh['row'=16,'col'=16] {'col'}, dimensions={0} | all-to-all | bytes 393216 | tf_op jit(solution)/shard_map/row_statistics/all_to_all | solution.py:527
  39.7 6.2 %feature_grads.1 = (bf16[1024,256]{1,0:T(8,128)(2,1)S(1)}, bf16[1024,256]{1,0:T(8,128)(2,1)S(1)}, f32[8,232,128]{2,1,0:T(8,128)S(1)}, f32[8,232,128]{2,1,0:T(8,128)S(1)}, f32[192,128]{1,0:T(8,128)S(1)}) custom-call(s32[16]{0:T(128)S(1)} %copy-done.14, s32[4096]{0:T(1024)S(1)} %copy-done.10, f32[12]{0:T(128)S(1)} %copy-done.15, s32[32,128]{1,0:T(8,128)S(1)} %bitcast.19, ...), custom_call_target="tpu_custom_call" | custom-call | flops 3000000000 | bytes 8000000 | tf_op jit(solution)/shard_map/feature_grads/pallas_call | solution.py:463
  45.9 1.9 %collective-permute-start = (f32[8,232,128]{2,1,0:T(8,128)S(1)}, f32[8,232,128]{2,1,0:T(8,128)S(1)}, u32[]{:S(2)}, u32[]{:S(2)}) collective-permute-start(f32[8,232,128]{2,1,0:T(8,128)S(1)} %get-tuple-element.30), channel_id=1, source_target_pairs={{0,16},{16,0},{32,48},{48,32},{64,80},{80,64},{96,112},{112,96},{1... | collective-permute-start | bytes 2850824 | tf_op jit(solution)/shard_map/row_sum/ppermute | solution.py:523
  47.9 2.1 %collective-permute-done = f32[8,232,128]{2,1,0:T(8,128)S(1)} collective-permute-done((f32[8,232,128]{2,1,0:T(8,128)S(1)}, f32[8,232,128]{2,1,0:T(8,128)S(1)}, u32[]{:S(2)}, u32[]{:S(2)}) %collective-permute-start) | collective-permute-done | bytes 950304 | tf_op jit(solution)/shard_map/row_sum/ppermute | solution.py:523
  50.0 1.1 add.3
  51.1 0.0 copy-start.12
  51.1 4.9 %all-to-all-start.1 = ((f32[8,232,128]{2,1,0:T(8,128)}), f32[8,232,128]{2,1,0:T(8,128)S(1)}, u32[]{:S(2)}, u32[]{:S(2)}) async-start(f32[8,232,128]{2,1,0:T(8,128)} %add.3), calls=%async_computation.1 | async-start | bytes 1900544 | tf_op jit(solution)/shard_map/row_sum/all_to_all | solution.py:527
  56.0 0.0 copy-done.12
  56.0 0.0 copy-start.2
  56.0 2.2 %copy-done.2 = bf16[64,256,128]{2,1,0:T(8,128)(2,1)S(1)} copy-done((bf16[64,256,128]{2,1,0:T(8,128)(2,1)S(1)}, bf16[64,256,128]{2,1,0:T(8,128)(2,1)}, u32[]{:S(2)}) %copy-start.2) | copy-done | bytes 4194328
  58.2 3.8 %pair_grads.1 = (bf16[64,256,128]{2,1,0:T(8,128)(2,1)}, f32[16,128]{1,0:T(8,128)S(1)}) custom-call(bf16[12,128]{1,0:T(8,128)(2,1)S(1)} %bitcast.21, bf16[64,256,128]{2,1,0:T(8,128)(2,1)S(1)} %copy-done.2, bf16[1024,256]{1,0:T(8,128)(2,1)S(1)} %get-tuple-element.31.weights, bf16[1024,256]{1,0:T(8,128)(2,1)S(1)} %get-tuple-element.32.scores, ...), custom_call_target="tpu_custom_call" | custom-call | flops 2000000000 | bytes 10000000 | tf_op jit(solution)/shard_map/pair_grads/pallas_call | solution.py:491
  61.9 0.0 copy-start.1
  61.9 8.2 %all-to-all-done.1 = f32[8,232,128]{2,1,0:T(8,128)S(1)} async-done(((f32[8,232,128]{2,1,0:T(8,128)}), f32[8,232,128]{2,1,0:T(8,128)S(1)}, u32[]{:S(2)}, u32[]{:S(2)}) %all-to-all-start.1) | async-done | bytes 950304 | tf_op jit(solution)/shard_map/row_sum/all_to_all | solution.py:527
  70.1 0.0 copy-done.1
  70.2 0.2 fusion
  70.5 7.7 %all_to_all.31 = f32[4,112,128]{2,1,0:T(8,128)S(1)} all-to-all(f32[4,112,128]{2,1,0:T(8,128)S(1)} %bitcast.22), channel_id=1, replica_groups={{0,4,8,12},{1,5,9,13},{2,6,10,14},{3,7,11,15},{16,20,24,28},{17,21,25,2..., dimensions={0} | all-to-all | bytes 458752 | tf_op jit(solution)/shard_map/col_sum/all_to_all | solution.py:527
  78.2 10.5 %all_to_all.32 = f32[4,112,128]{2,1,0:T(8,128)S(1)} all-to-all(f32[4,112,128]{2,1,0:T(8,128)S(1)} %broadcast_in_dim.9), channel_id=1, replica_groups={{0,1,2,3},{4,5,6,7},{8,9,10,11},{12,13,14,15},{16,17,18,19},{20,21,22,2..., dimensions={0} | all-to-all | bytes 458752 | tf_op jit(solution)/shard_map/col_sum/all_to_all | solution.py:527
  88.7 0.7 broadcast_in_dim.10
  89.4 3.4 %all-to-all-start.4 = ((f32[4,112,128]{2,1,0:T(8,128)}), f32[4,112,128]{2,1,0:T(8,128)S(1)}, u32[]{:S(2)}, u32[]{:S(2)}) async-start(f32[4,112,128]{2,1,0:T(8,128)} %broadcast_in_dim.10), calls=%async_computation.4 | async-start | bytes 458752 | tf_op jit(solution)/shard_map/col_sum/all_to_all | solution.py:527
  92.9 5.3 %all-to-all-done.4 = f32[4,112,128]{2,1,0:T(8,128)S(1)} async-done(((f32[4,112,128]{2,1,0:T(8,128)}), f32[4,112,128]{2,1,0:T(8,128)S(1)}, u32[]{:S(2)}, u32[]{:S(2)}) %all-to-all-start.4) | async-done | bytes 229408 | tf_op jit(solution)/shard_map/col_sum/all_to_all | solution.py:527
  98.2 0.1 broadcast_in_dim.11
  98.3 16.6 %all_to_all.33.own = f32[8,304,128]{2,1,0:T(8,128)S(1)} all-to-all(f32[8,304,128]{2,1,0:T(8,128)S(1)} %broadcast_in_dim.11), channel_id=1, replica_groups={{0,32,64,96,128,160,192,224},{16,48,80,112,144,176,208,240},{1,33,65,97..., dimensions={0} | all-to-all | bytes 2490368 | tf_op jit(solution)/shard_map/row_gather/all_to_all | solution.py:527
  114.8 5.8 %collective-permute-start.1 = (f32[8,304,128]{2,1,0:T(8,128)S(1)}, f32[8,304,128]{2,1,0:T(8,128)S(1)}, u32[]{:S(2)}, u32[]{:S(2)}) collective-permute-start(f32[8,304,128]{2,1,0:T(8,128)S(1)} %all_to_all.33.own), channel_id=1, source_target_pairs={{0,16},{16,0},{32,48},{48,32},{64,80},{80,64},{96,112},{112,96},{1... | collective-permute-start | bytes 3735560 | tf_op jit(solution)/shard_map/row_gather/ppermute | solution.py:523
  120.7 2.6 %collective-permute-done.1.other = f32[8,304,128]{2,1,0:T(8,128)S(1)} collective-permute-done((f32[8,304,128]{2,1,0:T(8,128)S(1)}, f32[8,304,128]{2,1,0:T(8,128)S(1)}, u32[]{:S(2)}, u32[]{:S(2)}) %collective-permute-start.1) | collective-permute-done | bytes 1245216 | tf_op jit(solution)/shard_map/row_gather/ppermute | solution.py:523
  123.2 1.8 %assemble.1 = (f32[816,384]{1,0:T(8,128)}, f32[336,384]{1,0:T(8,128)}, f32[256,384]{1,0:T(8,128)}, f32[64,384]{1,0:T(8,128)}, f32[12,128]{1,0:T(8,128)}) custom-call(f32[8,304,128]{2,1,0:T(8,128)S(1)} %all_to_all.33.own, f32[8,304,128]{2,1,0:T(8,128)S(1)} %collective-permute-done.1.other, f32[448,128]{1,0:T(8,128)S(1)} %bitcast.12), custom_call_target="tpu_custom_call" | custom-call | tf_op jit(solution)/shard_map/row_gather/assemble/pallas_call | solution.py:371
  (15 shorter events, 0.2 us)
Async XLA Ops:
  0.6 0.9 copy-start
  1.6 1.1 copy-start.3
  2.6 0.9 copy-start.4
  3.6 0.9 copy-start.5
  4.5 0.8 copy-start.6
  5.3 0.8 copy-start.7
  6.1 0.8 copy-start.8
  6.9 0.7 copy-start.9
  7.6 0.7 copy-start.10
  8.3 0.7 copy-start.11
  9.0 0.7 copy-start.13
  9.7 0.7 copy-start.14
  10.3 0.7 copy-start.15
  45.9 4.1 %collective-permute-start = (f32[8,232,128]{2,1,0:T(8,128)S(1)}, f32[8,232,128]{2,1,0:T(8,128)S(1)}, u32[]{:S(2)}, u32[]{:S(2)}) collective-permute-start(f32[8,232,128]{2,1,0:T(8,128)S(1)} %get-tuple-element.30), channel_id=1, source_target_pairs={{0,16},{16,0},{32,48},{48,32},{64,80},{80,64},{96,112},{112,96},{1... | collective-permute-start | bytes 2850824 | tf_op jit(solution)/shard_map/row_sum/ppermute | solution.py:523
  51.1 4.9 %copy-start.12 = (bf16[128,12]{0,1:T(8,128)(2,1)S(1)}, bf16[128,12]{0,1:T(8,128)(2,1)}, u32[]{:S(2)}) copy-start(bf16[128,12]{0,1:T(8,128)(2,1)} %param.18) | copy-start | bytes 9220
  51.1 19.0 %all-to-all-start.1 = ((f32[8,232,128]{2,1,0:T(8,128)}), f32[8,232,128]{2,1,0:T(8,128)S(1)}, u32[]{:S(2)}, u32[]{:S(2)}) async-start(f32[8,232,128]{2,1,0:T(8,128)} %add.3), calls=%async_computation.1 | async-start | bytes 1900544 | tf_op jit(solution)/shard_map/row_sum/all_to_all | solution.py:527
  56.0 2.2 %copy-start.2 = (bf16[64,256,128]{2,1,0:T(8,128)(2,1)S(1)}, bf16[64,256,128]{2,1,0:T(8,128)(2,1)}, u32[]{:S(2)}) copy-start(bf16[64,256,128]{2,1,0:T(8,128)(2,1)} %pair.3) | copy-start | bytes 12582916
  61.9 8.2 %copy-start.1 = (bf16[256,384]{1,0:T(8,128)(2,1)S(1)}, bf16[256,384]{1,0:T(8,128)(2,1)}, u32[]{:S(2)}) copy-start(bf16[256,384]{1,0:T(8,128)(2,1)} %key_single.1) | copy-start | bytes 589828
  89.4 8.7 %all-to-all-start.4 = ((f32[4,112,128]{2,1,0:T(8,128)}), f32[4,112,128]{2,1,0:T(8,128)S(1)}, u32[]{:S(2)}, u32[]{:S(2)}) async-start(f32[4,112,128]{2,1,0:T(8,128)} %broadcast_in_dim.10), calls=%async_computation.4 | async-start | bytes 458752 | tf_op jit(solution)/shard_map/col_sum/all_to_all | solution.py:527
  114.8 8.4 %collective-permute-start.1 = (f32[8,304,128]{2,1,0:T(8,128)S(1)}, f32[8,304,128]{2,1,0:T(8,128)S(1)}, u32[]{:S(2)}, u32[]{:S(2)}) collective-permute-start(f32[8,304,128]{2,1,0:T(8,128)S(1)} %all_to_all.33.own), channel_id=1, source_target_pairs={{0,16},{16,0},{32,48},{48,32},{64,80},{80,64},{96,112},{112,96},{1... | collective-permute-start | bytes 3735560 | tf_op jit(solution)/shard_map/row_gather/ppermute | solution.py:523

commit v4 on v3

--- a/solution.py
+++ b/solution.py
@@ -203,6 +203,26 @@
             stats_out[k, pl.ds(2 * step + half, 1), :] = turned[k : k + 1]
 
 
+def spread_kernel(query, grad_single, grad_point, out):
+    column = lax.broadcasted_iota(jnp.int32, (QB, ALL), 1)
+    row = lax.broadcasted_iota(jnp.int32, (QB, ALL), 0)
+    copies = jnp.where(lax.div(column, HP) == row, 1.0, 0.0).astype(BF16)
+
+    def put(begin, values, group, size):
+        count = values.shape[1]
+        feature = lax.broadcasted_iota(jnp.int32, (count, ALL), 0)
+        head = lax.rem(lax.broadcasted_iota(jnp.int32, (count, ALL), 1), HP)
+        of = lax.div(lax.rem(feature, group), size)
+        out[begin : begin + count] = jnp.where(
+            of == head, dot(values, copies, TN), 0.0
+        ).astype(BF16)
+
+    put(0, query[:, 0:VEC], VEC, C)
+    put(VEC, query[:, VEC:], H * P_SIZE, P_SIZE)
+    put(QF, grad_single[...], VEC, C)
+    put(QF + VEC, grad_point[...], H * PV, PV)
+
+
 def grad_kernel(
     offsets,
     mask_s,
@@ -217,8 +237,7 @@
     query_single,
     query_weight,
     key_weight,
-    grad_single,
-    grad_point,
+    columns_of,
     weight_out,
     score_out,
     kept_out,
@@ -267,17 +286,13 @@
     grad_coef = -2.0 * LOGIT_WEIGHT * POINT_SCALE
     key_points = head_mask(QPTS, H * P_SIZE, P_SIZE, axis=0)
     coef = jnp.sum(key_points * head_row(head_weight, grad_coef, QPTS), axis=1, keepdims=True)
-    raw = dot(rows.astype(BF16), scores, TN)
+    raw = dot(columns_of[0:QF], scores)
     key_grad[0:VEC] = SCALE_QK * raw[0:VEC]
-    key_grad[VEC : 2 * VEC] = dot(
-        spread(grad_single[...], head_mask(VEC, VEC, C)).astype(BF16), weights, TN
-    )
+    key_grad[VEC : 2 * VEC] = dot(columns_of[QF : QF + VEC], weights)
     key_grad[2 * VEC : 2 * VEC + QPTS] = coef * (
         key_qk[VEC:QF].astype(F32) * dot(key_points, col_score, NN, HIGHEST) - raw[VEC:QF]
     )
-    key_grad[2 * VEC + QPTS : KF] = dot(
-        spread(grad_point[...], head_mask(VPTS, H * PV, PV)).astype(BF16), weights, TN
-    )
+    key_grad[2 * VEC + QPTS : KF] = dot(columns_of[QF + VEC :], weights)
     key_grad[KF:] = jnp.zeros((ROWS * FEATS - KF, KB), F32)
     key_single_grad[...] = two_part_dot(key_weight[...], key_grad[0:KF], TN, values_first=True)
     raw = dot(scores, key_qk[...], NT)
@@ -380,7 +395,7 @@
         ),
         in_specs=[VECTORS] * 3,
         out_specs=(lanes(KF), lanes(QF), lanes(KB), lanes(QB), whole((H, DZ))),
-        compiler_params=PARAMS,
+        compiler_params=limit(16),
         name="assemble",
     )(own, other, share)
 
@@ -396,7 +411,10 @@
 SCALARS = pl.BlockSpec(memory_space=pltpu.SMEM)
 VECTORS = pl.BlockSpec(memory_space=pltpu.VMEM)
 MIB = 1024 * 1024
-PARAMS = pltpu.CompilerParams(dimension_semantics=("arbitrary",), vmem_limit_bytes=48 * MIB)
+
+
+def limit(mib):
+    return pltpu.CompilerParams(vmem_limit_bytes=mib * MIB)
 
 
 def scores_of(
@@ -444,7 +462,7 @@
             pltpu.VMEM((SLAB, 128), F32),
             pltpu.VMEM((STEP, HP, DZ), F32),
         ],
-        compiler_params=PARAMS,
+        compiler_params=limit(60),
         cost_estimate=pl.CostEstimate(
             flops=2_000_000_000, bytes_accessed=8_000_000, transcendentals=262144
         ),
@@ -458,7 +476,7 @@
 
 def grads_of(
     offsets, mask, head_weight, parts, own, exp_terms, up, key_qk, query, query_single,
-    query_weight, key_weight, grad_single, grad_point,
+    query_weight, key_weight, columns,
 ):
     return pl.pallas_call(
         grad_kernel,
@@ -469,22 +487,36 @@
             jax.ShapeDtypeStruct((ROWS // 2, SHARE, 128), F32),
             jax.ShapeDtypeStruct((3 * QB, 128), F32),
         ),
-        in_specs=[SCALARS] * 3 + [VECTORS] * 12,
+        in_specs=[SCALARS] * 3 + [VECTORS] * 11,
         out_specs=(VECTORS,) * 5,
         scratch_shapes=[
             pltpu.VMEM((ROWS * FEATS, KB), F32),
             pltpu.VMEM((KB, DS), F32),
             pltpu.VMEM((ROWS * 24, DS), F32),
         ],
-        compiler_params=pltpu.CompilerParams(vmem_limit_bytes=24 * MIB),
+        compiler_params=limit(24),
         cost_estimate=pl.CostEstimate(
             flops=3_000_000_000, bytes_accessed=8_000_000, transcendentals=20000
         ),
         name="feature_grads",
     )(
         offsets, mask, head_weight, mask.reshape(32, 128), parts, own, exp_terms, up, key_qk,
-        query, query_single, query_weight, key_weight, grad_single, grad_point,
-    )
+        query, query_single, query_weight, key_weight, columns,
+    )
+
+
+def spread_of(query, grad_single, grad_point):
+    return pl.pallas_call(
+        spread_kernel,
+        out_shape=jax.ShapeDtypeStruct((QF + VEC + VPTS, ALL), BF16),
+        in_specs=[VECTORS] * 3,
+        out_specs=VECTORS,
+        compiler_params=limit(16),
+        cost_estimate=pl.CostEstimate(
+            flops=400_000_000, bytes_accessed=4_000_000, transcendentals=0
+        ),
+        name="spread_features",
+    )(query, grad_single, grad_point)
 
 
 def pair_grads_of(pair_weight, pair, weights, scores, heads):
@@ -504,7 +536,7 @@
         ],
         out_specs=(rows_of(STEP, KB, DZ), whole((HP, DZ))),
         scratch_shapes=[pltpu.VMEM((2 * HP, DZ), BF16)],
-        compiler_params=PARAMS,
+        compiler_params=limit(40),
         cost_estimate=pl.CostEstimate(
             flops=2_000_000_000, bytes_accessed=10_000_000, transcendentals=0
         ),
@@ -574,11 +606,12 @@
         key_single, query_weight, key_weight, pair_weight, pair, grad_single_out,
         grad_point_out, grad_pair_out,
     )
+    columns = spread_of(query, grad_single_out, grad_point_out)
     with jax.named_scope("row_statistics"):
         parts = gather(own, "col", COLS)
     weights, scores, kept, given, query_single_part = grads_of(
         strip_offsets, residue_mask, head_weight, parts, own, terms, up, key_qk, query,
-        query_single, query_weight, key_weight, grad_single_out, grad_point_out,
+        query_single, query_weight, key_weight, columns,
     )
     with jax.named_scope("row_sum"):
         summed = scatter_row(kept, given)

time: 126 us -> 121 us (0.960)
  blocking collectives: 57.1 us -> 34.8 us
  starting transfers between devices: 16 us -> 27.6 us
  waiting for transfers between devices: 18.2 us -> 27.6 us
  local copies, waits for them, and re-layouts: 13.4 us -> 9.54 us
    all_to_all x4 -> x3, blocking collectives: 57.1 us -> 34.8 us  [exchange(): return lax.all_to_all(values, axis, 0, 0, axis_index_groups=groups)]
    all_to_all x2 -> x3, starting transfers between devices: 8.29 us -> 19.9 us  [exchange(): return lax.all_to_all(values, axis, 0, 0, axis_index_groups=groups)]
    all_to_all x2 -> x3, waiting for transfers between devices: 13.5 us -> 22.9 us  [exchange(): return lax.all_to_all(values, axis, 0, 0, axis_index_groups=groups)]
    unnamed x37 -> x45, local copies, waits for them, and re-layouts: 12.5 us -> 7.22 us
    pallas_call x1, Pallas kernels: 6.18 us -> 4.03 us  [grads_of(): pl.pallas_call(grad_kernel, out_shape=(jax.ShapeDtypeStruct((ALL, KB), BF...]
    broadcast_in_dim x4, local copies, waits for them, and re-layouts: 0.83 us -> 2.3 us  [gather(): jnp.broadcast_to(values[None], (parts, *values.shape))]
    pallas_call x1, Pallas kernels: 6.37 us -> 7.82 us  [scores_of(): pl.pallas_call(score_kernel, grid=(STEPS,), out_shape=(jax.ShapeDtypeStru...]
  transfers between devices with their start and end apart: 4 -> 5, of which waited for: 4 -> 5; matrix products, arithmetic and copies ran while one was open for 0% -> 0% of each run, Pallas kernels for 3% -> 4%
where the time goes in v4:
time: 121 us; the launch traced here: 120 us
  blocking collectives  34.8 us (29%)
  starting transfers between devices  27.6 us (23%)
  waiting for transfers between devices  27.6 us (23%)
  Pallas kernels  18.1 us (15%)
  local copies, waits for them, and re-layouts  9.54 us (8%)
    all_to_all x3, blocking collectives, exchange(): return lax.all_to_all(values, axis, 0, 0, axis_index_groups=groups)  34.8 us
    all_to_all x3, waiting for transfers between devices, exchange(): return lax.all_to_all(values, axis, 0, 0, axis_index_groups=groups)  22.9 us
    all_to_all x3, starting transfers between devices, exchange(): return lax.all_to_all(values, axis, 0, 0, axis_index_groups=groups)  19.9 us
    pallas_call x1, Pallas kernels, scores_of(): pl.pallas_call(score_kernel, grid=(STEPS,), out_shape=(jax.ShapeDtypeStru...  7.82 us
    ppermute x2, starting transfers between devices, other_core(): return lax.ppermute(values, 'row', [(i, i ^ 1) for i in range(ROWS)])  7.69 us
    unnamed x45, local copies, waits for them, and re-layouts  7.22 us
    ppermute x2, waiting for transfers between devices, other_core(): return lax.ppermute(values, 'row', [(i, i ^ 1) for i in range(ROWS)])  4.71 us
    pallas_call x1, Pallas kernels, grads_of(): pl.pallas_call(grad_kernel, out_shape=(jax.ShapeDtypeStruct((ALL, KB), BF...  4.03 us
  transfers between devices with their start and end apart: 5, of which 5 were waited for; matrix products, arithmetic and copies ran while one was open for 0% of the time, Pallas kernels for 4%

profile of v4, /device:TPU:1, one launch (start us, length us, event | category | flops | bytes accessed | tf_op | source)
XLA Modules:
  0.0 120.0 jit_solution(4751277531120533061)
XLA Ops:
  0.6 0.0 copy-start
  0.6 0.0 copy-start.3
  0.7 0.0 copy-start.6
  0.7 7.8 %row_scores.1 = (f32[1024,256]{1,0:T(8,128)}, f32[1024,256]{1,0:T(8,128)}, bf16[336,256]{1,0:T(8,128)(2,1)}, bf16[64,336]{1,0:T(8,128)(2,1)}, bf16[64,16,128]{2,1,0:T(8,128)(2,1)}, /*index=5*/f32[3,8,128]{2,1,0:T(8,128)}) custom-call(s32[16]{0:T(128)} %offsets.3, s32[4096]{0:T(1024)} %mask_s.3, s32[4096]{0:T(1024)} %chain_s.1, f32[12]{0:T(128)} %head_weight.3, ...), custom_call_target="tpu_custom_call" | custom-call | flops 2000000000 | bytes 8000000 | tf_op jit(solution)/shard_map/row_scores/pallas_call | solution.py:424
  8.5 0.0 copy-start.2
  8.5 0.0 copy-start.4
  8.5 0.0 copy-start.7
  8.5 0.0 copy-start.8
  8.5 0.0 copy-start.9
  8.5 0.0 copy-start.11
  8.6 0.0 copy-start.12
  8.6 1.5 %broadcast_in_dim.8 = f32[16,3,8,128]{3,2,1,0:T(8,128)} broadcast(f32[3,8,128]{2,1,0:T(8,128)} %get-tuple-element.24.own), dimensions={1,2,3} | broadcast | bytes 208896 | tf_op jit(solution)/shard_map/row_statistics/broadcast_in_dim | solution.py:563
  10.1 11.6 %all-to-all-start = ((f32[16,3,8,128]{3,2,1,0:T(8,128)}), f32[16,3,8,128]{3,2,1,0:T(8,128)S(1)}, u32[]{:S(2)}, u32[]{:S(2)}) async-start(f32[16,3,8,128]{3,2,1,0:T(8,128)} %broadcast_in_dim.8), calls=%async_computation | async-start | bytes 393216 | tf_op jit(solution)/shard_map/row_statistics/all_to_all | solution.py:559
  21.6 0.0 copy-done
  21.7 0.0 copy-done.3
  21.7 0.0 copy-start.1
  21.7 0.8 copy-done.1
  22.5 0.7 spread_features.1.columns_of
  23.1 9.5 %all-to-all-done.parts = f32[16,3,8,128]{3,2,1,0:T(8,128)S(1)} async-done(((f32[16,3,8,128]{3,2,1,0:T(8,128)}), f32[16,3,8,128]{3,2,1,0:T(8,128)S(1)}, u32[]{:S(2)}, u32[]{:S(2)}) %all-to-all-start) | async-done | bytes 196640 | tf_op jit(solution)/shard_map/row_statistics/all_to_all | solution.py:559
  32.6 0.0 copy-done.6
  32.6 0.0 copy-done.2
  32.6 0.0 copy-done.4
  32.6 0.0 copy-done.7
  32.6 0.0 copy-done.8
  32.6 0.0 copy-done.9
  32.6 0.0 copy-done.11
  32.6 0.0 copy-done.12
  32.7 0.0 copy-start.13
  32.7 1.2 %copy-done.13 = f32[1024,256]{1,0:T(8,128)S(1)} copy-done((f32[1024,256]{1,0:T(8,128)S(1)}, f32[1024,256]{1,0:T(8,128)}, u32[]{:S(2)}) %copy-start.13) | copy-done | bytes 1048600
  33.9 0.0 copy-start.14
  33.9 1.2 %copy-done.14 = f32[1024,256]{1,0:T(8,128)S(1)} copy-done((f32[1024,256]{1,0:T(8,128)S(1)}, f32[1024,256]{1,0:T(8,128)}, u32[]{:S(2)}) %copy-start.14) | copy-done | bytes 1048600
  35.1 0.0 copy-start.18
  35.1 0.9 copy-done.18
  36.0 4.0 %feature_grads.1 = (bf16[1024,256]{1,0:T(8,128)(2,1)S(1)}, bf16[1024,256]{1,0:T(8,128)(2,1)S(1)}, f32[8,232,128]{2,1,0:T(8,128)S(1)}, f32[8,232,128]{2,1,0:T(8,128)S(1)}, f32[192,128]{1,0:T(8,128)S(1)}) custom-call(s32[16]{0:T(128)S(1)} %copy-done.11, s32[4096]{0:T(1024)S(1)} %copy-done.9, f32[12]{0:T(128)S(1)} %copy-done.12, s32[32,128]{1,0:T(8,128)S(1)} %bitcast.18, ...), custom_call_target="tpu_custom_call" | custom-call | flops 3000000000 | bytes 8000000 | tf_op jit(solution)/shard_map/feature_grads/pallas_call | solution.py:481
  40.1 0.0 copy-start.15
  40.1 0.8 copy-done.15
  40.9 1.9 %collective-permute-start = (f32[8,232,128]{2,1,0:T(8,128)S(1)}, f32[8,232,128]{2,1,0:T(8,128)S(1)}, u32[]{:S(2)}, u32[]{:S(2)}) collective-permute-start(f32[8,232,128]{2,1,0:T(8,128)S(1)} %get-tuple-element.30), channel_id=1, source_target_pairs={{0,16},{16,0},{32,48},{48,32},{64,80},{80,64},{96,112},{112,96},{1... | collective-permute-start | bytes 2850824 | tf_op jit(solution)/shard_map/row_sum/ppermute | solution.py:555
  42.7 2.1 %collective-permute-done = f32[8,232,128]{2,1,0:T(8,128)S(1)} collective-permute-done((f32[8,232,128]{2,1,0:T(8,128)S(1)}, f32[8,232,128]{2,1,0:T(8,128)S(1)}, u32[]{:S(2)}, u32[]{:S(2)}) %collective-permute-start) | collective-permute-done | bytes 950304 | tf_op jit(solution)/shard_map/row_sum/ppermute | solution.py:555
  44.9 1.1 add.3
  46.0 0.0 copy-start.10
  46.0 0.0 copy-start.16
  46.0 0.0 copy-start.17
  46.0 4.9 %all-to-all-start.1 = ((f32[8,232,128]{2,1,0:T(8,128)}), f32[8,232,128]{2,1,0:T(8,128)S(1)}, u32[]{:S(2)}, u32[]{:S(2)}) async-start(f32[8,232,128]{2,1,0:T(8,128)} %add.3), calls=%async_computation.1 | async-start | bytes 1900544 | tf_op jit(solution)/shard_map/row_sum/all_to_all | solution.py:559
  50.9 0.0 copy-done.10
  50.9 0.0 copy-done.16
  50.9 0.0 copy-done.17
  50.9 0.0 copy-start.5
  50.9 2.2 %copy-done.5 = bf16[64,256,128]{2,1,0:T(8,128)(2,1)S(1)} copy-done((bf16[64,256,128]{2,1,0:T(8,128)(2,1)S(1)}, bf16[64,256,128]{2,1,0:T(8,128)(2,1)}, u32[]{:S(2)}) %copy-start.5) | copy-done | bytes 4194328
  53.1 3.7 %pair_grads.1 = (bf16[64,256,128]{2,1,0:T(8,128)(2,1)}, f32[16,128]{1,0:T(8,128)S(1)}) custom-call(bf16[12,128]{1,0:T(8,128)(2,1)S(1)} %bitcast.20, bf16[64,256,128]{2,1,0:T(8,128)(2,1)S(1)} %copy-done.5, bf16[1024,256]{1,0:T(8,128)(2,1)S(1)} %get-tuple-element.31.weights, bf16[1024,256]{1,0:T(8,128)(2,1)S(1)} %copy-done.16, bf16[64,16,128]{2,1,0:T(8,128)(2,1)S(1)} %copy-done.17), custom_call_target="tpu_custom_call" | custom-call | flops 2000000000 | bytes 10000000 | tf_op jit(solution)/shard_map/pair_grads/pallas_call | solution.py:523
  56.8 0.0 copy-start.19
  56.8 8.2 %all-to-all-done.1 = f32[8,232,128]{2,1,0:T(8,128)S(1)} async-done(((f32[8,232,128]{2,1,0:T(8,128)}), f32[8,232,128]{2,1,0:T(8,128)S(1)}, u32[]{:S(2)}, u32[]{:S(2)}) %all-to-all-start.1) | async-done | bytes 950304 | tf_op jit(solution)/shard_map/row_sum/all_to_all | solution.py:559
  65.1 0.0 copy-done.19
  65.1 0.2 fusion
  65.4 7.7 %all_to_all.30 = f32[4,112,128]{2,1,0:T(8,128)S(1)} all-to-all(f32[4,112,128]{2,1,0:T(8,128)S(1)} %bitcast.21), channel_id=1, replica_groups={{0,4,8,12},{1,5,9,13},{2,6,10,14},{3,7,11,15},{16,20,24,28},{17,21,25,2..., dimensions={0} | all-to-all | bytes 458752 | tf_op jit(solution)/shard_map/col_sum/all_to_all | solution.py:559
  73.1 10.5 %all_to_all.31 = f32[4,112,128]{2,1,0:T(8,128)S(1)} all-to-all(f32[4,112,128]{2,1,0:T(8,128)S(1)} %broadcast_in_dim.9), channel_id=1, replica_groups={{0,1,2,3},{4,5,6,7},{8,9,10,11},{12,13,14,15},{16,17,18,19},{20,21,22,2..., dimensions={0} | all-to-all | bytes 458752 | tf_op jit(solution)/shard_map/col_sum/all_to_all | solution.py:559
  83.7 0.7 broadcast_in_dim.10
  84.4 3.4 %all-to-all-start.4 = ((f32[4,112,128]{2,1,0:T(8,128)}), f32[4,112,128]{2,1,0:T(8,128)S(1)}, u32[]{:S(2)}, u32[]{:S(2)}) async-start(f32[4,112,128]{2,1,0:T(8,128)} %broadcast_in_dim.10), calls=%async_computation.4 | async-start | bytes 458752 | tf_op jit(solution)/shard_map/col_sum/all_to_all | solution.py:559
  87.8 5.3 %all-to-all-done.4 = f32[4,112,128]{2,1,0:T(8,128)S(1)} async-done(((f32[4,112,128]{2,1,0:T(8,128)}), f32[4,112,128]{2,1,0:T(8,128)S(1)}, u32[]{:S(2)}, u32[]{:S(2)}) %all-to-all-start.4) | async-done | bytes 229408 | tf_op jit(solution)/shard_map/col_sum/all_to_all | solution.py:559
  93.1 0.1 broadcast_in_dim.11
  93.2 16.6 %all_to_all.32.own = f32[8,304,128]{2,1,0:T(8,128)S(1)} all-to-all(f32[8,304,128]{2,1,0:T(8,128)S(1)} %broadcast_in_dim.11), channel_id=1, replica_groups={{0,32,64,96,128,160,192,224},{16,48,80,112,144,176,208,240},{1,33,65,97..., dimensions={0} | all-to-all | bytes 2490368 | tf_op jit(solution)/shard_map/row_gather/all_to_all | solution.py:559
  109.8 5.8 %collective-permute-start.1 = (f32[8,304,128]{2,1,0:T(8,128)S(1)}, f32[8,304,128]{2,1,0:T(8,128)S(1)}, u32[]{:S(2)}, u32[]{:S(2)}) collective-permute-start(f32[8,304,128]{2,1,0:T(8,128)S(1)} %all_to_all.32.own), channel_id=1, source_target_pairs={{0,16},{16,0},{32,48},{48,32},{64,80},{80,64},{96,112},{112,96},{1... | collective-permute-start | bytes 3735560 | tf_op jit(solution)/shard_map/row_gather/ppermute | solution.py:555
  115.6 2.6 %collective-permute-done.1.other = f32[8,304,128]{2,1,0:T(8,128)S(1)} collective-permute-done((f32[8,304,128]{2,1,0:T(8,128)S(1)}, f32[8,304,128]{2,1,0:T(8,128)S(1)}, u32[]{:S(2)}, u32[]{:S(2)}) %collective-permute-start.1) | collective-permute-done | bytes 1245216 | tf_op jit(solution)/shard_map/row_gather/ppermute | solution.py:555
  118.1 1.8 %assemble.1 = (f32[816,384]{1,0:T(8,128)}, f32[336,384]{1,0:T(8,128)}, f32[256,384]{1,0:T(8,128)}, f32[64,384]{1,0:T(8,128)}, f32[12,128]{1,0:T(8,128)}) custom-call(f32[8,304,128]{2,1,0:T(8,128)S(1)} %all_to_all.32.own, f32[8,304,128]{2,1,0:T(8,128)S(1)} %collective-permute-done.1.other, f32[448,128]{1,0:T(8,128)S(1)} %bitcast.12), custom_call_target="tpu_custom_call" | custom-call | tf_op jit(solution)/shard_map/row_gather/assemble/pallas_call | solution.py:386
  (14 shorter events, 0.2 us)
Async XLA Ops:
  0.6 21.0 %copy-start = (bf16[64,288]{1,0:T(8,128)(2,1)S(1)}, bf16[64,288]{1,0:T(8,128)(2,1)}, u32[]{:S(2)}) copy-start(bf16[64,288]{1,0:T(8,128)(2,1)} %grad_point.3) | copy-start | bytes 110596
  0.6 21.0 %copy-start.3 = (bf16[64,192]{1,0:T(8,128)(2,1)S(1)}, bf16[64,192]{1,0:T(8,128)(2,1)}, u32[]{:S(2)}) copy-start(bf16[64,192]{1,0:T(8,128)(2,1)} %grad_single.3) | copy-start | bytes 73732
  0.7 31.9 %copy-start.6 = (bf16[384,816]{0,1:T(8,128)(2,1)S(1)}, bf16[384,816]{0,1:T(8,128)(2,1)}, u32[]{:S(2)}) copy-start(bf16[384,816]{0,1:T(8,128)(2,1)} %param.17) | copy-start | bytes 1880068
  8.5 24.1 %copy-start.2 = (bf16[64,336]{1,0:T(8,128)(2,1)S(1)}, bf16[64,336]{1,0:T(8,128)(2,1)}, u32[]{:S(2)}) copy-start(bf16[64,336]{1,0:T(8,128)(2,1)} %get-tuple-element.28.query) | copy-start | bytes 129028
  8.5 24.1 %copy-start.4 = (f32[3,8,128]{2,1,0:T(8,128)S(1)}, f32[3,8,128]{2,1,0:T(8,128)}, u32[]{:S(2)}) copy-start(f32[3,8,128]{2,1,0:T(8,128)} %get-tuple-element.24.own) | copy-start | bytes 36868
  8.5 24.1 %copy-start.7 = (bf16[384,336]{0,1:T(8,128)(2,1)S(1)}, bf16[384,336]{0,1:T(8,128)(2,1)}, u32[]{:S(2)}) copy-start(bf16[384,336]{0,1:T(8,128)(2,1)} %param.16) | copy-start | bytes 774148
  8.5 24.1 %copy-start.8 = (bf16[64,384]{1,0:T(8,128)(2,1)S(1)}, bf16[64,384]{1,0:T(8,128)(2,1)}, u32[]{:S(2)}) copy-start(bf16[64,384]{1,0:T(8,128)(2,1)} %query_single.3) | copy-start | bytes 147460
  8.5 24.1 %copy-start.9 = (s32[4096]{0:T(1024)S(1)}, s32[4096]{0:T(1024)}, u32[]{:S(2)}) copy-start(s32[4096]{0:T(1024)} %mask_s.3) | copy-start | bytes 49156
  8.5 24.1 %copy-start.11 = (s32[16]{0:T(128)S(1)}, s32[16]{0:T(128)}, u32[]{:S(2)}) copy-start(s32[16]{0:T(128)} %offsets.3) | copy-start | bytes 196
  8.6 24.1 %copy-start.12 = (f32[12]{0:T(128)S(1)}, f32[12]{0:T(128)}, u32[]{:S(2)}) copy-start(f32[12]{0:T(128)} %head_weight.3) | copy-start | bytes 148
  10.1 22.5 %all-to-all-start = ((f32[16,3,8,128]{3,2,1,0:T(8,128)}), f32[16,3,8,128]{3,2,1,0:T(8,128)S(1)}, u32[]{:S(2)}, u32[]{:S(2)}) async-start(f32[16,3,8,128]{3,2,1,0:T(8,128)} %broadcast_in_dim.8), calls=%async_computation | async-start | bytes 393216 | tf_op jit(solution)/shard_map/row_statistics/all_to_all | solution.py:559
  21.7 0.8 copy-start.1
  32.7 1.2 %copy-start.13 = (f32[1024,256]{1,0:T(8,128)S(1)}, f32[1024,256]{1,0:T(8,128)}, u32[]{:S(2)}) copy-start(f32[1024,256]{1,0:T(8,128)} %get-tuple-element.25.exp_terms) | copy-start | bytes 3145732
  33.9 1.2 %copy-start.14 = (f32[1024,256]{1,0:T(8,128)S(1)}, f32[1024,256]{1,0:T(8,128)}, u32[]{:S(2)}) copy-start(f32[1024,256]{1,0:T(8,128)} %get-tuple-element.26.up) | copy-start | bytes 3145732
  35.1 0.9 copy-start.18
  40.1 0.8 copy-start.15
  40.9 4.0 %collective-permute-start = (f32[8,232,128]{2,1,0:T(8,128)S(1)}, f32[8,232,128]{2,1,0:T(8,128)S(1)}, u32[]{:S(2)}, u32[]{:S(2)}) collective-permute-start(f32[8,232,128]{2,1,0:T(8,128)S(1)} %get-tuple-element.30), channel_id=1, source_target_pairs={{0,16},{16,0},{32,48},{48,32},{64,80},{80,64},{96,112},{112,96},{1... | collective-permute-start | bytes 2850824 | tf_op jit(solution)/shard_map/row_sum/ppermute | solution.py:555
  46.0 4.9 %copy-start.10 = (bf16[128,12]{0,1:T(8,128)(2,1)S(1)}, bf16[128,12]{0,1:T(8,128)(2,1)}, u32[]{:S(2)}) copy-start(bf16[128,12]{0,1:T(8,128)(2,1)} %param.18) | copy-start | bytes 9220
  46.0 4.9 %copy-start.16 = (bf16[1024,256]{1,0:T(8,128)(2,1)S(1)}, bf16[1024,256]{1,0:T(8,128)(2,1)}, u32[]{:S(2)}) copy-start(bf16[1024,256]{1,0:T(8,128)(2,1)} %copy-done.15) | copy-start | bytes 1572868
  46.0 4.9 %copy-start.17 = (bf16[64,16,128]{2,1,0:T(8,128)(2,1)S(1)}, bf16[64,16,128]{2,1,0:T(8,128)(2,1)}, u32[]{:S(2)}) copy-start(bf16[64,16,128]{2,1,0:T(8,128)(2,1)} %get-tuple-element.33.heads) | copy-start | bytes 786436
  46.0 19.0 %all-to-all-start.1 = ((f32[8,232,128]{2,1,0:T(8,128)}), f32[8,232,128]{2,1,0:T(8,128)S(1)}, u32[]{:S(2)}, u32[]{:S(2)}) async-start(f32[8,232,128]{2,1,0:T(8,128)} %add.3), calls=%async_computation.1 | async-start | bytes 1900544 | tf_op jit(solution)/shard_map/row_sum/all_to_all | solution.py:559
  50.9 2.2 %copy-start.5 = (bf16[64,256,128]{2,1,0:T(8,128)(2,1)S(1)}, bf16[64,256,128]{2,1,0:T(8,128)(2,1)}, u32[]{:S(2)}) copy-start(bf16[64,256,128]{2,1,0:T(8,128)(2,1)} %pair.3) | copy-start | bytes 12582916
  56.8 8.2 %copy-start.19 = (bf16[256,384]{1,0:T(8,128)(2,1)S(1)}, bf16[256,384]{1,0:T(8,128)(2,1)}, u32[]{:S(2)}) copy-start(bf16[256,384]{1,0:T(8,128)(2,1)} %key_single.1) | copy-start | bytes 589828
  84.4 8.7 %all-to-all-start.4 = ((f32[4,112,128]{2,1,0:T(8,128)}), f32[4,112,128]{2,1,0:T(8,128)S(1)}, u32[]{:S(2)}, u32[]{:S(2)}) async-start(f32[4,112,128]{2,1,0:T(8,128)} %broadcast_in_dim.10), calls=%async_computation.4 | async-start | bytes 458752 | tf_op jit(solution)/shard_map/col_sum/all_to_all | solution.py:559
  109.8 8.4 %collective-permute-start.1 = (f32[8,304,128]{2,1,0:T(8,128)S(1)}, f32[8,304,128]{2,1,0:T(8,128)S(1)}, u32[]{:S(2)}, u32[]{:S(2)}) collective-permute-start(f32[8,304,128]{2,1,0:T(8,128)S(1)} %all_to_all.32.own), channel_id=1, source_target_pairs={{0,16},{16,0},{32,48},{48,32},{64,80},{80,64},{96,112},{112,96},{1... | collective-permute-start | bytes 3735560 | tf_op jit(solution)/shard_map/row_gather/ppermute | solution.py:555

commit v5 on v4

--- a/solution.py
+++ b/solution.py
@@ -1,3 +1,4 @@
+import functools
 import math
 
 import jax
@@ -27,8 +28,9 @@
 STEPS = QB // STEP
 SLAB = STEP * HP
 ALL = QB * HP
-FEATS = 56
-SHARE = 232
+FEATS = KF // ROWS
+QFEATS = QF // ROWS
+SHARE = 216
 
 LOGIT_WEIGHT = math.sqrt(1.0 / 3.0)
 MASKED_LOGIT = -100000.0
@@ -129,6 +131,7 @@
     both,
     stat,
     spread_pairs,
+    stats,
 ):
     step = pl.program_id(0)
 
@@ -200,7 +203,12 @@
     for half in range(2):
         turned = stat[128 * half : 128 * (half + 1)].T
         for k in range(3):
-            stats_out[k, pl.ds(2 * step + half, 1), :] = turned[k : k + 1]
+            stats[k, pl.ds(2 * step + half, 1), :] = turned[k : k + 1]
+
+    @pl.when(step == STEPS - 1)
+    def _():
+        for s in range(COLS):
+            stats_out[s] = stats[...]
 
 
 def spread_kernel(query, grad_single, grad_point, out):
@@ -229,7 +237,6 @@
     head_weight,
     mask_v,
     parts,
-    own,
     exp_terms,
     up,
     key_qk,
@@ -256,7 +263,7 @@
         share = jnp.exp(parts[s, 0] - row_top)
         row_total += share * parts[s, 1]
         moment += share * parts[s, 2]
-    factor = jnp.exp(own[0] - row_top) / row_total
+    factor = jnp.exp(parts[lax.axis_index("col"), 0] - row_top) / row_total
     centre = moment / row_total
     columns = jnp.concatenate([factor, centre], axis=0).T
     key_live = jnp.where(key_line(mask_v) == 1, 1.0, 0.0)
@@ -293,8 +300,7 @@
         key_qk[VEC:QF].astype(F32) * dot(key_points, col_score, NN, HIGHEST) - raw[VEC:QF]
     )
     key_grad[2 * VEC + QPTS : KF] = dot(columns_of[QF + VEC :], weights)
-    key_grad[KF:] = jnp.zeros((ROWS * FEATS - KF, KB), F32)
-    key_single_grad[...] = two_part_dot(key_weight[...], key_grad[0:KF], TN, values_first=True)
+    key_single_grad[...] = two_part_dot(key_weight[...], key_grad[...], TN, values_first=True)
     raw = dot(scores, key_qk[...], NT)
     head_coef = head_column(head_weight, grad_coef, QF)
     head_coef = jnp.concatenate([head_coef] * QB, axis=0)
@@ -304,25 +310,25 @@
     single = two_part_dot(query_weight[...], query_grad, NN, values_first=True)
     for k in range(3):
         single_out[QB * k : QB * (k + 1)] = single[:, 128 * k : 128 * (k + 1)]
-    query_weight_grad[0:QF] = two_part_dot(query_single[...], query_grad, TN, values_first=True)
-    query_weight_grad[QF:] = jnp.zeros((ROWS * 24 - QF, DS), F32)
-    core = lax.rem(lax.axis_index("row"), 2)
-    for out, parity in ((kept_out, core), (given_out, 1 - core)):
-        for q in range(ROWS // 2):
-            r = 2 * q + parity
-            at = pl.ds(pl.multiple_of(FEATS * r, 8), FEATS)
-            for k in range(2):
-                out[q, FEATS * k : FEATS * (k + 1)] = key_grad[at, 128 * k : 128 * (k + 1)]
-            at = pl.ds(pl.multiple_of(16 * r, 8), 16)
-            for k in range(3):
-                out[q, 112 + 16 * k : 128 + 16 * k] = key_single_grad[
-                    at, 128 * k : 128 * (k + 1)
-                ]
-            at = pl.ds(pl.multiple_of(24 * r, 8), 24)
-            for k in range(3):
-                out[q, 160 + 24 * k : 184 + 24 * k] = query_weight_grad[
-                    at, 128 * k : 128 * (k + 1)
-                ]
+    query_weight_grad[...] = two_part_dot(query_single[...], query_grad, TN, values_first=True)
+    first = lax.rem(lax.axis_index("row"), 2) == 0
+
+    def put(q, begin, source, count, k):
+        lanes = slice(128 * k, 128 * (k + 1))
+        even = source[count * 2 * q : count * (2 * q + 1), lanes]
+        odd = source[count * (2 * q + 1) : count * (2 * q + 2), lanes]
+        at = slice(begin + count * k, begin + count * (k + 1))
+        kept_out[q, at] = jnp.where(first, even, odd)
+        given_out[q, at] = jnp.where(first, odd, even)
+
+    for q in range(ROWS // 2):
+        for k in range(2):
+            put(q, 0, key_grad, FEATS, k)
+        for k in range(3):
+            put(q, 2 * FEATS, key_single_grad, 16, k)
+            put(q, 2 * FEATS + 48, query_weight_grad, QFEATS, k)
+        for out in (kept_out, given_out):
+            out[q, 2 * FEATS + 48 + 3 * QFEATS :] = jnp.zeros((3, 128), F32)
 
 
 def pair_kernel(pair_weight, pair, weights, scores, heads, pair_out, bias_out, lanes):
@@ -358,27 +364,27 @@
     lane = pl.program_id(0)
 
     def chunk(r, begin, count):
-        at = pl.ds(pl.multiple_of(begin, 8), count)
-        mine, theirs = own[r // 2, at], other[r // 2, at]
+        mine, theirs = own[r // 2, begin : begin + count], other[r // 2, begin : begin + count]
         if r % 2 == 1:
             mine, theirs = theirs, mine
         return jnp.where(first, mine, theirs)
 
-    for r in range(ROWS):
-        count = min(FEATS, KF - FEATS * r)
-        if count > 0:
-            key_out[FEATS * r : FEATS * r + count] = chunk(r, FEATS * lane, count)
-        if r < QF // 24:
-            query_out[24 * r : 24 * (r + 1)] = chunk(r, 184 + 24 * lane, 24)
-        single_out[16 * r : 16 * (r + 1)] = chunk(r, 256 + 16 * lane, 16)
-    query_single_out[...] = share[pl.ds(pl.multiple_of(256 + QB * lane, 8), QB)]
+    def put(k):
+        for r in range(ROWS):
+            key_out[FEATS * r : FEATS * (r + 1)] = chunk(r, FEATS * k, FEATS)
+            query_out[QFEATS * r : QFEATS * (r + 1)] = chunk(r, 165 + QFEATS * k, QFEATS)
+            single_out[16 * r : 16 * (r + 1)] = chunk(r, 228 + 16 * k, 16)
+        query_single_out[...] = share[228 + QB * k : 228 + QB * (k + 1)]
+
+    for k in range(3):
+        pl.when(lane == k)(functools.partial(put, k))
 
     @pl.when(lane == 0)
     def _():
-        total = chunk(0, 168, 16)
+        total = chunk(0, 153, H)
         for r in range(1, ROWS):
-            total += chunk(r, 168, 16)
-        pair_out[...] = total[0:H]
+            total += chunk(r, 153, H)
+        pair_out[...] = total
 
 
 def assembled(own, other, share):
@@ -430,7 +436,7 @@
             jax.ShapeDtypeStruct((QF, KB), BF16),
             jax.ShapeDtypeStruct((QB, QF), BF16),
             jax.ShapeDtypeStruct((QB, HP, DZ), BF16),
-            jax.ShapeDtypeStruct((3, 8, 128), F32),
+            jax.ShapeDtypeStruct((COLS, 3, 8, 128), F32),
         ),
         in_specs=[SCALARS] * 5
         + [
@@ -452,7 +458,7 @@
             whole((QF, KB)),
             rows_of(STEP, QF),
             rows_of(STEP, HP, DZ),
-            whole((3, 8, 128)),
+            whole((COLS, 3, 8, 128)),
         ),
         scratch_shapes=[
             pltpu.VMEM((QF, KB), BF16),
@@ -461,6 +467,7 @@
             pltpu.VMEM((HP, DZ), BF16),
             pltpu.VMEM((SLAB, 128), F32),
             pltpu.VMEM((STEP, HP, DZ), F32),
+            pltpu.VMEM((3, 8, 128), F32),
         ],
         compiler_params=limit(60),
         cost_estimate=pl.CostEstimate(
@@ -475,7 +482,7 @@
 
 
 def grads_of(
-    offsets, mask, head_weight, parts, own, exp_terms, up, key_qk, query, query_single,
+    offsets, mask, head_weight, parts, exp_terms, up, key_qk, query, query_single,
     query_weight, key_weight, columns,
 ):
     return pl.pallas_call(
@@ -487,12 +494,12 @@
             jax.ShapeDtypeStruct((ROWS // 2, SHARE, 128), F32),
             jax.ShapeDtypeStruct((3 * QB, 128), F32),
         ),
-        in_specs=[SCALARS] * 3 + [VECTORS] * 11,
+        in_specs=[SCALARS] * 3 + [VECTORS] * 10,
         out_specs=(VECTORS,) * 5,
         scratch_shapes=[
-            pltpu.VMEM((ROWS * FEATS, KB), F32),
+            pltpu.VMEM((KF, KB), F32),
             pltpu.VMEM((KB, DS), F32),
-            pltpu.VMEM((ROWS * 24, DS), F32),
+            pltpu.VMEM((QF, DS), F32),
         ],
         compiler_params=limit(24),
         cost_estimate=pl.CostEstimate(
@@ -500,7 +507,7 @@
         ),
         name="feature_grads",
     )(
-        offsets, mask, head_weight, mask.reshape(32, 128), parts, own, exp_terms, up, key_qk,
+        offsets, mask, head_weight, mask.reshape(32, 128), parts, exp_terms, up, key_qk,
         query, query_single, query_weight, key_weight, columns,
     )
 
@@ -608,9 +615,9 @@
     )
     columns = spread_of(query, grad_single_out, grad_point_out)
     with jax.named_scope("row_statistics"):
-        parts = gather(own, "col", COLS)
+        parts = exchange(own, "col")
     weights, scores, kept, given, query_single_part = grads_of(
-        strip_offsets, residue_mask, head_weight, parts, own, terms, up, key_qk, query,
+        strip_offsets, residue_mask, head_weight, parts, terms, up, key_qk, query,
         query_single, query_weight, key_weight, columns,
     )
     with jax.named_scope("row_sum"):
@@ -620,11 +627,15 @@
     key_share = jnp.dot(key_grad, key_single.astype(F32), precision=HIGHEST)
     with jax.named_scope("col_sum"):
         share = jnp.concatenate(
-            lanes_of(key_share) + [bias_part, summed[160:232], query_single_part], axis=0
+            lanes_of(key_share)
+            + [bias_part[:H], summed[150:213], query_single_part, jnp.zeros((28, 128), F32)],
+            axis=0,
         )
         share = sum_col(share)
     with jax.named_scope("row_gather"):
-        own = jnp.concatenate([share[:256], summed[112:160]], axis=0)
+        own = jnp.concatenate(
+            [share[:228], summed[102:150], jnp.zeros((4, 128), F32)], axis=0
+        )
         own = gather(own, "row", ROWS // 2, CHIPS)
         results = assembled(own, other_core(own), share)
     key_weight_grad, query_weight_grad, key_single_grad, query_single_grad, pair_weight_grad = results

time: 121 us -> 119 us (0.983)
    broadcast_in_dim x4 -> x3, local copies, waits for them, and re-layouts: 2.3 us -> 0.8 us  [gather(): jnp.broadcast_to(values[None], (parts, *values.shape))]
    unnamed x45 -> x38, local copies, waits for them, and re-layouts: 7.22 us -> 7.19 us
where the time goes in v5:
time: 119 us; the launch traced here: 118 us
  blocking collectives  34 us (29%)
  starting transfers between devices  27.6 us (23%)
  waiting for transfers between devices  26.6 us (22%)
  Pallas kernels  18.4 us (15%)
  local copies, waits for them, and re-layouts  9.11 us (8%)
    all_to_all x3, blocking collectives, exchange(): return lax.all_to_all(values, axis, 0, 0, axis_index_groups=groups)  34 us
    all_to_all x3, waiting for transfers between devices, exchange(): return lax.all_to_all(values, axis, 0, 0, axis_index_groups=groups)  22.2 us
    all_to_all x3, starting transfers between devices, exchange(): return lax.all_to_all(values, axis, 0, 0, axis_index_groups=groups)  20 us
    pallas_call x1, Pallas kernels, scores_of(): pl.pallas_call(score_kernel, grid=(STEPS,), out_shape=(jax.ShapeDtypeStru...  8.44 us
    ppermute x2, starting transfers between devices, other_core(): return lax.ppermute(values, 'row', [(i, i ^ 1) for i in range(ROWS)])  7.6 us
    unnamed x38, local copies, waits for them, and re-layouts  7.19 us
    ppermute x2, waiting for transfers between devices, other_core(): return lax.ppermute(values, 'row', [(i, i ^ 1) for i in range(ROWS)])  4.48 us
    pallas_call x1, Pallas kernels, pair_grads_of(): pl.pallas_call(pair_kernel, grid=(STEPS,), out_shape=(jax.ShapeDtypeStruc...  3.75 us
  transfers between devices with their start and end apart: 5, of which 5 were waited for; matrix products, arithmetic and copies ran while one was open for 0% of the time, Pallas kernels for 4%

profile of v5, /device:TPU:1, one launch (start us, length us, event | category | flops | bytes accessed | tf_op | source)
XLA Modules:
  0.0 118.1 jit_solution(10332932733084766412)
XLA Ops:
  0.6 0.0 copy-start
  0.6 0.0 copy-start.3
  0.7 0.0 copy-start.5
  0.7 8.4 %row_scores.1 = (f32[1024,256]{1,0:T(8,128)}, f32[1024,256]{1,0:T(8,128)}, bf16[336,256]{1,0:T(8,128)(2,1)}, bf16[64,336]{1,0:T(8,128)(2,1)}, bf16[64,16,128]{2,1,0:T(8,128)(2,1)}, /*index=5*/f32[16,3,8,128]{3,2,1,0:T(8,128)}) custom-call(s32[16]{0:T(128)} %offsets.3, s32[4096]{0:T(1024)} %mask_s.3, s32[4096]{0:T(1024)} %chain_s.1, f32[12]{0:T(128)} %head_weight.3, ...), custom_call_target="tpu_custom_call" | custom-call | flops 2000000000 | bytes 8000000 | tf_op jit(solution)/shard_map/row_scores/pallas_call | solution.py:430
  9.1 0.0 copy-start.2
  9.1 0.0 copy-start.6
  9.1 0.0 copy-start.7
  9.2 0.0 copy-start.8
  9.2 0.0 copy-start.10
  9.2 0.0 copy-start.11
  9.2 11.7 %all-to-all-start = ((f32[16,3,8,128]{3,2,1,0:T(8,128)}), f32[16,3,8,128]{3,2,1,0:T(8,128)S(1)}, u32[]{:S(2)}, u32[]{:S(2)}) async-start(f32[16,3,8,128]{3,2,1,0:T(8,128)} %get-tuple-element.24), calls=%async_computation | async-start | bytes 393216 | tf_op jit(solution)/shard_map/row_statistics/all_to_all | solution.py:566
  20.9 0.0 copy-done
  20.9 0.0 copy-done.3
  20.9 0.0 copy-start.1
  20.9 0.8 copy-done.1
  21.7 0.6 spread_features.1.columns_of
  22.4 9.5 %all-to-all-done.parts = f32[16,3,8,128]{3,2,1,0:T(8,128)S(1)} async-done(((f32[16,3,8,128]{3,2,1,0:T(8,128)}), f32[16,3,8,128]{3,2,1,0:T(8,128)S(1)}, u32[]{:S(2)}, u32[]{:S(2)}) %all-to-all-start) | async-done | bytes 196640 | tf_op jit(solution)/shard_map/row_statistics/all_to_all | solution.py:566
  31.9 0.0 copy-done.5
  31.9 0.0 copy-done.2
  31.9 0.0 copy-done.6
  31.9 0.0 copy-done.7
  31.9 0.0 copy-done.8
  31.9 0.0 copy-done.10
  31.9 0.0 copy-done.11
  31.9 0.0 copy-start.12
  31.9 1.2 %copy-done.12 = f32[1024,256]{1,0:T(8,128)S(1)} copy-done((f32[1024,256]{1,0:T(8,128)S(1)}, f32[1024,256]{1,0:T(8,128)}, u32[]{:S(2)}) %copy-start.12) | copy-done | bytes 1048600
  33.1 0.0 copy-start.13
  33.1 1.2 %copy-done.13 = f32[1024,256]{1,0:T(8,128)S(1)} copy-done((f32[1024,256]{1,0:T(8,128)S(1)}, f32[1024,256]{1,0:T(8,128)}, u32[]{:S(2)}) %copy-start.13) | copy-done | bytes 1048600
  34.4 0.0 copy-start.17
  34.4 0.9 copy-done.17
  35.3 3.7 %feature_grads.1 = (bf16[1024,256]{1,0:T(8,128)(2,1)S(1)}, bf16[1024,256]{1,0:T(8,128)(2,1)S(1)}, f32[8,216,128]{2,1,0:T(8,128)S(1)}, f32[8,216,128]{2,1,0:T(8,128)S(1)}, f32[192,128]{1,0:T(8,128)S(1)}) custom-call(s32[16]{0:T(128)S(1)} %copy-done.10, s32[4096]{0:T(1024)S(1)} %copy-done.8, f32[12]{0:T(128)S(1)} %copy-done.11, s32[32,128]{1,0:T(8,128)S(1)} %bitcast.20, ...), custom_call_target="tpu_custom_call" | custom-call | flops 3000000000 | bytes 8000000 | tf_op jit(solution)/shard_map/feature_grads/pallas_call | solution.py:488
  39.0 0.0 copy-start.14
  39.1 0.8 copy-done.14
  39.8 1.9 %collective-permute-start = (f32[8,216,128]{2,1,0:T(8,128)S(1)}, f32[8,216,128]{2,1,0:T(8,128)S(1)}, u32[]{:S(2)}, u32[]{:S(2)}) collective-permute-start(f32[8,216,128]{2,1,0:T(8,128)S(1)} %get-tuple-element.30), channel_id=1, source_target_pairs={{0,16},{16,0},{32,48},{48,32},{64,80},{80,64},{96,112},{112,96},{1... | collective-permute-start | bytes 2654216 | tf_op jit(solution)/shard_map/row_sum/ppermute | solution.py:562
  41.8 2.1 %collective-permute-done = f32[8,216,128]{2,1,0:T(8,128)S(1)} collective-permute-done((f32[8,216,128]{2,1,0:T(8,128)S(1)}, f32[8,216,128]{2,1,0:T(8,128)S(1)}, u32[]{:S(2)}, u32[]{:S(2)}) %collective-permute-start) | collective-permute-done | bytes 884768 | tf_op jit(solution)/shard_map/row_sum/ppermute | solution.py:562
  43.8 1.0 add.3
  44.8 0.0 copy-start.9
  44.8 0.0 copy-start.15
  44.8 0.0 copy-start.16
  44.8 4.9 %all-to-all-start.1 = ((f32[8,216,128]{2,1,0:T(8,128)}), f32[8,216,128]{2,1,0:T(8,128)S(1)}, u32[]{:S(2)}, u32[]{:S(2)}) async-start(f32[8,216,128]{2,1,0:T(8,128)} %add.3), calls=%async_computation.1 | async-start | bytes 1769472 | tf_op jit(solution)/shard_map/row_sum/all_to_all | solution.py:566
  49.7 0.0 copy-done.9
  49.7 0.0 copy-done.15
  49.7 0.0 copy-done.16
  49.7 0.0 copy-start.4
  49.8 2.2 %copy-done.4 = bf16[64,256,128]{2,1,0:T(8,128)(2,1)S(1)} copy-done((bf16[64,256,128]{2,1,0:T(8,128)(2,1)S(1)}, bf16[64,256,128]{2,1,0:T(8,128)(2,1)}, u32[]{:S(2)}) %copy-start.4) | copy-done | bytes 4194328
  51.9 3.8 %pair_grads.1 = (bf16[64,256,128]{2,1,0:T(8,128)(2,1)}, f32[16,128]{1,0:T(8,128)S(1)}) custom-call(bf16[12,128]{1,0:T(8,128)(2,1)S(1)} %bitcast.22, bf16[64,256,128]{2,1,0:T(8,128)(2,1)S(1)} %copy-done.4, bf16[1024,256]{1,0:T(8,128)(2,1)S(1)} %get-tuple-element.31.weights, bf16[1024,256]{1,0:T(8,128)(2,1)S(1)} %copy-done.15, bf16[64,16,128]{2,1,0:T(8,128)(2,1)S(1)} %copy-done.16), custom_call_target="tpu_custom_call" | custom-call | flops 2000000000 | bytes 10000000 | tf_op jit(solution)/shard_map/pair_grads/pallas_call | solution.py:530
  55.7 0.0 copy-start.18
  55.7 7.4 %all-to-all-done.1 = f32[8,216,128]{2,1,0:T(8,128)S(1)} async-done(((f32[8,216,128]{2,1,0:T(8,128)}), f32[8,216,128]{2,1,0:T(8,128)S(1)}, u32[]{:S(2)}, u32[]{:S(2)}) %all-to-all-start.1) | async-done | bytes 884768 | tf_op jit(solution)/shard_map/row_sum/all_to_all | solution.py:566
  63.2 0.0 copy-done.18
  63.2 0.2 fusion
  63.5 1.0 concatenate.10
  64.5 7.7 %all_to_all.30 = f32[4,112,128]{2,1,0:T(8,128)S(1)} all-to-all(f32[4,112,128]{2,1,0:T(8,128)S(1)} %bitcast.23), channel_id=1, replica_groups={{0,4,8,12},{1,5,9,13},{2,6,10,14},{3,7,11,15},{16,20,24,28},{17,21,25,2..., dimensions={0} | all-to-all | bytes 458752 | tf_op jit(solution)/shard_map/col_sum/all_to_all | solution.py:566
  72.3 10.5 %all_to_all.31 = f32[4,112,128]{2,1,0:T(8,128)S(1)} all-to-all(f32[4,112,128]{2,1,0:T(8,128)S(1)} %broadcast_in_dim.11), channel_id=1, replica_groups={{0,1,2,3},{4,5,6,7},{8,9,10,11},{12,13,14,15},{16,17,18,19},{20,21,22,2..., dimensions={0} | all-to-all | bytes 458752 | tf_op jit(solution)/shard_map/col_sum/all_to_all | solution.py:566
  82.8 0.7 broadcast_in_dim.12
  83.5 3.4 %all-to-all-start.4 = ((f32[4,112,128]{2,1,0:T(8,128)}), f32[4,112,128]{2,1,0:T(8,128)S(1)}, u32[]{:S(2)}, u32[]{:S(2)}) async-start(f32[4,112,128]{2,1,0:T(8,128)} %broadcast_in_dim.12), calls=%async_computation.4 | async-start | bytes 458752 | tf_op jit(solution)/shard_map/col_sum/all_to_all | solution.py:566
  86.9 0.1 pad.2.clone
  87.0 5.2 %all-to-all-done.4 = f32[4,112,128]{2,1,0:T(8,128)S(1)} async-done(((f32[4,112,128]{2,1,0:T(8,128)}), f32[4,112,128]{2,1,0:T(8,128)S(1)}, u32[]{:S(2)}, u32[]{:S(2)}) %all-to-all-start.4) | async-done | bytes 229408 | tf_op jit(solution)/shard_map/col_sum/all_to_all | solution.py:566
  92.2 0.1 maximum_maximum_fusion
  92.3 0.1 broadcast_in_dim.28
  92.4 15.7 %all_to_all.32.own = f32[8,280,128]{2,1,0:T(8,128)S(1)} all-to-all(f32[8,280,128]{2,1,0:T(8,128)S(1)} %broadcast_in_dim.28), channel_id=1, replica_groups={{0,32,64,96,128,160,192,224},{16,48,80,112,144,176,208,240},{1,33,65,97..., dimensions={0} | all-to-all | bytes 2293760 | tf_op jit(solution)/shard_map/row_gather/all_to_all | solution.py:566
  108.1 5.7 %collective-permute-start.1 = (f32[8,280,128]{2,1,0:T(8,128)S(1)}, f32[8,280,128]{2,1,0:T(8,128)S(1)}, u32[]{:S(2)}, u32[]{:S(2)}) collective-permute-start(f32[8,280,128]{2,1,0:T(8,128)S(1)} %all_to_all.32.own), channel_id=1, source_target_pairs={{0,16},{16,0},{32,48},{48,32},{64,80},{80,64},{96,112},{112,96},{1... | collective-permute-start | bytes 3440648 | tf_op jit(solution)/shard_map/row_gather/ppermute | solution.py:562
  113.8 2.4 %collective-permute-done.1.other = f32[8,280,128]{2,1,0:T(8,128)S(1)} collective-permute-done((f32[8,280,128]{2,1,0:T(8,128)S(1)}, f32[8,280,128]{2,1,0:T(8,128)S(1)}, u32[]{:S(2)}, u32[]{:S(2)}) %collective-permute-start.1) | collective-permute-done | bytes 1146912 | tf_op jit(solution)/shard_map/row_gather/ppermute | solution.py:562
  116.2 1.9 %assemble.1 = (f32[816,384]{1,0:T(8,128)}, f32[336,384]{1,0:T(8,128)}, f32[256,384]{1,0:T(8,128)}, f32[64,384]{1,0:T(8,128)}, f32[12,128]{1,0:T(8,128)}) custom-call(f32[8,280,128]{2,1,0:T(8,128)S(1)} %all_to_all.32.own, f32[8,280,128]{2,1,0:T(8,128)S(1)} %collective-permute-done.1.other, f32[448,128]{1,0:T(8,128)S(1)} %bitcast.13), custom_call_target="tpu_custom_call" | custom-call | tf_op jit(solution)/shard_map/row_gather/assemble/pallas_call | solution.py:392
  (11 shorter events, 0.1 us)
Async XLA Ops:
  0.6 20.3 %copy-start = (bf16[64,288]{1,0:T(8,128)(2,1)S(1)}, bf16[64,288]{1,0:T(8,128)(2,1)}, u32[]{:S(2)}) copy-start(bf16[64,288]{1,0:T(8,128)(2,1)} %grad_point.3) | copy-start | bytes 110596
  0.6 20.3 %copy-start.3 = (bf16[64,192]{1,0:T(8,128)(2,1)S(1)}, bf16[64,192]{1,0:T(8,128)(2,1)}, u32[]{:S(2)}) copy-start(bf16[64,192]{1,0:T(8,128)(2,1)} %grad_single.3) | copy-start | bytes 73732
  0.7 31.2 %copy-start.5 = (bf16[384,816]{0,1:T(8,128)(2,1)S(1)}, bf16[384,816]{0,1:T(8,128)(2,1)}, u32[]{:S(2)}) copy-start(bf16[384,816]{0,1:T(8,128)(2,1)} %param.17) | copy-start | bytes 1880068
  9.1 22.8 %copy-start.2 = (bf16[64,336]{1,0:T(8,128)(2,1)S(1)}, bf16[64,336]{1,0:T(8,128)(2,1)}, u32[]{:S(2)}) copy-start(bf16[64,336]{1,0:T(8,128)(2,1)} %get-tuple-element.28.query) | copy-start | bytes 129028
  9.1 22.7 %copy-start.6 = (bf16[384,336]{0,1:T(8,128)(2,1)S(1)}, bf16[384,336]{0,1:T(8,128)(2,1)}, u32[]{:S(2)}) copy-start(bf16[384,336]{0,1:T(8,128)(2,1)} %param.16) | copy-start | bytes 774148
  9.1 22.7 %copy-start.7 = (bf16[64,384]{1,0:T(8,128)(2,1)S(1)}, bf16[64,384]{1,0:T(8,128)(2,1)}, u32[]{:S(2)}) copy-start(bf16[64,384]{1,0:T(8,128)(2,1)} %query_single.3) | copy-start | bytes 147460
  9.2 22.7 %copy-start.8 = (s32[4096]{0:T(1024)S(1)}, s32[4096]{0:T(1024)}, u32[]{:S(2)}) copy-start(s32[4096]{0:T(1024)} %mask_s.3) | copy-start | bytes 49156
  9.2 22.7 %copy-start.10 = (s32[16]{0:T(128)S(1)}, s32[16]{0:T(128)}, u32[]{:S(2)}) copy-start(s32[16]{0:T(128)} %offsets.3) | copy-start | bytes 196
  9.2 22.7 %copy-start.11 = (f32[12]{0:T(128)S(1)}, f32[12]{0:T(128)}, u32[]{:S(2)}) copy-start(f32[12]{0:T(128)} %head_weight.3) | copy-start | bytes 148
  9.2 22.7 %all-to-all-start = ((f32[16,3,8,128]{3,2,1,0:T(8,128)}), f32[16,3,8,128]{3,2,1,0:T(8,128)S(1)}, u32[]{:S(2)}, u32[]{:S(2)}) async-start(f32[16,3,8,128]{3,2,1,0:T(8,128)} %get-tuple-element.24), calls=%async_computation | async-start | bytes 393216 | tf_op jit(solution)/shard_map/row_statistics/all_to_all | solution.py:566
  20.9 0.8 copy-start.1
  31.9 1.2 %copy-start.12 = (f32[1024,256]{1,0:T(8,128)S(1)}, f32[1024,256]{1,0:T(8,128)}, u32[]{:S(2)}) copy-start(f32[1024,256]{1,0:T(8,128)} %get-tuple-element.25.exp_terms) | copy-start | bytes 3145732
  33.1 1.2 %copy-start.13 = (f32[1024,256]{1,0:T(8,128)S(1)}, f32[1024,256]{1,0:T(8,128)}, u32[]{:S(2)}) copy-start(f32[1024,256]{1,0:T(8,128)} %get-tuple-element.26.up) | copy-start | bytes 3145732
  34.4 0.9 copy-start.17
  39.0 0.8 copy-start.14
  39.8 4.0 %collective-permute-start = (f32[8,216,128]{2,1,0:T(8,128)S(1)}, f32[8,216,128]{2,1,0:T(8,128)S(1)}, u32[]{:S(2)}, u32[]{:S(2)}) collective-permute-start(f32[8,216,128]{2,1,0:T(8,128)S(1)} %get-tuple-element.30), channel_id=1, source_target_pairs={{0,16},{16,0},{32,48},{48,32},{64,80},{80,64},{96,112},{112,96},{1... | collective-permute-start | bytes 2654216 | tf_op jit(solution)/shard_map/row_sum/ppermute | solution.py:562
  44.8 4.9 %copy-start.9 = (bf16[128,12]{0,1:T(8,128)(2,1)S(1)}, bf16[128,12]{0,1:T(8,128)(2,1)}, u32[]{:S(2)}) copy-start(bf16[128,12]{0,1:T(8,128)(2,1)} %param.18) | copy-start | bytes 9220
  44.8 4.9 %copy-start.15 = (bf16[1024,256]{1,0:T(8,128)(2,1)S(1)}, bf16[1024,256]{1,0:T(8,128)(2,1)}, u32[]{:S(2)}) copy-start(bf16[1024,256]{1,0:T(8,128)(2,1)} %copy-done.14) | copy-start | bytes 1572868
  44.8 4.9 %copy-start.16 = (bf16[64,16,128]{2,1,0:T(8,128)(2,1)S(1)}, bf16[64,16,128]{2,1,0:T(8,128)(2,1)}, u32[]{:S(2)}) copy-start(bf16[64,16,128]{2,1,0:T(8,128)(2,1)} %get-tuple-element.33.heads) | copy-start | bytes 786436
  44.8 18.3 %all-to-all-start.1 = ((f32[8,216,128]{2,1,0:T(8,128)}), f32[8,216,128]{2,1,0:T(8,128)S(1)}, u32[]{:S(2)}, u32[]{:S(2)}) async-start(f32[8,216,128]{2,1,0:T(8,128)} %add.3), calls=%async_computation.1 | async-start | bytes 1769472 | tf_op jit(solution)/shard_map/row_sum/all_to_all | solution.py:566
  49.7 2.2 %copy-start.4 = (bf16[64,256,128]{2,1,0:T(8,128)(2,1)S(1)}, bf16[64,256,128]{2,1,0:T(8,128)(2,1)}, u32[]{:S(2)}) copy-start(bf16[64,256,128]{2,1,0:T(8,128)(2,1)} %pair.3) | copy-start | bytes 12582916
  55.7 7.5 %copy-start.18 = (bf16[256,384]{1,0:T(8,128)(2,1)S(1)}, bf16[256,384]{1,0:T(8,128)(2,1)}, u32[]{:S(2)}) copy-start(bf16[256,384]{1,0:T(8,128)(2,1)} %key_single.1) | copy-start | bytes 589828
  83.5 8.7 %all-to-all-start.4 = ((f32[4,112,128]{2,1,0:T(8,128)}), f32[4,112,128]{2,1,0:T(8,128)S(1)}, u32[]{:S(2)}, u32[]{:S(2)}) async-start(f32[4,112,128]{2,1,0:T(8,128)} %broadcast_in_dim.12), calls=%async_computation.4 | async-start | bytes 458752 | tf_op jit(solution)/shard_map/col_sum/all_to_all | solution.py:566
  108.1 8.1 %collective-permute-start.1 = (f32[8,280,128]{2,1,0:T(8,128)S(1)}, f32[8,280,128]{2,1,0:T(8,128)S(1)}, u32[]{:S(2)}, u32[]{:S(2)}) collective-permute-start(f32[8,280,128]{2,1,0:T(8,128)S(1)} %all_to_all.32.own), channel_id=1, source_target_pairs={{0,16},{16,0},{32,48},{48,32},{64,80},{80,64},{96,112},{112,96},{1... | collective-permute-start | bytes 3440648 | tf_op jit(solution)/shard_map/row_gather/ppermute | solution.py:562

commit v6 on v5

--- a/solution.py
+++ b/solution.py
@@ -359,6 +359,40 @@
     bias_out[...] += LOGIT_WEIGHT * total
 
 
+def share_kernel(
+    got, key_single, bias_part, query_single_part, share_out, single_out, total
+):
+    value = got[0]
+    for s in range(1, ROWS // 2):
+        value += got[s]
+    total[...] = value
+    key_grad = jnp.concatenate([total[0:56], total[FEATS : FEATS + 56]], axis=1)
+    key_share = two_part_dot(key_single[...], key_grad, NN, values_first=True)
+    for k in range(3):
+        share_out[FEATS * k : FEATS * (k + 1)] = key_share[0:FEATS, 128 * k : 128 * (k + 1)]
+    share_out[153:165] = bias_part[0:H]
+    share_out[165:228] = total[150:213]
+    share_out[228:420] = query_single_part[...]
+    share_out[420:] = jnp.zeros((28, 128), F32)
+    single_out[0:48] = total[102:150]
+    single_out[48:] = jnp.zeros((4, 128), F32)
+
+
+def share_of(got, key_single, bias_part, query_single_part):
+    return pl.pallas_call(
+        share_kernel,
+        out_shape=(
+            jax.ShapeDtypeStruct((448, 128), F32),
+            jax.ShapeDtypeStruct((52, 128), F32),
+        ),
+        in_specs=[VECTORS] * 4,
+        out_specs=(VECTORS,) * 2,
+        scratch_shapes=[pltpu.VMEM((SHARE, 128), F32)],
+        compiler_params=limit(16),
+        name="row_share",
+    )(got, key_single, bias_part, query_single_part)
+
+
 def assemble_kernel(own, other, share, key_out, query_out, single_out, query_single_out, pair_out):
     first = lax.rem(lax.axis_index("row"), 2) == 0
     lane = pl.program_id(0)
@@ -571,7 +605,7 @@
 
 
 def scatter_row(kept, given):
-    return jnp.sum(exchange(kept + other_core(given), "row", CHIPS), axis=0)
+    return exchange(kept + other_core(given), "row", CHIPS)
 
 
 def sum_col(values):
@@ -579,16 +613,6 @@
     share = jnp.sum(share, axis=0)
     share = jnp.sum(gather(share, "col", 4, ALONG_Z), axis=0)
     return gather(share, "col", 4, ALONG_X).reshape(values.shape)
-
-
-def lanes_of(values):
-    return [values[..., 128 * k : 128 * (k + 1)] for k in range(values.shape[-1] // 128)]
-
-
-def joined(values, rows):
-    return jnp.concatenate(
-        [values[..., k : k + rows, :] for k in range(0, values.shape[-2], rows)], axis=-1
-    )
 
 
 def local(
@@ -621,20 +645,14 @@
         query_single, query_weight, key_weight, columns,
     )
     with jax.named_scope("row_sum"):
-        summed = scatter_row(kept, given)
+        got = scatter_row(kept, given)
     grad_pair, bias_part = pair_grads_of(pair_weight, pair, weights, scores, heads)
-    key_grad = joined(summed[: 2 * FEATS], FEATS)
-    key_share = jnp.dot(key_grad, key_single.astype(F32), precision=HIGHEST)
+    share, single = share_of(got, key_single, bias_part, query_single_part)
     with jax.named_scope("col_sum"):
-        share = jnp.concatenate(
-            lanes_of(key_share)
-            + [bias_part[:H], summed[150:213], query_single_part, jnp.zeros((28, 128), F32)],
-            axis=0,
-        )
         share = sum_col(share)
     with jax.named_scope("row_gather"):
         own = jnp.concatenate(
-            [share[:228], summed[102:150], jnp.zeros((4, 128), F32)], axis=0
+            [share[:228], single], axis=0
         )
         own = gather(own, "row", ROWS // 2, CHIPS)
         results = assembled(own, other_core(own), share)

time: 119 us -> 116 us (0.975)
  blocking collectives: 34 us -> 41.7 us
  waiting for transfers between devices: 26.6 us -> 21.4 us
  starting transfers between devices: 27.6 us -> 24.2 us
  local copies, waits for them, and re-layouts: 9.11 us -> 7.31 us
    all_to_all x3 -> x4, blocking collectives: 34 us -> 41.7 us  [exchange(): return lax.all_to_all(values, axis, 0, 0, axis_index_groups=groups)]
    all_to_all x3 -> x2, waiting for transfers between devices: 22.2 us -> 16.9 us  [exchange(): return lax.all_to_all(values, axis, 0, 0, axis_index_groups=groups)]
    all_to_all x3 -> x2, starting transfers between devices: 20 us -> 16.6 us  [exchange(): return lax.all_to_all(values, axis, 0, 0, axis_index_groups=groups)]
  transfers between devices with their start and end apart: 5 -> 4, of which waited for: 5 -> 4; matrix products, arithmetic and copies ran while one was open for 0% -> 0% of each run, Pallas kernels for 4% -> 4%
where the time goes in v6:
time: 116 us; the launch traced here: 115 us
  blocking collectives  41.7 us (36%)
  starting transfers between devices  24.2 us (21%)
  waiting for transfers between devices  21.4 us (18%)
  Pallas kernels  18.6 us (16%)
  local copies, waits for them, and re-layouts  7.31 us (6%)
    all_to_all x4, blocking collectives, exchange(): return lax.all_to_all(values, axis, 0, 0, axis_index_groups=groups)  41.7 us
    all_to_all x2, waiting for transfers between devices, exchange(): return lax.all_to_all(values, axis, 0, 0, axis_index_groups=groups)  16.9 us
    all_to_all x2, starting transfers between devices, exchange(): return lax.all_to_all(values, axis, 0, 0, axis_index_groups=groups)  16.6 us
    pallas_call x1, Pallas kernels, scores_of(): pl.pallas_call(score_kernel, grid=(STEPS,), out_shape=(jax.ShapeDtypeStru...  8.44 us
    ppermute x2, starting transfers between devices, other_core(): return lax.ppermute(values, 'row', [(i, i ^ 1) for i in range(ROWS)])  7.6 us
    unnamed x38, local copies, waits for them, and re-layouts  7.19 us
    ppermute x2, waiting for transfers between devices, other_core(): return lax.ppermute(values, 'row', [(i, i ^ 1) for i in range(ROWS)])  4.48 us
    pallas_call x1, Pallas kernels, pair_grads_of(): pl.pallas_call(pair_kernel, grid=(STEPS,), out_shape=(jax.ShapeDtypeStruc...  3.74 us
  transfers between devices with their start and end apart: 4, of which 4 were waited for; matrix products, arithmetic and copies ran while one was open for 0% of the time, Pallas kernels for 4%

profile of v6, /device:TPU:1, one launch (start us, length us, event | category | flops | bytes accessed | tf_op | source)
XLA Modules:
  0.0 115.2 jit_solution(9982547177415812204)
XLA Ops:
  0.6 0.0 copy-start.1
  0.6 0.0 copy-start.4
  0.7 0.0 copy-start.6
  0.7 8.4 %row_scores.1 = (f32[1024,256]{1,0:T(8,128)}, f32[1024,256]{1,0:T(8,128)}, bf16[336,256]{1,0:T(8,128)(2,1)}, bf16[64,336]{1,0:T(8,128)(2,1)}, bf16[64,16,128]{2,1,0:T(8,128)(2,1)}, /*index=5*/f32[16,3,8,128]{3,2,1,0:T(8,128)}) custom-call(s32[16]{0:T(128)} %offsets.3, s32[4096]{0:T(1024)} %mask_s.3, s32[4096]{0:T(1024)} %chain_s.1, f32[12]{0:T(128)} %head_weight.3, ...), custom_call_target="tpu_custom_call" | custom-call | flops 2000000000 | bytes 8000000 | tf_op jit(solution)/shard_map/row_scores/pallas_call | solution.py:464
  9.1 0.0 copy-start.3
  9.1 0.0 copy-start.7
  9.1 0.0 copy-start.8
  9.2 0.0 copy-start.9
  9.2 0.0 copy-start.11
  9.2 0.0 copy-start.12
  9.2 11.7 %all-to-all-start = ((f32[16,3,8,128]{3,2,1,0:T(8,128)}), f32[16,3,8,128]{3,2,1,0:T(8,128)S(1)}, u32[]{:S(2)}, u32[]{:S(2)}) async-start(f32[16,3,8,128]{3,2,1,0:T(8,128)} %get-tuple-element.26), calls=%async_computation | async-start | bytes 393216 | tf_op jit(solution)/shard_map/row_statistics/all_to_all | solution.py:600
  20.9 0.0 copy-done.1
  20.9 0.0 copy-done.4
  20.9 0.0 copy-start.2
  20.9 0.8 copy-done.2
  21.7 0.6 spread_features.1.columns_of
  22.4 9.5 %all-to-all-done.parts = f32[16,3,8,128]{3,2,1,0:T(8,128)S(1)} async-done(((f32[16,3,8,128]{3,2,1,0:T(8,128)}), f32[16,3,8,128]{3,2,1,0:T(8,128)S(1)}, u32[]{:S(2)}, u32[]{:S(2)}) %all-to-all-start) | async-done | bytes 196640 | tf_op jit(solution)/shard_map/row_statistics/all_to_all | solution.py:600
  31.9 0.0 copy-done.6
  31.9 0.0 copy-done.3
  31.9 0.0 copy-done.7
  31.9 0.0 copy-done.8
  31.9 0.0 copy-done.9
  31.9 0.0 copy-done.11
  31.9 0.0 copy-done.12
  31.9 0.0 copy-start.13
  31.9 1.2 %copy-done.13 = f32[1024,256]{1,0:T(8,128)S(1)} copy-done((f32[1024,256]{1,0:T(8,128)S(1)}, f32[1024,256]{1,0:T(8,128)}, u32[]{:S(2)}) %copy-start.13) | copy-done | bytes 1048600
  33.1 0.0 copy-start.14
  33.1 1.2 %copy-done.14 = f32[1024,256]{1,0:T(8,128)S(1)} copy-done((f32[1024,256]{1,0:T(8,128)S(1)}, f32[1024,256]{1,0:T(8,128)}, u32[]{:S(2)}) %copy-start.14) | copy-done | bytes 1048600
  34.4 0.0 copy-start.18
  34.4 0.9 copy-done.18
  35.3 3.7 %feature_grads.1 = (bf16[1024,256]{1,0:T(8,128)(2,1)S(1)}, bf16[1024,256]{1,0:T(8,128)(2,1)S(1)}, f32[8,216,128]{2,1,0:T(8,128)S(1)}, f32[8,216,128]{2,1,0:T(8,128)S(1)}, f32[192,128]{1,0:T(8,128)S(1)}) custom-call(s32[16]{0:T(128)S(1)} %copy-done.11, s32[4096]{0:T(1024)S(1)} %copy-done.9, f32[12]{0:T(128)S(1)} %copy-done.12, s32[32,128]{1,0:T(8,128)S(1)} %bitcast.18, ...), custom_call_target="tpu_custom_call" | custom-call | flops 3000000000 | bytes 8000000 | tf_op jit(solution)/shard_map/feature_grads/pallas_call | solution.py:522
  39.0 0.0 copy-start.15
  39.0 0.8 copy-done.15
  39.8 1.9 %collective-permute-start = (f32[8,216,128]{2,1,0:T(8,128)S(1)}, f32[8,216,128]{2,1,0:T(8,128)S(1)}, u32[]{:S(2)}, u32[]{:S(2)}) collective-permute-start(f32[8,216,128]{2,1,0:T(8,128)S(1)} %get-tuple-element.32), channel_id=1, source_target_pairs={{0,16},{16,0},{32,48},{48,32},{64,80},{80,64},{96,112},{112,96},{1... | collective-permute-start | bytes 2654216 | tf_op jit(solution)/shard_map/row_sum/ppermute | solution.py:596
  41.7 2.1 %collective-permute-done = f32[8,216,128]{2,1,0:T(8,128)S(1)} collective-permute-done((f32[8,216,128]{2,1,0:T(8,128)S(1)}, f32[8,216,128]{2,1,0:T(8,128)S(1)}, u32[]{:S(2)}, u32[]{:S(2)}) %collective-permute-start) | collective-permute-done | bytes 884768 | tf_op jit(solution)/shard_map/row_sum/ppermute | solution.py:596
  43.8 1.0 add.3
  44.8 0.0 copy-start.10
  44.8 0.0 copy-start.16
  44.8 0.0 copy-start.17
  44.8 4.9 %all-to-all-start.1 = ((f32[8,216,128]{2,1,0:T(8,128)}), f32[8,216,128]{2,1,0:T(8,128)S(1)}, u32[]{:S(2)}, u32[]{:S(2)}) async-start(f32[8,216,128]{2,1,0:T(8,128)} %add.3), calls=%async_computation.1 | async-start | bytes 1769472 | tf_op jit(solution)/shard_map/row_sum/all_to_all | solution.py:600
  49.7 0.0 copy-done.10
  49.7 0.0 copy-done.16
  49.7 0.0 copy-done.17
  49.7 0.0 copy-start.5
  49.7 2.2 %copy-done.5 = bf16[64,256,128]{2,1,0:T(8,128)(2,1)S(1)} copy-done((bf16[64,256,128]{2,1,0:T(8,128)(2,1)S(1)}, bf16[64,256,128]{2,1,0:T(8,128)(2,1)}, u32[]{:S(2)}) %copy-start.5) | copy-done | bytes 4194328
  51.9 0.0 copy-start
  51.9 3.7 %pair_grads.1 = (bf16[64,256,128]{2,1,0:T(8,128)(2,1)}, f32[16,128]{1,0:T(8,128)S(1)}) custom-call(bf16[12,128]{1,0:T(8,128)(2,1)S(1)} %bitcast.20, bf16[64,256,128]{2,1,0:T(8,128)(2,1)S(1)} %copy-done.5, bf16[1024,256]{1,0:T(8,128)(2,1)S(1)} %get-tuple-element.33.weights, bf16[1024,256]{1,0:T(8,128)(2,1)S(1)} %copy-done.16, bf16[64,16,128]{2,1,0:T(8,128)(2,1)S(1)} %copy-done.17), custom_call_target="tpu_custom_call" | custom-call | flops 2000000000 | bytes 10000000 | tf_op jit(solution)/shard_map/pair_grads/pallas_call | solution.py:564
  55.6 7.5 %all-to-all-done.1.got = f32[8,216,128]{2,1,0:T(8,128)S(1)} async-done(((f32[8,216,128]{2,1,0:T(8,128)}), f32[8,216,128]{2,1,0:T(8,128)S(1)}, u32[]{:S(2)}, u32[]{:S(2)}) %all-to-all-start.1) | async-done | bytes 884768 | tf_op jit(solution)/shard_map/row_sum/all_to_all | solution.py:600
  63.1 0.0 copy-done
  63.1 0.2 row_share.1
  63.3 7.7 %all_to_all.30 = f32[4,112,128]{2,1,0:T(8,128)S(1)} all-to-all(f32[4,112,128]{2,1,0:T(8,128)S(1)} %bitcast.12), channel_id=1, replica_groups={{0,4,8,12},{1,5,9,13},{2,6,10,14},{3,7,11,15},{16,20,24,28},{17,21,25,2..., dimensions={0} | all-to-all | bytes 458752 | tf_op jit(solution)/shard_map/col_sum/all_to_all | solution.py:600
  71.1 10.5 %all_to_all.31 = f32[4,112,128]{2,1,0:T(8,128)S(1)} all-to-all(f32[4,112,128]{2,1,0:T(8,128)S(1)} %broadcast_in_dim.6), channel_id=1, replica_groups={{0,1,2,3},{4,5,6,7},{8,9,10,11},{12,13,14,15},{16,17,18,19},{20,21,22,2..., dimensions={0} | all-to-all | bytes 458752 | tf_op jit(solution)/shard_map/col_sum/all_to_all | solution.py:600
  81.6 7.7 %all_to_all.32 = f32[4,112,128]{2,1,0:T(8,128)S(1)} all-to-all(f32[4,112,128]{2,1,0:T(8,128)S(1)} %broadcast_in_dim.7), channel_id=1, replica_groups={{0,4,8,12},{1,5,9,13},{2,6,10,14},{3,7,11,15},{16,20,24,28},{17,21,25,2..., dimensions={0} | all-to-all | bytes 458752 | tf_op jit(solution)/shard_map/col_sum/all_to_all | solution.py:600
  89.4 0.1 broadcast_in_dim.8
  89.5 15.7 %all_to_all.33.own = f32[8,280,128]{2,1,0:T(8,128)S(1)} all-to-all(f32[8,280,128]{2,1,0:T(8,128)S(1)} %broadcast_in_dim.8), channel_id=1, replica_groups={{0,32,64,96,128,160,192,224},{16,48,80,112,144,176,208,240},{1,33,65,97..., dimensions={0} | all-to-all | bytes 2293760 | tf_op jit(solution)/shard_map/row_gather/all_to_all | solution.py:600
  105.2 5.7 %collective-permute-start.1 = (f32[8,280,128]{2,1,0:T(8,128)S(1)}, f32[8,280,128]{2,1,0:T(8,128)S(1)}, u32[]{:S(2)}, u32[]{:S(2)}) collective-permute-start(f32[8,280,128]{2,1,0:T(8,128)S(1)} %all_to_all.33.own), channel_id=1, source_target_pairs={{0,16},{16,0},{32,48},{48,32},{64,80},{80,64},{96,112},{112,96},{1... | collective-permute-start | bytes 3440648 | tf_op jit(solution)/shard_map/row_gather/ppermute | solution.py:596
  110.9 2.4 %collective-permute-done.1.other = f32[8,280,128]{2,1,0:T(8,128)S(1)} collective-permute-done((f32[8,280,128]{2,1,0:T(8,128)S(1)}, f32[8,280,128]{2,1,0:T(8,128)S(1)}, u32[]{:S(2)}, u32[]{:S(2)}) %collective-permute-start.1) | collective-permute-done | bytes 1146912 | tf_op jit(solution)/shard_map/row_gather/ppermute | solution.py:596
  113.3 1.9 %assemble.1 = (f32[816,384]{1,0:T(8,128)}, f32[336,384]{1,0:T(8,128)}, f32[256,384]{1,0:T(8,128)}, f32[64,384]{1,0:T(8,128)}, f32[12,128]{1,0:T(8,128)}) custom-call(f32[8,280,128]{2,1,0:T(8,128)S(1)} %all_to_all.33.own, f32[8,280,128]{2,1,0:T(8,128)S(1)} %collective-permute-done.1.other, f32[448,128]{1,0:T(8,128)S(1)} %bitcast.11), custom_call_target="tpu_custom_call" | custom-call | tf_op jit(solution)/shard_map/row_gather/assemble/pallas_call | solution.py:426
  (6 shorter events, 0.1 us)
Async XLA Ops:
  0.6 20.3 %copy-start.1 = (bf16[64,288]{1,0:T(8,128)(2,1)S(1)}, bf16[64,288]{1,0:T(8,128)(2,1)}, u32[]{:S(2)}) copy-start(bf16[64,288]{1,0:T(8,128)(2,1)} %grad_point.3) | copy-start | bytes 110596
  0.6 20.3 %copy-start.4 = (bf16[64,192]{1,0:T(8,128)(2,1)S(1)}, bf16[64,192]{1,0:T(8,128)(2,1)}, u32[]{:S(2)}) copy-start(bf16[64,192]{1,0:T(8,128)(2,1)} %grad_single.3) | copy-start | bytes 73732
  0.7 31.2 %copy-start.6 = (bf16[384,816]{0,1:T(8,128)(2,1)S(1)}, bf16[384,816]{0,1:T(8,128)(2,1)}, u32[]{:S(2)}) copy-start(bf16[384,816]{0,1:T(8,128)(2,1)} %param.17) | copy-start | bytes 1880068
  9.1 22.8 %copy-start.3 = (bf16[64,336]{1,0:T(8,128)(2,1)S(1)}, bf16[64,336]{1,0:T(8,128)(2,1)}, u32[]{:S(2)}) copy-start(bf16[64,336]{1,0:T(8,128)(2,1)} %get-tuple-element.30.query) | copy-start | bytes 129028
  9.1 22.7 %copy-start.7 = (bf16[384,336]{0,1:T(8,128)(2,1)S(1)}, bf16[384,336]{0,1:T(8,128)(2,1)}, u32[]{:S(2)}) copy-start(bf16[384,336]{0,1:T(8,128)(2,1)} %param.16) | copy-start | bytes 774148
  9.1 22.7 %copy-start.8 = (bf16[64,384]{1,0:T(8,128)(2,1)S(1)}, bf16[64,384]{1,0:T(8,128)(2,1)}, u32[]{:S(2)}) copy-start(bf16[64,384]{1,0:T(8,128)(2,1)} %query_single.3) | copy-start | bytes 147460
  9.2 22.7 %copy-start.9 = (s32[4096]{0:T(1024)S(1)}, s32[4096]{0:T(1024)}, u32[]{:S(2)}) copy-start(s32[4096]{0:T(1024)} %mask_s.3) | copy-start | bytes 49156
  9.2 22.7 %copy-start.11 = (s32[16]{0:T(128)S(1)}, s32[16]{0:T(128)}, u32[]{:S(2)}) copy-start(s32[16]{0:T(128)} %offsets.3) | copy-start | bytes 196
  9.2 22.7 %copy-start.12 = (f32[12]{0:T(128)S(1)}, f32[12]{0:T(128)}, u32[]{:S(2)}) copy-start(f32[12]{0:T(128)} %head_weight.3) | copy-start | bytes 148
  9.2 22.7 %all-to-all-start = ((f32[16,3,8,128]{3,2,1,0:T(8,128)}), f32[16,3,8,128]{3,2,1,0:T(8,128)S(1)}, u32[]{:S(2)}, u32[]{:S(2)}) async-start(f32[16,3,8,128]{3,2,1,0:T(8,128)} %get-tuple-element.26), calls=%async_computation | async-start | bytes 393216 | tf_op jit(solution)/shard_map/row_statistics/all_to_all | solution.py:600
  20.9 0.8 copy-start.2
  31.9 1.2 %copy-start.13 = (f32[1024,256]{1,0:T(8,128)S(1)}, f32[1024,256]{1,0:T(8,128)}, u32[]{:S(2)}) copy-start(f32[1024,256]{1,0:T(8,128)} %get-tuple-element.27.exp_terms) | copy-start | bytes 3145732
  33.1 1.2 %copy-start.14 = (f32[1024,256]{1,0:T(8,128)S(1)}, f32[1024,256]{1,0:T(8,128)}, u32[]{:S(2)}) copy-start(f32[1024,256]{1,0:T(8,128)} %get-tuple-element.28.up) | copy-start | bytes 3145732
  34.4 0.9 copy-start.18
  39.0 0.8 copy-start.15
  39.8 4.0 %collective-permute-start = (f32[8,216,128]{2,1,0:T(8,128)S(1)}, f32[8,216,128]{2,1,0:T(8,128)S(1)}, u32[]{:S(2)}, u32[]{:S(2)}) collective-permute-start(f32[8,216,128]{2,1,0:T(8,128)S(1)} %get-tuple-element.32), channel_id=1, source_target_pairs={{0,16},{16,0},{32,48},{48,32},{64,80},{80,64},{96,112},{112,96},{1... | collective-permute-start | bytes 2654216 | tf_op jit(solution)/shard_map/row_sum/ppermute | solution.py:596
  44.8 4.9 %copy-start.10 = (bf16[128,12]{0,1:T(8,128)(2,1)S(1)}, bf16[128,12]{0,1:T(8,128)(2,1)}, u32[]{:S(2)}) copy-start(bf16[128,12]{0,1:T(8,128)(2,1)} %param.18) | copy-start | bytes 9220
  44.8 4.9 %copy-start.16 = (bf16[1024,256]{1,0:T(8,128)(2,1)S(1)}, bf16[1024,256]{1,0:T(8,128)(2,1)}, u32[]{:S(2)}) copy-start(bf16[1024,256]{1,0:T(8,128)(2,1)} %copy-done.15) | copy-start | bytes 1572868
  44.8 4.9 %copy-start.17 = (bf16[64,16,128]{2,1,0:T(8,128)(2,1)S(1)}, bf16[64,16,128]{2,1,0:T(8,128)(2,1)}, u32[]{:S(2)}) copy-start(bf16[64,16,128]{2,1,0:T(8,128)(2,1)} %get-tuple-element.35.heads) | copy-start | bytes 786436
  44.8 18.3 %all-to-all-start.1 = ((f32[8,216,128]{2,1,0:T(8,128)}), f32[8,216,128]{2,1,0:T(8,128)S(1)}, u32[]{:S(2)}, u32[]{:S(2)}) async-start(f32[8,216,128]{2,1,0:T(8,128)} %add.3), calls=%async_computation.1 | async-start | bytes 1769472 | tf_op jit(solution)/shard_map/row_sum/all_to_all | solution.py:600
  49.7 2.2 %copy-start.5 = (bf16[64,256,128]{2,1,0:T(8,128)(2,1)S(1)}, bf16[64,256,128]{2,1,0:T(8,128)(2,1)}, u32[]{:S(2)}) copy-start(bf16[64,256,128]{2,1,0:T(8,128)(2,1)} %pair.3) | copy-start | bytes 12582916
  51.9 11.2 %copy-start = (bf16[256,384]{1,0:T(8,128)(2,1)S(1)}, bf16[256,384]{1,0:T(8,128)(2,1)}, u32[]{:S(2)}) copy-start(bf16[256,384]{1,0:T(8,128)(2,1)} %key_single.3) | copy-start | bytes 589828
  105.2 8.1 %collective-permute-start.1 = (f32[8,280,128]{2,1,0:T(8,128)S(1)}, f32[8,280,128]{2,1,0:T(8,128)S(1)}, u32[]{:S(2)}, u32[]{:S(2)}) collective-permute-start(f32[8,280,128]{2,1,0:T(8,128)S(1)} %all_to_all.33.own), channel_id=1, source_target_pairs={{0,16},{16,0},{32,48},{48,32},{64,80},{80,64},{96,112},{112,96},{1... | collective-permute-start | bytes 3440648 | tf_op jit(solution)/shard_map/row_gather/ppermute | solution.py:596

commit v7 on v6

--- a/solution.py
+++ b/solution.py
@@ -211,7 +211,7 @@
             stats_out[s] = stats[...]
 
 
-def spread_kernel(query, grad_single, grad_point, out):
+def spread_features(query, grad_single, grad_point, out):
     column = lax.broadcasted_iota(jnp.int32, (QB, ALL), 1)
     row = lax.broadcasted_iota(jnp.int32, (QB, ALL), 0)
     copies = jnp.where(lax.div(column, HP) == row, 1.0, 0.0).astype(BF16)
@@ -244,7 +244,8 @@
     query_single,
     query_weight,
     key_weight,
-    columns_of,
+    grad_single,
+    grad_point,
     weight_out,
     score_out,
     kept_out,
@@ -253,7 +254,9 @@
     key_grad,
     key_single_grad,
     query_weight_grad,
+    columns_of,
 ):
+    spread_features(query, grad_single, grad_point, columns_of)
     row_top = parts[0, 0]
     for s in range(1, COLS):
         row_top = jnp.maximum(row_top, parts[s, 0])
@@ -503,21 +506,26 @@
             pltpu.VMEM((STEP, HP, DZ), F32),
             pltpu.VMEM((3, 8, 128), F32),
         ],
-        compiler_params=limit(60),
+        compiler_params=limit(30),
         cost_estimate=pl.CostEstimate(
             flops=2_000_000_000, bytes_accessed=8_000_000, transcendentals=262144
         ),
         name="row_scores",
     )(
-        offsets, mask, chain, head_weight, chain_bias, mask.reshape(32, 128),
-        chain.reshape(32, 128), query_single, key_single, query_weight, key_weight,
-        pair_weight, pair, grad_single, grad_point, grad_pairs,
+        *(
+            pltpu.with_memory_space_constraint(x, pltpu.HBM)
+            for x in (
+                offsets, mask, chain, head_weight, chain_bias,
+                mask.reshape(32, 128), chain.reshape(32, 128), query_single, key_single,
+                query_weight, key_weight, pair_weight, pair, grad_single, grad_point, grad_pairs,
+            )
+        ),
     )
 
 
 def grads_of(
     offsets, mask, head_weight, parts, exp_terms, up, key_qk, query, query_single,
-    query_weight, key_weight, columns,
+    query_weight, key_weight, grad_single, grad_point,
 ):
     return pl.pallas_call(
         grad_kernel,
@@ -528,12 +536,13 @@
             jax.ShapeDtypeStruct((ROWS // 2, SHARE, 128), F32),
             jax.ShapeDtypeStruct((3 * QB, 128), F32),
         ),
-        in_specs=[SCALARS] * 3 + [VECTORS] * 10,
+        in_specs=[SCALARS] * 3 + [VECTORS] * 11,
         out_specs=(VECTORS,) * 5,
         scratch_shapes=[
             pltpu.VMEM((KF, KB), F32),
             pltpu.VMEM((KB, DS), F32),
             pltpu.VMEM((QF, DS), F32),
+            pltpu.VMEM((QF + VEC + VPTS, ALL), BF16),
         ],
         compiler_params=limit(24),
         cost_estimate=pl.CostEstimate(
@@ -542,22 +551,8 @@
         name="feature_grads",
     )(
         offsets, mask, head_weight, mask.reshape(32, 128), parts, exp_terms, up, key_qk,
-        query, query_single, query_weight, key_weight, columns,
-    )
-
-
-def spread_of(query, grad_single, grad_point):
-    return pl.pallas_call(
-        spread_kernel,
-        out_shape=jax.ShapeDtypeStruct((QF + VEC + VPTS, ALL), BF16),
-        in_specs=[VECTORS] * 3,
-        out_specs=VECTORS,
-        compiler_params=limit(16),
-        cost_estimate=pl.CostEstimate(
-            flops=400_000_000, bytes_accessed=4_000_000, transcendentals=0
-        ),
-        name="spread_features",
-    )(query, grad_single, grad_point)
+        query, query_single, query_weight, key_weight, grad_single, grad_point,
+    )
 
 
 def pair_grads_of(pair_weight, pair, weights, scores, heads):
@@ -637,12 +632,11 @@
         key_single, query_weight, key_weight, pair_weight, pair, grad_single_out,
         grad_point_out, grad_pair_out,
     )
-    columns = spread_of(query, grad_single_out, grad_point_out)
     with jax.named_scope("row_statistics"):
         parts = exchange(own, "col")
     weights, scores, kept, given, query_single_part = grads_of(
         strip_offsets, residue_mask, head_weight, parts, terms, up, key_qk, query,
-        query_single, query_weight, key_weight, columns,
+        query_single, query_weight, key_weight, grad_single_out, grad_point_out,
     )
     with jax.named_scope("row_sum"):
         got = scatter_row(kept, given)

time: 116 us -> 111 us (0.957)
  blocking collectives: 41.7 us -> 64 us
  starting transfers between devices: 24.2 us -> 12.6 us
  waiting for transfers between devices: 21.4 us -> 12 us
  local copies, waits for them, and re-layouts: 7.31 us -> 2.34 us
  Pallas kernels: 18.6 us -> 17.3 us
    all_to_all x4 -> x5, blocking collectives: 41.7 us -> 64 us  [exchange(): return lax.all_to_all(values, axis, 0, 0, axis_index_groups=groups)]
    all_to_all x2 -> x1, starting transfers between devices: 16.6 us -> 4.9 us  [exchange(): return lax.all_to_all(values, axis, 0, 0, axis_index_groups=groups)]
    all_to_all x2 -> x1, waiting for transfers between devices: 16.9 us -> 7.47 us  [exchange(): return lax.all_to_all(values, axis, 0, 0, axis_index_groups=groups)]
    unnamed x38 -> x22, local copies, waits for them, and re-layouts: 7.19 us -> 2.22 us
    pallas_call x1, Pallas kernels: 8.44 us -> 7.19 us  [scores_of(): pl.pallas_call(score_kernel, grid=(STEPS,), out_shape=(jax.ShapeDtypeStru...]
  transfers between devices with their start and end apart: 4 -> 3, of which waited for: 4 -> 3; matrix products, arithmetic and copies ran while one was open for 0% -> 0% of each run, Pallas kernels for 4% -> 3%
where the time goes in v7:
time: 111 us; the launch traced here: 110 us
  blocking collectives  64 us (58%)
  Pallas kernels  17.3 us (16%)
  starting transfers between devices  12.6 us (11%)
  waiting for transfers between devices  12 us (11%)
  local copies, waits for them, and re-layouts  2.34 us (2%)
    all_to_all x5, blocking collectives, exchange(): return lax.all_to_all(values, axis, 0, 0, axis_index_groups=groups)  64 us
    ppermute x2, starting transfers between devices, other_core(): return lax.ppermute(values, 'row', [(i, i ^ 1) for i in range(ROWS)])  7.68 us
    all_to_all x1, waiting for transfers between devices, exchange(): return lax.all_to_all(values, axis, 0, 0, axis_index_groups=groups)  7.47 us
    pallas_call x1, Pallas kernels, scores_of(): pl.pallas_call(score_kernel, grid=(STEPS,), out_shape=(jax.ShapeDtypeStru...  7.19 us
    all_to_all x1, starting transfers between devices, exchange(): return lax.all_to_all(values, axis, 0, 0, axis_index_groups=groups)  4.9 us
    ppermute x2, waiting for transfers between devices, other_core(): return lax.ppermute(values, 'row', [(i, i ^ 1) for i in range(ROWS)])  4.48 us
    pallas_call x1, Pallas kernels, grads_of(): pl.pallas_call(grad_kernel, out_shape=(jax.ShapeDtypeStruct((ALL, KB), BF...  4.28 us
    pallas_call x1, Pallas kernels, pair_grads_of(): pl.pallas_call(pair_kernel, grid=(STEPS,), out_shape=(jax.ShapeDtypeStruc...  3.75 us
  transfers between devices with their start and end apart: 3, of which 3 were waited for; matrix products, arithmetic and copies ran while one was open for 0% of the time, Pallas kernels for 3%

profile of v7, /device:TPU:1, one launch (start us, length us, event | category | flops | bytes accessed | tf_op | source)
XLA Modules:
  0.0 110.1 jit_solution(3970996179076145896)
XLA Ops:
  0.6 0.0 copy-start.2
  0.6 0.0 copy-start.3
  0.7 0.0 copy-start.4
  0.7 0.0 copy-start.5
  0.7 0.0 copy-start.6
  0.7 0.0 copy-start.7
  0.7 0.0 copy-start.9
  0.7 0.0 copy-start.10
  0.7 7.2 %row_scores.1 = (f32[1024,256]{1,0:T(8,128)S(1)}, f32[1024,256]{1,0:T(8,128)S(1)}, bf16[336,256]{1,0:T(8,128)(2,1)S(1)}, bf16[64,336]{1,0:T(8,128)(2,1)S(1)}, bf...) custom-call(s32[16]{0:T(128)} %offsets.3, s32[4096]{0:T(1024)} %mask_s.3, s32[4096]{0:T(1024)} %chain_s.1, ...), custom_call_target="tpu_custom_call" | custom-call | flops 2000000000 | bytes 8000000 | tf_op jit(solution)/shard_map/row_scores/pallas_call | solution.py:467
  7.9 22.3 %all_to_all.30.parts = f32[16,3,8,128]{3,2,1,0:T(8,128)S(1)} all-to-all(f32[16,3,8,128]{3,2,1,0:T(8,128)S(1)} %get-tuple-element.26), channel_id=1, replica_groups=mesh['row'=16,'col'=16] {'col'}, dimensions={0} | all-to-all | bytes 393216 | tf_op jit(solution)/shard_map/row_statistics/all_to_all | solution.py:595
  30.2 0.0 copy-done.2
  30.2 0.0 copy-done.3
  30.2 0.0 copy-done.4
  30.3 0.0 copy-done.5
  30.3 0.0 copy-done.6
  30.3 0.0 copy-done.7
  30.3 0.0 copy-done.9
  30.3 0.0 copy-done.10
  30.3 4.3 %feature_grads.1 = (bf16[1024,256]{1,0:T(8,128)(2,1)S(1)}, bf16[1024,256]{1,0:T(8,128)(2,1)S(1)}, f32[8,216,128]{2,1,0:T(8,128)S(1)}, f32[8,216,128]{2,1,0:T(8,128)S(1)}, f32[192,128]{1,0:T(8,128)S(1)}) custom-call(s32[16]{0:T(128)S(1)} %copy-done.9, s32[4096]{0:T(1024)S(1)} %copy-done.7, f32[12]{0:T(128)S(1)} %copy-done.10, s32[32,128]{1,0:T(8,128)S(1)} %bitcast.18, ...), custom_call_target="tpu_custom_call" | custom-call | flops 3000000000 | bytes 8000000 | tf_op jit(solution)/shard_map/feature_grads/pallas_call | solution.py:530
  34.6 2.0 %collective-permute-start = (f32[8,216,128]{2,1,0:T(8,128)S(1)}, f32[8,216,128]{2,1,0:T(8,128)S(1)}, u32[]{:S(2)}, u32[]{:S(2)}) collective-permute-start(f32[8,216,128]{2,1,0:T(8,128)S(1)} %get-tuple-element.32), channel_id=1, source_target_pairs={{0,16},{16,0},{32,48},{48,32},{64,80},{80,64},{96,112},{112,96},{1... | collective-permute-start | bytes 2654216 | tf_op jit(solution)/shard_map/row_sum/ppermute | solution.py:591
  36.6 2.1 %collective-permute-done = f32[8,216,128]{2,1,0:T(8,128)S(1)} collective-permute-done((f32[8,216,128]{2,1,0:T(8,128)S(1)}, f32[8,216,128]{2,1,0:T(8,128)S(1)}, u32[]{:S(2)}, u32[]{:S(2)}) %collective-permute-start) | collective-permute-done | bytes 884768 | tf_op jit(solution)/shard_map/row_sum/ppermute | solution.py:591
  38.7 1.0 add.3
  39.7 0.0 copy-start.8
  39.7 4.9 %all-to-all-start.1 = ((f32[8,216,128]{2,1,0:T(8,128)}), f32[8,216,128]{2,1,0:T(8,128)S(1)}, u32[]{:S(2)}, u32[]{:S(2)}) async-start(f32[8,216,128]{2,1,0:T(8,128)} %add.3), calls=%async_computation.1 | async-start | bytes 1769472 | tf_op jit(solution)/shard_map/row_sum/all_to_all | solution.py:595
  44.6 0.0 copy-done.8
  44.6 0.0 copy-start.1
  44.6 2.2 %copy-done.1 = bf16[64,256,128]{2,1,0:T(8,128)(2,1)S(1)} copy-done((bf16[64,256,128]{2,1,0:T(8,128)(2,1)S(1)}, bf16[64,256,128]{2,1,0:T(8,128)(2,1)}, u32[]{:S(2)}) %copy-start.1) | copy-done | bytes 4194328
  46.8 0.0 copy-start
  46.8 3.7 %pair_grads.1 = (bf16[64,256,128]{2,1,0:T(8,128)(2,1)}, f32[16,128]{1,0:T(8,128)S(1)}) custom-call(bf16[12,128]{1,0:T(8,128)(2,1)S(1)} %bitcast.20, bf16[64,256,128]{2,1,0:T(8,128)(2,1)S(1)} %copy-done.1, bf16[1024,256]{1,0:T(8,128)(2,1)S(1)} %get-tuple-element.33.weights, bf16[1024,256]{1,0:T(8,128)(2,1)S(1)} %get-tuple-element.34.scores, ...), custom_call_target="tpu_custom_call" | custom-call | flops 2000000000 | bytes 10000000 | tf_op jit(solution)/shard_map/pair_grads/pallas_call | solution.py:559
  50.5 7.5 %all-to-all-done.1.got = f32[8,216,128]{2,1,0:T(8,128)S(1)} async-done(((f32[8,216,128]{2,1,0:T(8,128)}), f32[8,216,128]{2,1,0:T(8,128)S(1)}, u32[]{:S(2)}, u32[]{:S(2)}) %all-to-all-start.1) | async-done | bytes 884768 | tf_op jit(solution)/shard_map/row_sum/all_to_all | solution.py:595
  58.0 0.0 copy-done
  58.0 0.2 row_share.1
  58.2 7.7 %all_to_all.31 = f32[4,112,128]{2,1,0:T(8,128)S(1)} all-to-all(f32[4,112,128]{2,1,0:T(8,128)S(1)} %bitcast.12), channel_id=1, replica_groups={{0,4,8,12},{1,5,9,13},{2,6,10,14},{3,7,11,15},{16,20,24,28},{17,21,25,2..., dimensions={0} | all-to-all | bytes 458752 | tf_op jit(solution)/shard_map/col_sum/all_to_all | solution.py:595
  66.0 10.5 %all_to_all.32 = f32[4,112,128]{2,1,0:T(8,128)S(1)} all-to-all(f32[4,112,128]{2,1,0:T(8,128)S(1)} %broadcast_in_dim.6), channel_id=1, replica_groups={{0,1,2,3},{4,5,6,7},{8,9,10,11},{12,13,14,15},{16,17,18,19},{20,21,22,2..., dimensions={0} | all-to-all | bytes 458752 | tf_op jit(solution)/shard_map/col_sum/all_to_all | solution.py:595
  76.5 7.7 %all_to_all.33 = f32[4,112,128]{2,1,0:T(8,128)S(1)} all-to-all(f32[4,112,128]{2,1,0:T(8,128)S(1)} %broadcast_in_dim.7), channel_id=1, replica_groups={{0,4,8,12},{1,5,9,13},{2,6,10,14},{3,7,11,15},{16,20,24,28},{17,21,25,2..., dimensions={0} | all-to-all | bytes 458752 | tf_op jit(solution)/shard_map/col_sum/all_to_all | solution.py:595
  84.3 0.1 broadcast_in_dim.8
  84.4 15.7 %all_to_all.34.own = f32[8,280,128]{2,1,0:T(8,128)S(1)} all-to-all(f32[8,280,128]{2,1,0:T(8,128)S(1)} %broadcast_in_dim.8), channel_id=1, replica_groups={{0,32,64,96,128,160,192,224},{16,48,80,112,144,176,208,240},{1,33,65,97..., dimensions={0} | all-to-all | bytes 2293760 | tf_op jit(solution)/shard_map/row_gather/all_to_all | solution.py:595
  100.1 5.7 %collective-permute-start.1 = (f32[8,280,128]{2,1,0:T(8,128)S(1)}, f32[8,280,128]{2,1,0:T(8,128)S(1)}, u32[]{:S(2)}, u32[]{:S(2)}) collective-permute-start(f32[8,280,128]{2,1,0:T(8,128)S(1)} %all_to_all.34.own), channel_id=1, source_target_pairs={{0,16},{16,0},{32,48},{48,32},{64,80},{80,64},{96,112},{112,96},{1... | collective-permute-start | bytes 3440648 | tf_op jit(solution)/shard_map/row_gather/ppermute | solution.py:591
  105.8 2.4 %collective-permute-done.1.other = f32[8,280,128]{2,1,0:T(8,128)S(1)} collective-permute-done((f32[8,280,128]{2,1,0:T(8,128)S(1)}, f32[8,280,128]{2,1,0:T(8,128)S(1)}, u32[]{:S(2)}, u32[]{:S(2)}) %collective-permute-start.1) | collective-permute-done | bytes 1146912 | tf_op jit(solution)/shard_map/row_gather/ppermute | solution.py:591
  108.2 1.9 %assemble.1 = (f32[816,384]{1,0:T(8,128)}, f32[336,384]{1,0:T(8,128)}, f32[256,384]{1,0:T(8,128)}, f32[64,384]{1,0:T(8,128)}, f32[12,128]{1,0:T(8,128)}) custom-call(f32[8,280,128]{2,1,0:T(8,128)S(1)} %all_to_all.34.own, f32[8,280,128]{2,1,0:T(8,128)S(1)} %collective-permute-done.1.other, f32[448,128]{1,0:T(8,128)S(1)} %bitcast.11), custom_call_target="tpu_custom_call" | custom-call | tf_op jit(solution)/shard_map/row_gather/assemble/pallas_call | solution.py:429
  (6 shorter events, 0.1 us)
Async XLA Ops:
  0.6 29.6 %copy-start.2 = (bf16[384,816]{0,1:T(8,128)(2,1)S(1)}, bf16[384,816]{0,1:T(8,128)(2,1)}, u32[]{:S(2)}) copy-start(bf16[384,816]{0,1:T(8,128)(2,1)} %param.17) | copy-start | bytes 1880068
  0.6 29.6 %copy-start.3 = (bf16[384,336]{0,1:T(8,128)(2,1)S(1)}, bf16[384,336]{0,1:T(8,128)(2,1)}, u32[]{:S(2)}) copy-start(bf16[384,336]{0,1:T(8,128)(2,1)} %param.16) | copy-start | bytes 774148
  0.7 29.6 %copy-start.4 = (bf16[64,384]{1,0:T(8,128)(2,1)S(1)}, bf16[64,384]{1,0:T(8,128)(2,1)}, u32[]{:S(2)}) copy-start(bf16[64,384]{1,0:T(8,128)(2,1)} %query_single.3) | copy-start | bytes 147460
  0.7 29.6 %copy-start.5 = (bf16[64,288]{1,0:T(8,128)(2,1)S(1)}, bf16[64,288]{1,0:T(8,128)(2,1)}, u32[]{:S(2)}) copy-start(bf16[64,288]{1,0:T(8,128)(2,1)} %grad_point.3) | copy-start | bytes 110596
  0.7 29.6 %copy-start.6 = (bf16[64,192]{1,0:T(8,128)(2,1)S(1)}, bf16[64,192]{1,0:T(8,128)(2,1)}, u32[]{:S(2)}) copy-start(bf16[64,192]{1,0:T(8,128)(2,1)} %grad_single.3) | copy-start | bytes 73732
  0.7 29.6 %copy-start.7 = (s32[4096]{0:T(1024)S(1)}, s32[4096]{0:T(1024)}, u32[]{:S(2)}) copy-start(s32[4096]{0:T(1024)} %mask_s.3) | copy-start | bytes 49156
  0.7 29.6 %copy-start.9 = (s32[16]{0:T(128)S(1)}, s32[16]{0:T(128)}, u32[]{:S(2)}) copy-start(s32[16]{0:T(128)} %offsets.3) | copy-start | bytes 196
  0.7 29.6 %copy-start.10 = (f32[12]{0:T(128)S(1)}, f32[12]{0:T(128)}, u32[]{:S(2)}) copy-start(f32[12]{0:T(128)} %head_weight.3) | copy-start | bytes 148
  34.6 4.1 %collective-permute-start = (f32[8,216,128]{2,1,0:T(8,128)S(1)}, f32[8,216,128]{2,1,0:T(8,128)S(1)}, u32[]{:S(2)}, u32[]{:S(2)}) collective-permute-start(f32[8,216,128]{2,1,0:T(8,128)S(1)} %get-tuple-element.32), channel_id=1, source_target_pairs={{0,16},{16,0},{32,48},{48,32},{64,80},{80,64},{96,112},{112,96},{1... | collective-permute-start | bytes 2654216 | tf_op jit(solution)/shard_map/row_sum/ppermute | solution.py:591
  39.7 4.9 %copy-start.8 = (bf16[128,12]{0,1:T(8,128)(2,1)S(1)}, bf16[128,12]{0,1:T(8,128)(2,1)}, u32[]{:S(2)}) copy-start(bf16[128,12]{0,1:T(8,128)(2,1)} %param.18) | copy-start | bytes 9220
  39.7 18.3 %all-to-all-start.1 = ((f32[8,216,128]{2,1,0:T(8,128)}), f32[8,216,128]{2,1,0:T(8,128)S(1)}, u32[]{:S(2)}, u32[]{:S(2)}) async-start(f32[8,216,128]{2,1,0:T(8,128)} %add.3), calls=%async_computation.1 | async-start | bytes 1769472 | tf_op jit(solution)/shard_map/row_sum/all_to_all | solution.py:595
  44.6 2.2 %copy-start.1 = (bf16[64,256,128]{2,1,0:T(8,128)(2,1)S(1)}, bf16[64,256,128]{2,1,0:T(8,128)(2,1)}, u32[]{:S(2)}) copy-start(bf16[64,256,128]{2,1,0:T(8,128)(2,1)} %pair.3) | copy-start | bytes 12582916
  46.8 11.2 %copy-start = (bf16[256,384]{1,0:T(8,128)(2,1)S(1)}, bf16[256,384]{1,0:T(8,128)(2,1)}, u32[]{:S(2)}) copy-start(bf16[256,384]{1,0:T(8,128)(2,1)} %key_single.3) | copy-start | bytes 589828
  100.1 8.1 %collective-permute-start.1 = (f32[8,280,128]{2,1,0:T(8,128)S(1)}, f32[8,280,128]{2,1,0:T(8,128)S(1)}, u32[]{:S(2)}, u32[]{:S(2)}) collective-permute-start(f32[8,280,128]{2,1,0:T(8,128)S(1)} %all_to_all.34.own), channel_id=1, source_target_pairs={{0,16},{16,0},{32,48},{48,32},{64,80},{80,64},{96,112},{112,96},{1... | collective-permute-start | bytes 3440648 | tf_op jit(solution)/shard_map/row_gather/ppermute | solution.py:591

commit v8 on v7

--- a/solution.py
+++ b/solution.py
@@ -577,7 +577,9 @@
             flops=2_000_000_000, bytes_accessed=10_000_000, transcendentals=0
         ),
         name="pair_grads",
-    )(pair_weight, pair, weights, scores, heads)
+    )(
+        pair_weight, pltpu.with_memory_space_constraint(pair, pltpu.HBM), weights, scores, heads
+    )
 
 
 CHIPS = [[2 * i + core for i in range(ROWS // 2)] for core in range(2)]

time: 111 us -> 111 us (level)
  Pallas kernels: 17.3 us -> 19.5 us
  local copies, waits for them, and re-layouts: 2.34 us -> 0.16 us
    pallas_call x1, Pallas kernels: 3.75 us -> 5.96 us  [pair_grads_of(): pl.pallas_call(pair_kernel, grid=(STEPS,), out_shape=(jax.ShapeDtypeStruc...]
    unnamed x22 -> x20, local copies, waits for them, and re-layouts: 2.22 us -> 0.04 us
  transfers between devices with their start and end apart: 3 -> 3, of which waited for: 3 -> 3; matrix products, arithmetic and copies ran while one was open for 0% -> 0% of each run, Pallas kernels for 3% -> 5%
where the time goes in v8:
time: 111 us; the launch traced here: 110 us
  blocking collectives  64 us (58%)
  Pallas kernels  19.5 us (18%)
  starting transfers between devices  12.6 us (11%)
  waiting for transfers between devices  11.9 us (11%)
    all_to_all x5, blocking collectives, exchange(): return lax.all_to_all(values, axis, 0, 0, axis_index_groups=groups)  64 us
    ppermute x2, starting transfers between devices, other_core(): return lax.ppermute(values, 'row', [(i, i ^ 1) for i in range(ROWS)])  7.68 us
    all_to_all x1, waiting for transfers between devices, exchange(): return lax.all_to_all(values, axis, 0, 0, axis_index_groups=groups)  7.44 us
    pallas_call x1, Pallas kernels, scores_of(): pl.pallas_call(score_kernel, grid=(STEPS,), out_shape=(jax.ShapeDtypeStru...  7.19 us
    pallas_call x1, Pallas kernels, pair_grads_of(): pl.pallas_call(pair_kernel, grid=(STEPS,), out_shape=(jax.ShapeDtypeStruc...  5.96 us
    all_to_all x1, starting transfers between devices, exchange(): return lax.all_to_all(values, axis, 0, 0, axis_index_groups=groups)  4.9 us
    ppermute x2, waiting for transfers between devices, other_core(): return lax.ppermute(values, 'row', [(i, i ^ 1) for i in range(ROWS)])  4.48 us
    pallas_call x1, Pallas kernels, grads_of(): pl.pallas_call(grad_kernel, out_shape=(jax.ShapeDtypeStruct((ALL, KB), BF...  4.28 us
  transfers between devices with their start and end apart: 3, of which 3 were waited for; matrix products, arithmetic and copies ran while one was open for 0% of the time, Pallas kernels for 5%

profile of v8, /device:TPU:1, one launch (start us, length us, event | category | flops | bytes accessed | tf_op | source)
XLA Modules:
  0.0 110.1 jit_solution(10392959162301525287)
XLA Ops:
  0.6 0.0 copy-start.1
  0.6 0.0 copy-start.2
  0.7 0.0 copy-start.3
  0.7 0.0 copy-start.4
  0.7 0.0 copy-start.5
  0.7 0.0 copy-start.6
  0.7 0.0 copy-start.8
  0.7 0.0 copy-start.9
  0.7 7.2 %row_scores.1 = (f32[1024,256]{1,0:T(8,128)S(1)}, f32[1024,256]{1,0:T(8,128)S(1)}, bf16[336,256]{1,0:T(8,128)(2,1)S(1)}, bf16[64,336]{1,0:T(8,128)(2,1)S(1)}, bf...) custom-call(s32[16]{0:T(128)} %offsets.3, s32[4096]{0:T(1024)} %mask_s.3, s32[4096]{0:T(1024)} %chain_s.1, ...), custom_call_target="tpu_custom_call" | custom-call | flops 2000000000 | bytes 8000000 | tf_op jit(solution)/shard_map/row_scores/pallas_call | solution.py:467
  7.9 22.3 %all_to_all.30.parts = f32[16,3,8,128]{3,2,1,0:T(8,128)S(1)} all-to-all(f32[16,3,8,128]{3,2,1,0:T(8,128)S(1)} %get-tuple-element.26), channel_id=1, replica_groups=mesh['row'=16,'col'=16] {'col'}, dimensions={0} | all-to-all | bytes 393216 | tf_op jit(solution)/shard_map/row_statistics/all_to_all | solution.py:597
  30.2 0.0 copy-done.1
  30.2 0.0 copy-done.2
  30.2 0.0 copy-done.3
  30.3 0.0 copy-done.4
  30.3 0.0 copy-done.5
  30.3 0.0 copy-done.6
  30.3 0.0 copy-done.8
  30.3 0.0 copy-done.9
  30.3 4.3 %feature_grads.1 = (bf16[1024,256]{1,0:T(8,128)(2,1)S(1)}, bf16[1024,256]{1,0:T(8,128)(2,1)S(1)}, f32[8,216,128]{2,1,0:T(8,128)S(1)}, f32[8,216,128]{2,1,0:T(8,128)S(1)}, f32[192,128]{1,0:T(8,128)S(1)}) custom-call(s32[16]{0:T(128)S(1)} %copy-done.8, s32[4096]{0:T(1024)S(1)} %copy-done.6, f32[12]{0:T(128)S(1)} %copy-done.9, s32[32,128]{1,0:T(8,128)S(1)} %bitcast.18, ...), custom_call_target="tpu_custom_call" | custom-call | flops 3000000000 | bytes 8000000 | tf_op jit(solution)/shard_map/feature_grads/pallas_call | solution.py:530
  34.6 2.0 %collective-permute-start = (f32[8,216,128]{2,1,0:T(8,128)S(1)}, f32[8,216,128]{2,1,0:T(8,128)S(1)}, u32[]{:S(2)}, u32[]{:S(2)}) collective-permute-start(f32[8,216,128]{2,1,0:T(8,128)S(1)} %get-tuple-element.32), channel_id=1, source_target_pairs={{0,16},{16,0},{32,48},{48,32},{64,80},{80,64},{96,112},{112,96},{1... | collective-permute-start | bytes 2654216 | tf_op jit(solution)/shard_map/row_sum/ppermute | solution.py:593
  36.6 2.1 %collective-permute-done = f32[8,216,128]{2,1,0:T(8,128)S(1)} collective-permute-done((f32[8,216,128]{2,1,0:T(8,128)S(1)}, f32[8,216,128]{2,1,0:T(8,128)S(1)}, u32[]{:S(2)}, u32[]{:S(2)}) %collective-permute-start) | collective-permute-done | bytes 884768 | tf_op jit(solution)/shard_map/row_sum/ppermute | solution.py:593
  38.7 1.0 add.3
  39.7 0.0 copy-start.7
  39.7 4.9 %all-to-all-start.1 = ((f32[8,216,128]{2,1,0:T(8,128)}), f32[8,216,128]{2,1,0:T(8,128)S(1)}, u32[]{:S(2)}, u32[]{:S(2)}) async-start(f32[8,216,128]{2,1,0:T(8,128)} %add.3), calls=%async_computation.1 | async-start | bytes 1769472 | tf_op jit(solution)/shard_map/row_sum/all_to_all | solution.py:597
  44.6 0.0 copy-done.7
  44.6 0.0 copy-start
  44.6 6.0 %pair_grads.1 = (bf16[64,256,128]{2,1,0:T(8,128)(2,1)}, f32[16,128]{1,0:T(8,128)S(1)}) custom-call(bf16[12,128]{1,0:T(8,128)(2,1)S(1)} %bitcast.20, bf16[64,256,128]{2,1,0:T(8,128)(2,1)} %pair.3, bf16[1024,256]{1,0:T(8,128)(2,1)S(1)} %get-tuple-element.33.weights, bf16[1024,256]{1,0:T(8,128)(2,1)S(1)} %get-tuple-element.34.scores, ...), custom_call_target="tpu_custom_call" | custom-call | flops 2000000000 | bytes 10000000 | tf_op jit(solution)/shard_map/pair_grads/pallas_call | solution.py:559
  50.5 7.4 %all-to-all-done.1.got = f32[8,216,128]{2,1,0:T(8,128)S(1)} async-done(((f32[8,216,128]{2,1,0:T(8,128)}), f32[8,216,128]{2,1,0:T(8,128)S(1)}, u32[]{:S(2)}, u32[]{:S(2)}) %all-to-all-start.1) | async-done | bytes 884768 | tf_op jit(solution)/shard_map/row_sum/all_to_all | solution.py:597
  58.0 0.0 copy-done
  58.0 0.2 row_share.1
  58.2 7.7 %all_to_all.31 = f32[4,112,128]{2,1,0:T(8,128)S(1)} all-to-all(f32[4,112,128]{2,1,0:T(8,128)S(1)} %bitcast.12), channel_id=1, replica_groups={{0,4,8,12},{1,5,9,13},{2,6,10,14},{3,7,11,15},{16,20,24,28},{17,21,25,2..., dimensions={0} | all-to-all | bytes 458752 | tf_op jit(solution)/shard_map/col_sum/all_to_all | solution.py:597
  66.0 10.5 %all_to_all.32 = f32[4,112,128]{2,1,0:T(8,128)S(1)} all-to-all(f32[4,112,128]{2,1,0:T(8,128)S(1)} %broadcast_in_dim.6), channel_id=1, replica_groups={{0,1,2,3},{4,5,6,7},{8,9,10,11},{12,13,14,15},{16,17,18,19},{20,21,22,2..., dimensions={0} | all-to-all | bytes 458752 | tf_op jit(solution)/shard_map/col_sum/all_to_all | solution.py:597
  76.5 7.7 %all_to_all.33 = f32[4,112,128]{2,1,0:T(8,128)S(1)} all-to-all(f32[4,112,128]{2,1,0:T(8,128)S(1)} %broadcast_in_dim.7), channel_id=1, replica_groups={{0,4,8,12},{1,5,9,13},{2,6,10,14},{3,7,11,15},{16,20,24,28},{17,21,25,2..., dimensions={0} | all-to-all | bytes 458752 | tf_op jit(solution)/shard_map/col_sum/all_to_all | solution.py:597
  84.3 0.1 broadcast_in_dim.8
  84.4 15.7 %all_to_all.34.own = f32[8,280,128]{2,1,0:T(8,128)S(1)} all-to-all(f32[8,280,128]{2,1,0:T(8,128)S(1)} %broadcast_in_dim.8), channel_id=1, replica_groups={{0,32,64,96,128,160,192,224},{16,48,80,112,144,176,208,240},{1,33,65,97..., dimensions={0} | all-to-all | bytes 2293760 | tf_op jit(solution)/shard_map/row_gather/all_to_all | solution.py:597
  100.1 5.7 %collective-permute-start.1 = (f32[8,280,128]{2,1,0:T(8,128)S(1)}, f32[8,280,128]{2,1,0:T(8,128)S(1)}, u32[]{:S(2)}, u32[]{:S(2)}) collective-permute-start(f32[8,280,128]{2,1,0:T(8,128)S(1)} %all_to_all.34.own), channel_id=1, source_target_pairs={{0,16},{16,0},{32,48},{48,32},{64,80},{80,64},{96,112},{112,96},{1... | collective-permute-start | bytes 3440648 | tf_op jit(solution)/shard_map/row_gather/ppermute | solution.py:593
  105.8 2.4 %collective-permute-done.1.other = f32[8,280,128]{2,1,0:T(8,128)S(1)} collective-permute-done((f32[8,280,128]{2,1,0:T(8,128)S(1)}, f32[8,280,128]{2,1,0:T(8,128)S(1)}, u32[]{:S(2)}, u32[]{:S(2)}) %collective-permute-start.1) | collective-permute-done | bytes 1146912 | tf_op jit(solution)/shard_map/row_gather/ppermute | solution.py:593
  108.2 1.9 %assemble.1 = (f32[816,384]{1,0:T(8,128)}, f32[336,384]{1,0:T(8,128)}, f32[256,384]{1,0:T(8,128)}, f32[64,384]{1,0:T(8,128)}, f32[12,128]{1,0:T(8,128)}) custom-call(f32[8,280,128]{2,1,0:T(8,128)S(1)} %all_to_all.34.own, f32[8,280,128]{2,1,0:T(8,128)S(1)} %collective-permute-done.1.other, f32[448,128]{1,0:T(8,128)S(1)} %bitcast.11), custom_call_target="tpu_custom_call" | custom-call | tf_op jit(solution)/shard_map/row_gather/assemble/pallas_call | solution.py:429
  (6 shorter events, 0.1 us)
Async XLA Ops:
  0.6 29.6 %copy-start.1 = (bf16[384,816]{0,1:T(8,128)(2,1)S(1)}, bf16[384,816]{0,1:T(8,128)(2,1)}, u32[]{:S(2)}) copy-start(bf16[384,816]{0,1:T(8,128)(2,1)} %param.17) | copy-start | bytes 1880068
  0.6 29.6 %copy-start.2 = (bf16[384,336]{0,1:T(8,128)(2,1)S(1)}, bf16[384,336]{0,1:T(8,128)(2,1)}, u32[]{:S(2)}) copy-start(bf16[384,336]{0,1:T(8,128)(2,1)} %param.16) | copy-start | bytes 774148
  0.7 29.6 %copy-start.3 = (bf16[64,384]{1,0:T(8,128)(2,1)S(1)}, bf16[64,384]{1,0:T(8,128)(2,1)}, u32[]{:S(2)}) copy-start(bf16[64,384]{1,0:T(8,128)(2,1)} %query_single.3) | copy-start | bytes 147460
  0.7 29.6 %copy-start.4 = (bf16[64,288]{1,0:T(8,128)(2,1)S(1)}, bf16[64,288]{1,0:T(8,128)(2,1)}, u32[]{:S(2)}) copy-start(bf16[64,288]{1,0:T(8,128)(2,1)} %grad_point.3) | copy-start | bytes 110596
  0.7 29.6 %copy-start.5 = (bf16[64,192]{1,0:T(8,128)(2,1)S(1)}, bf16[64,192]{1,0:T(8,128)(2,1)}, u32[]{:S(2)}) copy-start(bf16[64,192]{1,0:T(8,128)(2,1)} %grad_single.3) | copy-start | bytes 73732
  0.7 29.6 %copy-start.6 = (s32[4096]{0:T(1024)S(1)}, s32[4096]{0:T(1024)}, u32[]{:S(2)}) copy-start(s32[4096]{0:T(1024)} %mask_s.3) | copy-start | bytes 49156
  0.7 29.6 %copy-start.8 = (s32[16]{0:T(128)S(1)}, s32[16]{0:T(128)}, u32[]{:S(2)}) copy-start(s32[16]{0:T(128)} %offsets.3) | copy-start | bytes 196
  0.7 29.6 %copy-start.9 = (f32[12]{0:T(128)S(1)}, f32[12]{0:T(128)}, u32[]{:S(2)}) copy-start(f32[12]{0:T(128)} %head_weight.3) | copy-start | bytes 148
  34.6 4.1 %collective-permute-start = (f32[8,216,128]{2,1,0:T(8,128)S(1)}, f32[8,216,128]{2,1,0:T(8,128)S(1)}, u32[]{:S(2)}, u32[]{:S(2)}) collective-permute-start(f32[8,216,128]{2,1,0:T(8,128)S(1)} %get-tuple-element.32), channel_id=1, source_target_pairs={{0,16},{16,0},{32,48},{48,32},{64,80},{80,64},{96,112},{112,96},{1... | collective-permute-start | bytes 2654216 | tf_op jit(solution)/shard_map/row_sum/ppermute | solution.py:593
  39.7 4.9 %copy-start.7 = (bf16[128,12]{0,1:T(8,128)(2,1)S(1)}, bf16[128,12]{0,1:T(8,128)(2,1)}, u32[]{:S(2)}) copy-start(bf16[128,12]{0,1:T(8,128)(2,1)} %param.18) | copy-start | bytes 9220
  39.7 18.3 %all-to-all-start.1 = ((f32[8,216,128]{2,1,0:T(8,128)}), f32[8,216,128]{2,1,0:T(8,128)S(1)}, u32[]{:S(2)}, u32[]{:S(2)}) async-start(f32[8,216,128]{2,1,0:T(8,128)} %add.3), calls=%async_computation.1 | async-start | bytes 1769472 | tf_op jit(solution)/shard_map/row_sum/all_to_all | solution.py:597
  44.6 13.4 %copy-start = (bf16[256,384]{1,0:T(8,128)(2,1)S(1)}, bf16[256,384]{1,0:T(8,128)(2,1)}, u32[]{:S(2)}) copy-start(bf16[256,384]{1,0:T(8,128)(2,1)} %key_single.3) | copy-start | bytes 589828
  100.1 8.1 %collective-permute-start.1 = (f32[8,280,128]{2,1,0:T(8,128)S(1)}, f32[8,280,128]{2,1,0:T(8,128)S(1)}, u32[]{:S(2)}, u32[]{:S(2)}) collective-permute-start(f32[8,280,128]{2,1,0:T(8,128)S(1)} %all_to_all.34.own), channel_id=1, source_target_pairs={{0,16},{16,0},{32,48},{48,32},{64,80},{80,64},{96,112},{112,96},{1... | collective-permute-start | bytes 3440648 | tf_op jit(solution)/shard_map/row_gather/ppermute | solution.py:593
